TPU v7x, 512 devices: a whole 4x4x16 slice. The times are simulated.
512 devices in a mesh: prompt: 4 (over y_lo, core), seq: 16 (over z), head: 8 (over x, y_hi).
Axes of the slice: x: 4, y: 4 (y_hi: 2, y_lo: 2; y = y_hi * 2 + y_lo), z: 16, core: 2. Of those that a mesh axis runs over, the one named last changes fastest.
Arguments:
- queries: bfloat16 [64, 64, 5120], P(('prompt', 'seq'), None, 'head'), parts along dimension 0, may hold values from -1024 to 1024
- prefix_keys: bfloat16 [262144, 1024], P(('prompt', 'seq'), 'head'), parts along dimension 0, may hold values from -6 to 6
- prefix_values: bfloat16 [262144, 1024], P(('prompt', 'seq'), 'head'), parts along dimension 0, may hold values from -6 to 6
- suffix_keys: bfloat16 [64, 2048, 1024], P(('prompt', 'seq'), None, 'head'), parts along dimension 0, may hold values from -6 to 6
- suffix_values: bfloat16 [64, 2048, 1024], P(('prompt', 'seq'), None, 'head'), parts along dimension 0, may hold values from -6 to 6
- kept_blocks: int32 [64, 64], P('prompt'), parts along dimension 0, may hold values from 0 to 511, as said below
- suffix_lengths: int32 [64], P(('prompt', 'seq')), parts along dimension 0, may hold values from 64 to 2048, as said below
- out_weight: bfloat16 [5120, 5120], P('head', 'seq'), may hold values from -1.75 to 1.75
Outputs:
- projected: float32 [4096, 5120], P(('prompt', 'head'), 'seq'), parts along dimension 0
There are 4 independent parts, one for each index of `prompt`. A program takes and returns all parts, laid end to end along the dimension named above; an argument that names none is the same for every part. Nothing has to cross between parts.
Inputs may be any that keep to these rules, and one draw needn't show every extreme that they name: `kept_blocks`: each row names 64 different prefix blocks. Among the blocks k * 32 to (k + 1) * 32 - 1, for each k, at most 8 are named by one row, and every row names exactly 8 of one such run. `suffix_lengths`: A sample's query tokens are the last 64 of its filled slots; some sample fills all 2048.
All inputs are finite; a program needn't handle non-finite values.
Results may differ from a plain program's by a relative error of at most 0.008.
Values may be sent and summed in bfloat16 or wider, within the bound.
No kernel may reach another device: no remote copies, remote signals or barrier semaphores. Data moves between devices by JAX's collectives and lax.ppermute only.
A program may use at most 64 MiB of HBM per device.

v0:
```python
import math

import jax
import jax.numpy as jnp
from jax import lax
from jax.sharding import PartitionSpec as P

HD = 128
GQA = 5
QB = 64
BLOCK = 128
MOST = 8


floor_value = -1e30


def passed_along(block, axis, distance):
    devices = range(lax.axis_size(axis))
    route = [((i - distance) % len(devices), i) for i in devices]
    return lax.ppermute(block, axis, route)


def from_everyone(x, axis):
    size = lax.axis_size(axis)
    return lax.all_to_all(jnp.broadcast_to(x[None], (size, *x.shape)), axis, 0, 0, tiled=True)


def laid_out(pieces, dim):
    pieces = jnp.moveaxis(pieces, 0, dim)
    lengths = pieces.shape
    return pieces.reshape(*lengths[:dim], lengths[dim] * lengths[dim + 1], *lengths[dim + 2 :])


def gathered_copies(x, axis, dim):
    pieces = from_everyone(x, axis)
    return laid_out(pieces, dim)


def split_up(x, dim, size):
    lengths = x.shape
    pieces = x.reshape(*lengths[:dim], size, lengths[dim] // size, *lengths[dim + 1 :])
    return jnp.moveaxis(pieces, dim, 0)


def sent_and_summed(x, axis, dim):
    pieces = split_up(x, dim, lax.axis_size(axis))
    arrived = lax.all_to_all(pieces, axis, split_axis=0, concat_axis=0, tiled=True)
    return arrived.sum(axis=0)


def partial_softmax(asking, key_rows, value_rows, visible):
    scores = jnp.einsum("tgjd,sgd->tgjs", asking, key_rows, preferred_element_type=jnp.float32) * (
        1.0 / math.sqrt(asking.shape[-1])
    )
    maximum = jnp.maximum(jnp.max(jnp.where(visible, scores, -jnp.inf), axis=-1), floor_value)
    weights = jnp.where(visible, jnp.exp(scores - maximum[..., None]), 0.0).astype(jnp.bfloat16)
    weight_sum = jnp.sum(weights, axis=-1, dtype=jnp.float32)
    summed = jnp.einsum("tgjs,sgd->tgjd", weights, value_rows, preferred_element_type=jnp.float32)
    return (maximum, weight_sum, summed)


def combine(earlier, latest):
    maximum = jnp.maximum(earlier[0], latest[0])
    shrink_one = jnp.exp(earlier[0] - maximum)
    shrink_two = jnp.exp(latest[0] - maximum)
    weight_sum = earlier[1] * shrink_one + latest[1] * shrink_two
    summed = earlier[2] * shrink_one[..., None] + latest[2] * shrink_two[..., None]
    return (maximum, weight_sum, summed)


def body(
    queries,
    prefix_keys,
    prefix_values,
    suffix_keys,
    suffix_values,
    kept_blocks,
    suffix_lengths,
    out_weight,
):
    kv_heads = prefix_keys.shape[1] // HD
    blocks_here = prefix_keys.shape[0] // BLOCK
    block_keys = prefix_keys.reshape(blocks_here, BLOCK, kv_heads, HD)
    block_values = prefix_values.reshape(blocks_here, BLOCK, kv_heads, HD)
    position = lax.axis_index("seq")
    members = lax.axis_size("seq")
    numbers = position * blocks_here + jnp.arange(blocks_here, dtype=jnp.int32)
    present = jnp.any(kept_blocks[:, :, None] == numbers[None, None, :], axis=1)
    slot_ids = jnp.argsort(jnp.where(present, 0, 1).astype(jnp.int32), axis=1, stable=True)[
        :, :MOST
    ]
    usable = jnp.take_along_axis(present, slot_ids, axis=1)

    def prefix_part(asking, sample):
        chosen = slot_ids[sample]
        key_rows = block_keys[chosen].reshape(MOST * BLOCK, kv_heads, HD)
        value_rows = block_values[chosen].reshape(MOST * BLOCK, kv_heads, HD)
        visible = jnp.repeat(usable[sample], BLOCK)
        return partial_softmax(asking, key_rows, value_rows, visible)

    slots_own = suffix_keys.shape[1]
    asking = queries[0].reshape(QB, kv_heads, GQA, HD)
    last_seen = suffix_lengths[0] - QB + jnp.arange(QB, dtype=jnp.int32)
    own_mask = (jnp.arange(slots_own, dtype=jnp.int32)[None, :] <= last_seen[:, None])[
        :, None, None, :
    ]
    at_home = partial_softmax(
        asking,
        suffix_keys[0].reshape(slots_own, kv_heads, HD),
        suffix_values[0].reshape(slots_own, kv_heads, HD),
        own_mask,
    )

    def turn(hop_index, state_now):
        sample = (position - hop_index) % members
        running = combine(state_now[1:], prefix_part(state_now[0], sample))
        return (
            passed_along(state_now[0].astype(jnp.float32), "seq", 1).astype(jnp.bfloat16),
            passed_along(running[0], "seq", 1),
            passed_along(running[1], "seq", 1),
            passed_along(running[2], "seq", 1),
        )

    returned = lax.fori_loop(0, members, turn, (asking, at_home[0], at_home[1], at_home[2]))
    running = returned[1:]
    attended = (
        (running[2] / running[1][..., None]).astype(jnp.bfloat16).reshape(QB, kv_heads * GQA * HD)
    )
    partial_value = jnp.dot(
        gathered_copies(attended, "seq", 0), out_weight, preferred_element_type=jnp.float32
    )
    return sent_and_summed(partial_value, "head", 0)


def solution(mesh):
    in_specs = (
        P(("prompt", "seq"), None, "head"),
        P(("prompt", "seq"), "head"),
        P(("prompt", "seq"), "head"),
        P(("prompt", "seq"), None, "head"),
        P(("prompt", "seq"), None, "head"),
        P("prompt", None),
        P(("prompt", "seq")),
        P("head", "seq"),
    )
    out_specs = P(("prompt", "head"), "seq")
    return jax.shard_map(body, mesh=mesh, in_specs=in_specs, out_specs=out_specs, check_vma=False)
```

profile of v0, /device:TPU:32, one launch (start us, length us, event | category | flops | bytes accessed | tf_op | source)
XLA Modules:
  0.0 410.8 jit_solution(16158687313716852367)
XLA Ops:
  9.3 333.4 %while.21 = (s32[]{:T(128)}, bf16[64,1,5,128]{3,0,2,1:T(8,128)(2,1)S(1)}, f32[64,1,5]{0,2,1:T(8,128)S(1)}, f32[64,1,5]{0,2,1:T(8,128)S(1)}, f32[64,1,5,128]{3,0,...) while((s32[]{:T(128)}, ...), condition=%wide.region_7.8_spmd, body=%wide.region_4.7_spmd.sunk | while | flops 171502496 | bytes 7101056 | solution.py:125
  14.3 3.8 collective-permute-start.3
  18.2 3.8 collective-permute-start
  22.0 5.0 %collective-permute-start.1 = (f32[64,1,5]{0,2,1:T(8,128)S(1)}, f32[64,1,5]{0,2,1:T(8,128)S(1)}, u32[]{:S(2)}, u32[]{:S(2)}) collective-permute-start(f32[64,1,5]{0,2,1:T(8,128)S(1)} %get-tuple-element.382), channel_id=1, source_target_pairs={{120,0},{0,8},{8,16},{16,24},{24,32},{32,40},{40,48},{48,56},{56,6... | collective-permute-start | bytes 3848 | tf_op jit(solution)/shard_map/while/body/eval_jaxpr/ppermute | solution.py:21
  27.1 3.8 collective-permute-start.2
  37.6 3.8 collective-permute-start.3
  41.4 3.8 collective-permute-start
  45.2 5.0 %collective-permute-start.1 = (f32[64,1,5]{0,2,1:T(8,128)S(1)}, f32[64,1,5]{0,2,1:T(8,128)S(1)}, u32[]{:S(2)}, u32[]{:S(2)}) collective-permute-start(f32[64,1,5]{0,2,1:T(8,128)S(1)} %get-tuple-element.382), channel_id=1, source_target_pairs={{120,0},{0,8},{8,16},{16,24},{24,32},{32,40},{40,48},{48,56},{56,6... | collective-permute-start | bytes 3848 | tf_op jit(solution)/shard_map/while/body/eval_jaxpr/ppermute | solution.py:21
  50.3 3.8 collective-permute-start.2
  60.8 3.8 collective-permute-start.3
  64.6 2.9 collective-permute-start
  67.6 4.1 %collective-permute-start.1 = (f32[64,1,5]{0,2,1:T(8,128)S(1)}, f32[64,1,5]{0,2,1:T(8,128)S(1)}, u32[]{:S(2)}, u32[]{:S(2)}) collective-permute-start(f32[64,1,5]{0,2,1:T(8,128)S(1)} %get-tuple-element.382), channel_id=1, source_target_pairs={{120,0},{0,8},{8,16},{16,24},{24,32},{32,40},{40,48},{48,56},{56,6... | collective-permute-start | bytes 3848 | tf_op jit(solution)/shard_map/while/body/eval_jaxpr/ppermute | solution.py:21
  71.7 2.9 collective-permute-start.2
  74.7 2.5 collective-permute-done.2
  82.2 2.9 collective-permute-start.3
  87.1 3.9 collective-permute-start.1
  91.0 2.9 collective-permute-start.2
  94.0 2.5 collective-permute-done.2
  101.5 2.9 collective-permute-start.3
  104.5 2.9 collective-permute-start
  107.4 3.1 collective-permute-start.1
  112.9 3.1 collective-permute-done.2
  124.9 3.1 collective-permute-start.1
  128.1 2.1 collective-permute-start.2
  130.4 3.1 collective-permute-done.2
  138.6 2.1 collective-permute-start.3
  140.7 3.8 collective-permute-start
  144.5 5.0 %collective-permute-start.1 = (f32[64,1,5]{0,2,1:T(8,128)S(1)}, f32[64,1,5]{0,2,1:T(8,128)S(1)}, u32[]{:S(2)}, u32[]{:S(2)}) collective-permute-start(f32[64,1,5]{0,2,1:T(8,128)S(1)} %get-tuple-element.382), channel_id=1, source_target_pairs={{120,0},{0,8},{8,16},{16,24},{24,32},{32,40},{40,48},{48,56},{56,6... | collective-permute-start | bytes 3848 | tf_op jit(solution)/shard_map/while/body/eval_jaxpr/ppermute | solution.py:21
  149.6 3.8 collective-permute-start.2
  160.1 3.7 collective-permute-start.3
  163.9 3.9 collective-permute-start
  167.8 4.2 %collective-permute-start.1 = (f32[64,1,5]{0,2,1:T(8,128)S(1)}, f32[64,1,5]{0,2,1:T(8,128)S(1)}, u32[]{:S(2)}, u32[]{:S(2)}) collective-permute-start(f32[64,1,5]{0,2,1:T(8,128)S(1)} %get-tuple-element.382), channel_id=1, source_target_pairs={{120,0},{0,8},{8,16},{16,24},{24,32},{32,40},{40,48},{48,56},{56,6... | collective-permute-start | bytes 3848 | tf_op jit(solution)/shard_map/while/body/eval_jaxpr/ppermute | solution.py:21
  172.0 2.9 collective-permute-start.2
  174.9 2.6 collective-permute-done.2
  182.5 2.9 collective-permute-start.3
  185.4 2.9 collective-permute-start
  188.3 3.2 collective-permute-start.1
  191.5 2.7 collective-permute-start.2
  194.2 2.8 collective-permute-done.2
  202.0 2.7 collective-permute-start.3
  204.7 2.9 collective-permute-start
  207.6 4.2 %collective-permute-start.1 = (f32[64,1,5]{0,2,1:T(8,128)S(1)}, f32[64,1,5]{0,2,1:T(8,128)S(1)}, u32[]{:S(2)}, u32[]{:S(2)}) collective-permute-start(f32[64,1,5]{0,2,1:T(8,128)S(1)} %get-tuple-element.382), channel_id=1, source_target_pairs={{120,0},{0,8},{8,16},{16,24},{24,32},{32,40},{40,48},{48,56},{56,6... | collective-permute-start | bytes 3848 | tf_op jit(solution)/shard_map/while/body/eval_jaxpr/ppermute | solution.py:21
  213.7 3.5 collective-permute-done.2
  226.1 3.1 collective-permute-start.1
  231.6 3.1 collective-permute-done.2
  243.8 5.0 %collective-permute-start.1 = (f32[64,1,5]{0,2,1:T(8,128)S(1)}, f32[64,1,5]{0,2,1:T(8,128)S(1)}, u32[]{:S(2)}, u32[]{:S(2)}) collective-permute-start(f32[64,1,5]{0,2,1:T(8,128)S(1)} %get-tuple-element.382), channel_id=1, source_target_pairs={{120,0},{0,8},{8,16},{16,24},{24,32},{32,40},{40,48},{48,56},{56,6... | collective-permute-start | bytes 3848 | tf_op jit(solution)/shard_map/while/body/eval_jaxpr/ppermute | solution.py:21
  248.8 3.9 collective-permute-start.2
  259.3 3.9 collective-permute-start.3
  263.2 3.7 collective-permute-start
  266.9 5.1 %collective-permute-start.1 = (f32[64,1,5]{0,2,1:T(8,128)S(1)}, f32[64,1,5]{0,2,1:T(8,128)S(1)}, u32[]{:S(2)}, u32[]{:S(2)}) collective-permute-start(f32[64,1,5]{0,2,1:T(8,128)S(1)} %get-tuple-element.382), channel_id=1, source_target_pairs={{120,0},{0,8},{8,16},{16,24},{24,32},{32,40},{40,48},{48,56},{56,6... | collective-permute-start | bytes 3848 | tf_op jit(solution)/shard_map/while/body/eval_jaxpr/ppermute | solution.py:21
  272.0 3.0 collective-permute-start.2
  275.0 2.5 collective-permute-done.2
  282.6 3.0 collective-permute-start.3
  285.5 2.9 collective-permute-start
  288.5 4.1 %collective-permute-start.1 = (f32[64,1,5]{0,2,1:T(8,128)S(1)}, f32[64,1,5]{0,2,1:T(8,128)S(1)}, u32[]{:S(2)}, u32[]{:S(2)}) collective-permute-start(f32[64,1,5]{0,2,1:T(8,128)S(1)} %get-tuple-element.382), channel_id=1, source_target_pairs={{120,0},{0,8},{8,16},{16,24},{24,32},{32,40},{40,48},{48,56},{56,6... | collective-permute-start | bytes 3848 | tf_op jit(solution)/shard_map/while/body/eval_jaxpr/ppermute | solution.py:21
  294.6 3.5 collective-permute-done.2
  305.1 2.7 collective-permute-start
  307.7 4.1 %collective-permute-start.1 = (f32[64,1,5]{0,2,1:T(8,128)S(1)}, f32[64,1,5]{0,2,1:T(8,128)S(1)}, u32[]{:S(2)}, u32[]{:S(2)}) collective-permute-start(f32[64,1,5]{0,2,1:T(8,128)S(1)} %get-tuple-element.382), channel_id=1, source_target_pairs={{120,0},{0,8},{8,16},{16,24},{24,32},{32,40},{40,48},{48,56},{56,6... | collective-permute-start | bytes 3848 | tf_op jit(solution)/shard_map/while/body/eval_jaxpr/ppermute | solution.py:21
  311.9 3.0 collective-permute-start.2
  314.8 2.6 collective-permute-done.2
  322.5 5.8 %collective-permute-start.3 = (f32[64,1,5,128]{3,0,2,1:T(8,128)S(1)}, f32[64,1,5,128]{3,0,2,1:T(8,128)S(1)}, u32[]{:S(2)}, u32[]{:S(2)}) collective-permute-start(f32[64,1,5,128]{3,0,2,1:T(8,128)S(1)} %fusion.39), channel_id=1, source_target_pairs={{120,0},{0,8},{8,16},{16,24},{24,32},{32,40},{40,48},{48,56},{56,6... | collective-permute-start | bytes 491528 | tf_op jit(solution)/shard_map/while/body/eval_jaxpr/ppermute | solution.py:21
  334.1 8.2 %collective-permute-done.1 = f32[64,1,5]{0,2,1:T(8,128)S(1)} collective-permute-done((f32[64,1,5]{0,2,1:T(8,128)S(1)}, f32[64,1,5]{0,2,1:T(8,128)S(1)}, u32[]{:S(2)}, u32[]{:S(2)}) %collective-permute-start.1) | collective-permute-done | bytes 1312 | tf_op jit(solution)/shard_map/while/body/eval_jaxpr/ppermute | solution.py:21
  343.1 45.5 %all_to_all.10 = bf16[16,64,640]{2,1,0:T(8,128)(2,1)S(1)} all-to-all(bf16[16,64,640]{2,1,0:T(8,128)(2,1)S(1)} %broadcast_in_dim.107), channel_id=1, replica_groups=mesh['prompt'=4,'seq'=16,'head'=8] {'seq'}, dimensions={0} | all-to-all | bytes 2621440 | tf_op jit(solution)/shard_map/all_to_all | solution.py:26
  389.3 20.8 %all_to_all.11 = f32[8,128,320]{1,2,0:T(8,128)S(1)} all-to-all(f32[8,128,320]{1,2,0:T(8,128)S(1)} %fusion.20), channel_id=1, replica_groups=mesh['prompt'=4,'seq'=16,'head'=8] {'head'}, dimensions={0} | all-to-all | bytes 2621440 | tf_op jit(solution)/shard_map/all_to_all | solution.py:48
  (296 shorter events, 126.7 us)
Async XLA Ops:
  14.3 18.2 %collective-permute-start.3 = (f32[64,1,5,128]{3,0,2,1:T(8,128)S(1)}, f32[64,1,5,128]{3,0,2,1:T(8,128)S(1)}, u32[]{:S(2)}, u32[]{:S(2)}) collective-permute-start(f32[64,1,5,128]{3,0,2,1:T(8,128)S(1)} %fusion.39), channel_id=1, source_target_pairs={{120,0},{0,8},{8,16},{16,24},{24,32},{32,40},{40,48},{48,56},{56,6... | collective-permute-start | bytes 491528 | tf_op jit(solution)/shard_map/while/body/eval_jaxpr/ppermute | solution.py:21
  18.2 14.4 %collective-permute-start = (bf16[64,1,5,128]{3,0,2,1:T(8,128)(2,1)S(1)}, bf16[64,1,5,128]{3,0,2,1:T(8,128)(2,1)S(1)}, u32[]{:S(2)}, u32[]{:S(2)}) collective-permute-start(bf16[64,1,5,128]{3,0,2,1:T(8,128)(2,1)S(1)} %copy.43), channel_id=1, source_target_pairs={{120,0},{0,8},{8,16},{16,24},{24,32},{32,40},{40,48},{48,56},{56,6... | collective-permute-start | bytes 245768 | tf_op jit(solution)/shard_map/while/body/eval_jaxpr/ppermute | solution.py:21
  22.0 8.9 %collective-permute-start.1 = (f32[64,1,5]{0,2,1:T(8,128)S(1)}, f32[64,1,5]{0,2,1:T(8,128)S(1)}, u32[]{:S(2)}, u32[]{:S(2)}) collective-permute-start(f32[64,1,5]{0,2,1:T(8,128)S(1)} %get-tuple-element.382), channel_id=1, source_target_pairs={{120,0},{0,8},{8,16},{16,24},{24,32},{32,40},{40,48},{48,56},{56,6... | collective-permute-start | bytes 3848 | tf_op jit(solution)/shard_map/while/body/eval_jaxpr/ppermute | solution.py:21
  27.1 5.5 %collective-permute-start.2 = (f32[64,1,5]{0,2,1:T(8,128)S(1)}, f32[64,1,5]{0,2,1:T(8,128)S(1)}, u32[]{:S(2)}, u32[]{:S(2)}) collective-permute-start(f32[64,1,5]{0,2,1:T(8,128)S(1)} %get-tuple-element.383), channel_id=1, source_target_pairs={{120,0},{0,8},{8,16},{16,24},{24,32},{32,40},{40,48},{48,56},{56,6... | collective-permute-start | bytes 3848 | tf_op jit(solution)/shard_map/while/body/eval_jaxpr/ppermute | solution.py:21
  37.6 18.2 %collective-permute-start.3 = (f32[64,1,5,128]{3,0,2,1:T(8,128)S(1)}, f32[64,1,5,128]{3,0,2,1:T(8,128)S(1)}, u32[]{:S(2)}, u32[]{:S(2)}) collective-permute-start(f32[64,1,5,128]{3,0,2,1:T(8,128)S(1)} %fusion.39), channel_id=1, source_target_pairs={{120,0},{0,8},{8,16},{16,24},{24,32},{32,40},{40,48},{48,56},{56,6... | collective-permute-start | bytes 491528 | tf_op jit(solution)/shard_map/while/body/eval_jaxpr/ppermute | solution.py:21
  41.4 14.4 %collective-permute-start = (bf16[64,1,5,128]{3,0,2,1:T(8,128)(2,1)S(1)}, bf16[64,1,5,128]{3,0,2,1:T(8,128)(2,1)S(1)}, u32[]{:S(2)}, u32[]{:S(2)}) collective-permute-start(bf16[64,1,5,128]{3,0,2,1:T(8,128)(2,1)S(1)} %copy.43), channel_id=1, source_target_pairs={{120,0},{0,8},{8,16},{16,24},{24,32},{32,40},{40,48},{48,56},{56,6... | collective-permute-start | bytes 245768 | tf_op jit(solution)/shard_map/while/body/eval_jaxpr/ppermute | solution.py:21
  45.2 8.9 %collective-permute-start.1 = (f32[64,1,5]{0,2,1:T(8,128)S(1)}, f32[64,1,5]{0,2,1:T(8,128)S(1)}, u32[]{:S(2)}, u32[]{:S(2)}) collective-permute-start(f32[64,1,5]{0,2,1:T(8,128)S(1)} %get-tuple-element.382), channel_id=1, source_target_pairs={{120,0},{0,8},{8,16},{16,24},{24,32},{32,40},{40,48},{48,56},{56,6... | collective-permute-start | bytes 3848 | tf_op jit(solution)/shard_map/while/body/eval_jaxpr/ppermute | solution.py:21
  50.3 5.5 %collective-permute-start.2 = (f32[64,1,5]{0,2,1:T(8,128)S(1)}, f32[64,1,5]{0,2,1:T(8,128)S(1)}, u32[]{:S(2)}, u32[]{:S(2)}) collective-permute-start(f32[64,1,5]{0,2,1:T(8,128)S(1)} %get-tuple-element.383), channel_id=1, source_target_pairs={{120,0},{0,8},{8,16},{16,24},{24,32},{32,40},{40,48},{48,56},{56,6... | collective-permute-start | bytes 3848 | tf_op jit(solution)/shard_map/while/body/eval_jaxpr/ppermute | solution.py:21
  60.8 16.4 %collective-permute-start.3 = (f32[64,1,5,128]{3,0,2,1:T(8,128)S(1)}, f32[64,1,5,128]{3,0,2,1:T(8,128)S(1)}, u32[]{:S(2)}, u32[]{:S(2)}) collective-permute-start(f32[64,1,5,128]{3,0,2,1:T(8,128)S(1)} %fusion.39), channel_id=1, source_target_pairs={{120,0},{0,8},{8,16},{16,24},{24,32},{32,40},{40,48},{48,56},{56,6... | collective-permute-start | bytes 491528 | tf_op jit(solution)/shard_map/while/body/eval_jaxpr/ppermute | solution.py:21
  64.6 12.6 %collective-permute-start = (bf16[64,1,5,128]{3,0,2,1:T(8,128)(2,1)S(1)}, bf16[64,1,5,128]{3,0,2,1:T(8,128)(2,1)S(1)}, u32[]{:S(2)}, u32[]{:S(2)}) collective-permute-start(bf16[64,1,5,128]{3,0,2,1:T(8,128)(2,1)S(1)} %copy.43), channel_id=1, source_target_pairs={{120,0},{0,8},{8,16},{16,24},{24,32},{32,40},{40,48},{48,56},{56,6... | collective-permute-start | bytes 245768 | tf_op jit(solution)/shard_map/while/body/eval_jaxpr/ppermute | solution.py:21
  67.6 7.1 %collective-permute-start.1 = (f32[64,1,5]{0,2,1:T(8,128)S(1)}, f32[64,1,5]{0,2,1:T(8,128)S(1)}, u32[]{:S(2)}, u32[]{:S(2)}) collective-permute-start(f32[64,1,5]{0,2,1:T(8,128)S(1)} %get-tuple-element.382), channel_id=1, source_target_pairs={{120,0},{0,8},{8,16},{16,24},{24,32},{32,40},{40,48},{48,56},{56,6... | collective-permute-start | bytes 3848 | tf_op jit(solution)/shard_map/while/body/eval_jaxpr/ppermute | solution.py:21
  71.7 5.5 %collective-permute-start.2 = (f32[64,1,5]{0,2,1:T(8,128)S(1)}, f32[64,1,5]{0,2,1:T(8,128)S(1)}, u32[]{:S(2)}, u32[]{:S(2)}) collective-permute-start(f32[64,1,5]{0,2,1:T(8,128)S(1)} %get-tuple-element.383), channel_id=1, source_target_pairs={{120,0},{0,8},{8,16},{16,24},{24,32},{32,40},{40,48},{48,56},{56,6... | collective-permute-start | bytes 3848 | tf_op jit(solution)/shard_map/while/body/eval_jaxpr/ppermute | solution.py:21
  82.2 14.3 %collective-permute-start.3 = (f32[64,1,5,128]{3,0,2,1:T(8,128)S(1)}, f32[64,1,5,128]{3,0,2,1:T(8,128)S(1)}, u32[]{:S(2)}, u32[]{:S(2)}) collective-permute-start(f32[64,1,5,128]{3,0,2,1:T(8,128)S(1)} %fusion.39), channel_id=1, source_target_pairs={{120,0},{0,8},{8,16},{16,24},{24,32},{32,40},{40,48},{48,56},{56,6... | collective-permute-start | bytes 491528 | tf_op jit(solution)/shard_map/while/body/eval_jaxpr/ppermute | solution.py:21
  85.2 11.4 %collective-permute-start = (bf16[64,1,5,128]{3,0,2,1:T(8,128)(2,1)S(1)}, bf16[64,1,5,128]{3,0,2,1:T(8,128)(2,1)S(1)}, u32[]{:S(2)}, u32[]{:S(2)}) collective-permute-start(bf16[64,1,5,128]{3,0,2,1:T(8,128)(2,1)S(1)} %copy.43), channel_id=1, source_target_pairs={{120,0},{0,8},{8,16},{16,24},{24,32},{32,40},{40,48},{48,56},{56,6... | collective-permute-start | bytes 245768 | tf_op jit(solution)/shard_map/while/body/eval_jaxpr/ppermute | solution.py:21
  87.1 6.9 %collective-permute-start.1 = (f32[64,1,5]{0,2,1:T(8,128)S(1)}, f32[64,1,5]{0,2,1:T(8,128)S(1)}, u32[]{:S(2)}, u32[]{:S(2)}) collective-permute-start(f32[64,1,5]{0,2,1:T(8,128)S(1)} %get-tuple-element.382), channel_id=1, source_target_pairs={{120,0},{0,8},{8,16},{16,24},{24,32},{32,40},{40,48},{48,56},{56,6... | collective-permute-start | bytes 3848 | tf_op jit(solution)/shard_map/while/body/eval_jaxpr/ppermute | solution.py:21
  91.0 5.5 %collective-permute-start.2 = (f32[64,1,5]{0,2,1:T(8,128)S(1)}, f32[64,1,5]{0,2,1:T(8,128)S(1)}, u32[]{:S(2)}, u32[]{:S(2)}) collective-permute-start(f32[64,1,5]{0,2,1:T(8,128)S(1)} %get-tuple-element.383), channel_id=1, source_target_pairs={{120,0},{0,8},{8,16},{16,24},{24,32},{32,40},{40,48},{48,56},{56,6... | collective-permute-start | bytes 3848 | tf_op jit(solution)/shard_map/while/body/eval_jaxpr/ppermute | solution.py:21
  101.5 14.5 %collective-permute-start.3 = (f32[64,1,5,128]{3,0,2,1:T(8,128)S(1)}, f32[64,1,5,128]{3,0,2,1:T(8,128)S(1)}, u32[]{:S(2)}, u32[]{:S(2)}) collective-permute-start(f32[64,1,5,128]{3,0,2,1:T(8,128)S(1)} %fusion.39), channel_id=1, source_target_pairs={{120,0},{0,8},{8,16},{16,24},{24,32},{32,40},{40,48},{48,56},{56,6... | collective-permute-start | bytes 491528 | tf_op jit(solution)/shard_map/while/body/eval_jaxpr/ppermute | solution.py:21
  104.5 11.6 %collective-permute-start = (bf16[64,1,5,128]{3,0,2,1:T(8,128)(2,1)S(1)}, bf16[64,1,5,128]{3,0,2,1:T(8,128)(2,1)S(1)}, u32[]{:S(2)}, u32[]{:S(2)}) collective-permute-start(bf16[64,1,5,128]{3,0,2,1:T(8,128)(2,1)S(1)} %copy.43), channel_id=1, source_target_pairs={{120,0},{0,8},{8,16},{16,24},{24,32},{32,40},{40,48},{48,56},{56,6... | collective-permute-start | bytes 245768 | tf_op jit(solution)/shard_map/while/body/eval_jaxpr/ppermute | solution.py:21
  107.4 5.5 %collective-permute-start.1 = (f32[64,1,5]{0,2,1:T(8,128)S(1)}, f32[64,1,5]{0,2,1:T(8,128)S(1)}, u32[]{:S(2)}, u32[]{:S(2)}) collective-permute-start(f32[64,1,5]{0,2,1:T(8,128)S(1)} %get-tuple-element.382), channel_id=1, source_target_pairs={{120,0},{0,8},{8,16},{16,24},{24,32},{32,40},{40,48},{48,56},{56,6... | collective-permute-start | bytes 3848 | tf_op jit(solution)/shard_map/while/body/eval_jaxpr/ppermute | solution.py:21
  110.5 5.5 %collective-permute-start.2 = (f32[64,1,5]{0,2,1:T(8,128)S(1)}, f32[64,1,5]{0,2,1:T(8,128)S(1)}, u32[]{:S(2)}, u32[]{:S(2)}) collective-permute-start(f32[64,1,5]{0,2,1:T(8,128)S(1)} %get-tuple-element.383), channel_id=1, source_target_pairs={{120,0},{0,8},{8,16},{16,24},{24,32},{32,40},{40,48},{48,56},{56,6... | collective-permute-start | bytes 3848 | tf_op jit(solution)/shard_map/while/body/eval_jaxpr/ppermute | solution.py:21
  121.1 12.5 %collective-permute-start.3 = (f32[64,1,5,128]{3,0,2,1:T(8,128)S(1)}, f32[64,1,5,128]{3,0,2,1:T(8,128)S(1)}, u32[]{:S(2)}, u32[]{:S(2)}) collective-permute-start(f32[64,1,5,128]{3,0,2,1:T(8,128)S(1)} %fusion.39), channel_id=1, source_target_pairs={{120,0},{0,8},{8,16},{16,24},{24,32},{32,40},{40,48},{48,56},{56,6... | collective-permute-start | bytes 491528 | tf_op jit(solution)/shard_map/while/body/eval_jaxpr/ppermute | solution.py:21
  123.0 10.6 %collective-permute-start = (bf16[64,1,5,128]{3,0,2,1:T(8,128)(2,1)S(1)}, bf16[64,1,5,128]{3,0,2,1:T(8,128)(2,1)S(1)}, u32[]{:S(2)}, u32[]{:S(2)}) collective-permute-start(bf16[64,1,5,128]{3,0,2,1:T(8,128)(2,1)S(1)} %copy.43), channel_id=1, source_target_pairs={{120,0},{0,8},{8,16},{16,24},{24,32},{32,40},{40,48},{48,56},{56,6... | collective-permute-start | bytes 245768 | tf_op jit(solution)/shard_map/while/body/eval_jaxpr/ppermute | solution.py:21
  124.9 5.5 %collective-permute-start.1 = (f32[64,1,5]{0,2,1:T(8,128)S(1)}, f32[64,1,5]{0,2,1:T(8,128)S(1)}, u32[]{:S(2)}, u32[]{:S(2)}) collective-permute-start(f32[64,1,5]{0,2,1:T(8,128)S(1)} %get-tuple-element.382), channel_id=1, source_target_pairs={{120,0},{0,8},{8,16},{16,24},{24,32},{32,40},{40,48},{48,56},{56,6... | collective-permute-start | bytes 3848 | tf_op jit(solution)/shard_map/while/body/eval_jaxpr/ppermute | solution.py:21
  128.1 5.5 %collective-permute-start.2 = (f32[64,1,5]{0,2,1:T(8,128)S(1)}, f32[64,1,5]{0,2,1:T(8,128)S(1)}, u32[]{:S(2)}, u32[]{:S(2)}) collective-permute-start(f32[64,1,5]{0,2,1:T(8,128)S(1)} %get-tuple-element.383), channel_id=1, source_target_pairs={{120,0},{0,8},{8,16},{16,24},{24,32},{32,40},{40,48},{48,56},{56,6... | collective-permute-start | bytes 3848 | tf_op jit(solution)/shard_map/while/body/eval_jaxpr/ppermute | solution.py:21
  138.6 16.5 %collective-permute-start.3 = (f32[64,1,5,128]{3,0,2,1:T(8,128)S(1)}, f32[64,1,5,128]{3,0,2,1:T(8,128)S(1)}, u32[]{:S(2)}, u32[]{:S(2)}) collective-permute-start(f32[64,1,5,128]{3,0,2,1:T(8,128)S(1)} %fusion.39), channel_id=1, source_target_pairs={{120,0},{0,8},{8,16},{16,24},{24,32},{32,40},{40,48},{48,56},{56,6... | collective-permute-start | bytes 491528 | tf_op jit(solution)/shard_map/while/body/eval_jaxpr/ppermute | solution.py:21
  140.7 14.4 %collective-permute-start = (bf16[64,1,5,128]{3,0,2,1:T(8,128)(2,1)S(1)}, bf16[64,1,5,128]{3,0,2,1:T(8,128)(2,1)S(1)}, u32[]{:S(2)}, u32[]{:S(2)}) collective-permute-start(bf16[64,1,5,128]{3,0,2,1:T(8,128)(2,1)S(1)} %copy.43), channel_id=1, source_target_pairs={{120,0},{0,8},{8,16},{16,24},{24,32},{32,40},{40,48},{48,56},{56,6... | collective-permute-start | bytes 245768 | tf_op jit(solution)/shard_map/while/body/eval_jaxpr/ppermute | solution.py:21
  144.5 8.8 %collective-permute-start.1 = (f32[64,1,5]{0,2,1:T(8,128)S(1)}, f32[64,1,5]{0,2,1:T(8,128)S(1)}, u32[]{:S(2)}, u32[]{:S(2)}) collective-permute-start(f32[64,1,5]{0,2,1:T(8,128)S(1)} %get-tuple-element.382), channel_id=1, source_target_pairs={{120,0},{0,8},{8,16},{16,24},{24,32},{32,40},{40,48},{48,56},{56,6... | collective-permute-start | bytes 3848 | tf_op jit(solution)/shard_map/while/body/eval_jaxpr/ppermute | solution.py:21
  149.6 5.5 %collective-permute-start.2 = (f32[64,1,5]{0,2,1:T(8,128)S(1)}, f32[64,1,5]{0,2,1:T(8,128)S(1)}, u32[]{:S(2)}, u32[]{:S(2)}) collective-permute-start(f32[64,1,5]{0,2,1:T(8,128)S(1)} %get-tuple-element.383), channel_id=1, source_target_pairs={{120,0},{0,8},{8,16},{16,24},{24,32},{32,40},{40,48},{48,56},{56,6... | collective-permute-start | bytes 3848 | tf_op jit(solution)/shard_map/while/body/eval_jaxpr/ppermute | solution.py:21
  160.1 17.3 %collective-permute-start.3 = (f32[64,1,5,128]{3,0,2,1:T(8,128)S(1)}, f32[64,1,5,128]{3,0,2,1:T(8,128)S(1)}, u32[]{:S(2)}, u32[]{:S(2)}) collective-permute-start(f32[64,1,5,128]{3,0,2,1:T(8,128)S(1)} %fusion.39), channel_id=1, source_target_pairs={{120,0},{0,8},{8,16},{16,24},{24,32},{32,40},{40,48},{48,56},{56,6... | collective-permute-start | bytes 491528 | tf_op jit(solution)/shard_map/while/body/eval_jaxpr/ppermute | solution.py:21
  163.9 13.6 %collective-permute-start = (bf16[64,1,5,128]{3,0,2,1:T(8,128)(2,1)S(1)}, bf16[64,1,5,128]{3,0,2,1:T(8,128)(2,1)S(1)}, u32[]{:S(2)}, u32[]{:S(2)}) collective-permute-start(bf16[64,1,5,128]{3,0,2,1:T(8,128)(2,1)S(1)} %copy.43), channel_id=1, source_target_pairs={{120,0},{0,8},{8,16},{16,24},{24,32},{32,40},{40,48},{48,56},{56,6... | collective-permute-start | bytes 245768 | tf_op jit(solution)/shard_map/while/body/eval_jaxpr/ppermute | solution.py:21
  167.8 7.1 %collective-permute-start.1 = (f32[64,1,5]{0,2,1:T(8,128)S(1)}, f32[64,1,5]{0,2,1:T(8,128)S(1)}, u32[]{:S(2)}, u32[]{:S(2)}) collective-permute-start(f32[64,1,5]{0,2,1:T(8,128)S(1)} %get-tuple-element.382), channel_id=1, source_target_pairs={{120,0},{0,8},{8,16},{16,24},{24,32},{32,40},{40,48},{48,56},{56,6... | collective-permute-start | bytes 3848 | tf_op jit(solution)/shard_map/while/body/eval_jaxpr/ppermute | solution.py:21
  172.0 5.5 %collective-permute-start.2 = (f32[64,1,5]{0,2,1:T(8,128)S(1)}, f32[64,1,5]{0,2,1:T(8,128)S(1)}, u32[]{:S(2)}, u32[]{:S(2)}) collective-permute-start(f32[64,1,5]{0,2,1:T(8,128)S(1)} %get-tuple-element.383), channel_id=1, source_target_pairs={{120,0},{0,8},{8,16},{16,24},{24,32},{32,40},{40,48},{48,56},{56,6... | collective-permute-start | bytes 3848 | tf_op jit(solution)/shard_map/while/body/eval_jaxpr/ppermute | solution.py:21
  182.5 14.5 %collective-permute-start.3 = (f32[64,1,5,128]{3,0,2,1:T(8,128)S(1)}, f32[64,1,5,128]{3,0,2,1:T(8,128)S(1)}, u32[]{:S(2)}, u32[]{:S(2)}) collective-permute-start(f32[64,1,5,128]{3,0,2,1:T(8,128)S(1)} %fusion.39), channel_id=1, source_target_pairs={{120,0},{0,8},{8,16},{16,24},{24,32},{32,40},{40,48},{48,56},{56,6... | collective-permute-start | bytes 491528 | tf_op jit(solution)/shard_map/while/body/eval_jaxpr/ppermute | solution.py:21
  185.4 11.6 %collective-permute-start = (bf16[64,1,5,128]{3,0,2,1:T(8,128)(2,1)S(1)}, bf16[64,1,5,128]{3,0,2,1:T(8,128)(2,1)S(1)}, u32[]{:S(2)}, u32[]{:S(2)}) collective-permute-start(bf16[64,1,5,128]{3,0,2,1:T(8,128)(2,1)S(1)} %copy.43), channel_id=1, source_target_pairs={{120,0},{0,8},{8,16},{16,24},{24,32},{32,40},{40,48},{48,56},{56,6... | collective-permute-start | bytes 245768 | tf_op jit(solution)/shard_map/while/body/eval_jaxpr/ppermute | solution.py:21
  188.3 5.9 %collective-permute-start.1 = (f32[64,1,5]{0,2,1:T(8,128)S(1)}, f32[64,1,5]{0,2,1:T(8,128)S(1)}, u32[]{:S(2)}, u32[]{:S(2)}) collective-permute-start(f32[64,1,5]{0,2,1:T(8,128)S(1)} %get-tuple-element.382), channel_id=1, source_target_pairs={{120,0},{0,8},{8,16},{16,24},{24,32},{32,40},{40,48},{48,56},{56,6... | collective-permute-start | bytes 3848 | tf_op jit(solution)/shard_map/while/body/eval_jaxpr/ppermute | solution.py:21
  191.5 5.5 %collective-permute-start.2 = (f32[64,1,5]{0,2,1:T(8,128)S(1)}, f32[64,1,5]{0,2,1:T(8,128)S(1)}, u32[]{:S(2)}, u32[]{:S(2)}) collective-permute-start(f32[64,1,5]{0,2,1:T(8,128)S(1)} %get-tuple-element.383), channel_id=1, source_target_pairs={{120,0},{0,8},{8,16},{16,24},{24,32},{32,40},{40,48},{48,56},{56,6... | collective-permute-start | bytes 3848 | tf_op jit(solution)/shard_map/while/body/eval_jaxpr/ppermute | solution.py:21
  202.0 15.3 %collective-permute-start.3 = (f32[64,1,5,128]{3,0,2,1:T(8,128)S(1)}, f32[64,1,5,128]{3,0,2,1:T(8,128)S(1)}, u32[]{:S(2)}, u32[]{:S(2)}) collective-permute-start(f32[64,1,5,128]{3,0,2,1:T(8,128)S(1)} %fusion.39), channel_id=1, source_target_pairs={{120,0},{0,8},{8,16},{16,24},{24,32},{32,40},{40,48},{48,56},{56,6... | collective-permute-start | bytes 491528 | tf_op jit(solution)/shard_map/while/body/eval_jaxpr/ppermute | solution.py:21
  204.7 12.6 %collective-permute-start = (bf16[64,1,5,128]{3,0,2,1:T(8,128)(2,1)S(1)}, bf16[64,1,5,128]{3,0,2,1:T(8,128)(2,1)S(1)}, u32[]{:S(2)}, u32[]{:S(2)}) collective-permute-start(bf16[64,1,5,128]{3,0,2,1:T(8,128)(2,1)S(1)} %copy.43), channel_id=1, source_target_pairs={{120,0},{0,8},{8,16},{16,24},{24,32},{32,40},{40,48},{48,56},{56,6... | collective-permute-start | bytes 245768 | tf_op jit(solution)/shard_map/while/body/eval_jaxpr/ppermute | solution.py:21
  207.6 6.1 %collective-permute-start.1 = (f32[64,1,5]{0,2,1:T(8,128)S(1)}, f32[64,1,5]{0,2,1:T(8,128)S(1)}, u32[]{:S(2)}, u32[]{:S(2)}) collective-permute-start(f32[64,1,5]{0,2,1:T(8,128)S(1)} %get-tuple-element.382), channel_id=1, source_target_pairs={{120,0},{0,8},{8,16},{16,24},{24,32},{32,40},{40,48},{48,56},{56,6... | collective-permute-start | bytes 3848 | tf_op jit(solution)/shard_map/while/body/eval_jaxpr/ppermute | solution.py:21
  211.8 5.5 %collective-permute-start.2 = (f32[64,1,5]{0,2,1:T(8,128)S(1)}, f32[64,1,5]{0,2,1:T(8,128)S(1)}, u32[]{:S(2)}, u32[]{:S(2)}) collective-permute-start(f32[64,1,5]{0,2,1:T(8,128)S(1)} %get-tuple-element.383), channel_id=1, source_target_pairs={{120,0},{0,8},{8,16},{16,24},{24,32},{32,40},{40,48},{48,56},{56,6... | collective-permute-start | bytes 3848 | tf_op jit(solution)/shard_map/while/body/eval_jaxpr/ppermute | solution.py:21
  222.3 12.5 %collective-permute-start.3 = (f32[64,1,5,128]{3,0,2,1:T(8,128)S(1)}, f32[64,1,5,128]{3,0,2,1:T(8,128)S(1)}, u32[]{:S(2)}, u32[]{:S(2)}) collective-permute-start(f32[64,1,5,128]{3,0,2,1:T(8,128)S(1)} %fusion.39), channel_id=1, source_target_pairs={{120,0},{0,8},{8,16},{16,24},{24,32},{32,40},{40,48},{48,56},{56,6... | collective-permute-start | bytes 491528 | tf_op jit(solution)/shard_map/while/body/eval_jaxpr/ppermute | solution.py:21
  224.2 10.6 %collective-permute-start = (bf16[64,1,5,128]{3,0,2,1:T(8,128)(2,1)S(1)}, bf16[64,1,5,128]{3,0,2,1:T(8,128)(2,1)S(1)}, u32[]{:S(2)}, u32[]{:S(2)}) collective-permute-start(bf16[64,1,5,128]{3,0,2,1:T(8,128)(2,1)S(1)} %copy.43), channel_id=1, source_target_pairs={{120,0},{0,8},{8,16},{16,24},{24,32},{32,40},{40,48},{48,56},{56,6... | collective-permute-start | bytes 245768 | tf_op jit(solution)/shard_map/while/body/eval_jaxpr/ppermute | solution.py:21
  226.1 5.5 %collective-permute-start.1 = (f32[64,1,5]{0,2,1:T(8,128)S(1)}, f32[64,1,5]{0,2,1:T(8,128)S(1)}, u32[]{:S(2)}, u32[]{:S(2)}) collective-permute-start(f32[64,1,5]{0,2,1:T(8,128)S(1)} %get-tuple-element.382), channel_id=1, source_target_pairs={{120,0},{0,8},{8,16},{16,24},{24,32},{32,40},{40,48},{48,56},{56,6... | collective-permute-start | bytes 3848 | tf_op jit(solution)/shard_map/while/body/eval_jaxpr/ppermute | solution.py:21
  229.3 5.5 %collective-permute-start.2 = (f32[64,1,5]{0,2,1:T(8,128)S(1)}, f32[64,1,5]{0,2,1:T(8,128)S(1)}, u32[]{:S(2)}, u32[]{:S(2)}) collective-permute-start(f32[64,1,5]{0,2,1:T(8,128)S(1)} %get-tuple-element.383), channel_id=1, source_target_pairs={{120,0},{0,8},{8,16},{16,24},{24,32},{32,40},{40,48},{48,56},{56,6... | collective-permute-start | bytes 3848 | tf_op jit(solution)/shard_map/while/body/eval_jaxpr/ppermute | solution.py:21
  239.8 14.5 %collective-permute-start.3 = (f32[64,1,5,128]{3,0,2,1:T(8,128)S(1)}, f32[64,1,5,128]{3,0,2,1:T(8,128)S(1)}, u32[]{:S(2)}, u32[]{:S(2)}) collective-permute-start(f32[64,1,5,128]{3,0,2,1:T(8,128)S(1)} %fusion.39), channel_id=1, source_target_pairs={{120,0},{0,8},{8,16},{16,24},{24,32},{32,40},{40,48},{48,56},{56,6... | collective-permute-start | bytes 491528 | tf_op jit(solution)/shard_map/while/body/eval_jaxpr/ppermute | solution.py:21
  241.7 12.6 %collective-permute-start = (bf16[64,1,5,128]{3,0,2,1:T(8,128)(2,1)S(1)}, bf16[64,1,5,128]{3,0,2,1:T(8,128)(2,1)S(1)}, u32[]{:S(2)}, u32[]{:S(2)}) collective-permute-start(bf16[64,1,5,128]{3,0,2,1:T(8,128)(2,1)S(1)} %copy.43), channel_id=1, source_target_pairs={{120,0},{0,8},{8,16},{16,24},{24,32},{32,40},{40,48},{48,56},{56,6... | collective-permute-start | bytes 245768 | tf_op jit(solution)/shard_map/while/body/eval_jaxpr/ppermute | solution.py:21
  243.8 9.0 %collective-permute-start.1 = (f32[64,1,5]{0,2,1:T(8,128)S(1)}, f32[64,1,5]{0,2,1:T(8,128)S(1)}, u32[]{:S(2)}, u32[]{:S(2)}) collective-permute-start(f32[64,1,5]{0,2,1:T(8,128)S(1)} %get-tuple-element.382), channel_id=1, source_target_pairs={{120,0},{0,8},{8,16},{16,24},{24,32},{32,40},{40,48},{48,56},{56,6... | collective-permute-start | bytes 3848 | tf_op jit(solution)/shard_map/while/body/eval_jaxpr/ppermute | solution.py:21
  248.8 5.5 %collective-permute-start.2 = (f32[64,1,5]{0,2,1:T(8,128)S(1)}, f32[64,1,5]{0,2,1:T(8,128)S(1)}, u32[]{:S(2)}, u32[]{:S(2)}) collective-permute-start(f32[64,1,5]{0,2,1:T(8,128)S(1)} %get-tuple-element.383), channel_id=1, source_target_pairs={{120,0},{0,8},{8,16},{16,24},{24,32},{32,40},{40,48},{48,56},{56,6... | collective-permute-start | bytes 3848 | tf_op jit(solution)/shard_map/while/body/eval_jaxpr/ppermute | solution.py:21
  259.3 18.2 %collective-permute-start.3 = (f32[64,1,5,128]{3,0,2,1:T(8,128)S(1)}, f32[64,1,5,128]{3,0,2,1:T(8,128)S(1)}, u32[]{:S(2)}, u32[]{:S(2)}) collective-permute-start(f32[64,1,5,128]{3,0,2,1:T(8,128)S(1)} %fusion.39), channel_id=1, source_target_pairs={{120,0},{0,8},{8,16},{16,24},{24,32},{32,40},{40,48},{48,56},{56,6... | collective-permute-start | bytes 491528 | tf_op jit(solution)/shard_map/while/body/eval_jaxpr/ppermute | solution.py:21
  263.2 14.3 %collective-permute-start = (bf16[64,1,5,128]{3,0,2,1:T(8,128)(2,1)S(1)}, bf16[64,1,5,128]{3,0,2,1:T(8,128)(2,1)S(1)}, u32[]{:S(2)}, u32[]{:S(2)}) collective-permute-start(bf16[64,1,5,128]{3,0,2,1:T(8,128)(2,1)S(1)} %copy.43), channel_id=1, source_target_pairs={{120,0},{0,8},{8,16},{16,24},{24,32},{32,40},{40,48},{48,56},{56,6... | collective-permute-start | bytes 245768 | tf_op jit(solution)/shard_map/while/body/eval_jaxpr/ppermute | solution.py:21
  266.9 8.1 %collective-permute-start.1 = (f32[64,1,5]{0,2,1:T(8,128)S(1)}, f32[64,1,5]{0,2,1:T(8,128)S(1)}, u32[]{:S(2)}, u32[]{:S(2)}) collective-permute-start(f32[64,1,5]{0,2,1:T(8,128)S(1)} %get-tuple-element.382), channel_id=1, source_target_pairs={{120,0},{0,8},{8,16},{16,24},{24,32},{32,40},{40,48},{48,56},{56,6... | collective-permute-start | bytes 3848 | tf_op jit(solution)/shard_map/while/body/eval_jaxpr/ppermute | solution.py:21
  272.0 5.5 %collective-permute-start.2 = (f32[64,1,5]{0,2,1:T(8,128)S(1)}, f32[64,1,5]{0,2,1:T(8,128)S(1)}, u32[]{:S(2)}, u32[]{:S(2)}) collective-permute-start(f32[64,1,5]{0,2,1:T(8,128)S(1)} %get-tuple-element.383), channel_id=1, source_target_pairs={{120,0},{0,8},{8,16},{16,24},{24,32},{32,40},{40,48},{48,56},{56,6... | collective-permute-start | bytes 3848 | tf_op jit(solution)/shard_map/while/body/eval_jaxpr/ppermute | solution.py:21
  282.6 15.5 %collective-permute-start.3 = (f32[64,1,5,128]{3,0,2,1:T(8,128)S(1)}, f32[64,1,5,128]{3,0,2,1:T(8,128)S(1)}, u32[]{:S(2)}, u32[]{:S(2)}) collective-permute-start(f32[64,1,5,128]{3,0,2,1:T(8,128)S(1)} %fusion.39), channel_id=1, source_target_pairs={{120,0},{0,8},{8,16},{16,24},{24,32},{32,40},{40,48},{48,56},{56,6... | collective-permute-start | bytes 491528 | tf_op jit(solution)/shard_map/while/body/eval_jaxpr/ppermute | solution.py:21
  285.5 12.6 %collective-permute-start = (bf16[64,1,5,128]{3,0,2,1:T(8,128)(2,1)S(1)}, bf16[64,1,5,128]{3,0,2,1:T(8,128)(2,1)S(1)}, u32[]{:S(2)}, u32[]{:S(2)}) collective-permute-start(bf16[64,1,5,128]{3,0,2,1:T(8,128)(2,1)S(1)} %copy.43), channel_id=1, source_target_pairs={{120,0},{0,8},{8,16},{16,24},{24,32},{32,40},{40,48},{48,56},{56,6... | collective-permute-start | bytes 245768 | tf_op jit(solution)/shard_map/while/body/eval_jaxpr/ppermute | solution.py:21
  288.5 6.1 %collective-permute-start.1 = (f32[64,1,5]{0,2,1:T(8,128)S(1)}, f32[64,1,5]{0,2,1:T(8,128)S(1)}, u32[]{:S(2)}, u32[]{:S(2)}) collective-permute-start(f32[64,1,5]{0,2,1:T(8,128)S(1)} %get-tuple-element.382), channel_id=1, source_target_pairs={{120,0},{0,8},{8,16},{16,24},{24,32},{32,40},{40,48},{48,56},{56,6... | collective-permute-start | bytes 3848 | tf_op jit(solution)/shard_map/while/body/eval_jaxpr/ppermute | solution.py:21
  292.6 5.5 %collective-permute-start.2 = (f32[64,1,5]{0,2,1:T(8,128)S(1)}, f32[64,1,5]{0,2,1:T(8,128)S(1)}, u32[]{:S(2)}, u32[]{:S(2)}) collective-permute-start(f32[64,1,5]{0,2,1:T(8,128)S(1)} %get-tuple-element.383), channel_id=1, source_target_pairs={{120,0},{0,8},{8,16},{16,24},{24,32},{32,40},{40,48},{48,56},{56,6... | collective-permute-start | bytes 3848 | tf_op jit(solution)/shard_map/while/body/eval_jaxpr/ppermute | solution.py:21
  303.1 14.4 %collective-permute-start.3 = (f32[64,1,5,128]{3,0,2,1:T(8,128)S(1)}, f32[64,1,5,128]{3,0,2,1:T(8,128)S(1)}, u32[]{:S(2)}, u32[]{:S(2)}) collective-permute-start(f32[64,1,5,128]{3,0,2,1:T(8,128)S(1)} %fusion.39), channel_id=1, source_target_pairs={{120,0},{0,8},{8,16},{16,24},{24,32},{32,40},{40,48},{48,56},{56,6... | collective-permute-start | bytes 491528 | tf_op jit(solution)/shard_map/while/body/eval_jaxpr/ppermute | solution.py:21
  305.1 12.4 %collective-permute-start = (bf16[64,1,5,128]{3,0,2,1:T(8,128)(2,1)S(1)}, bf16[64,1,5,128]{3,0,2,1:T(8,128)(2,1)S(1)}, u32[]{:S(2)}, u32[]{:S(2)}) collective-permute-start(bf16[64,1,5,128]{3,0,2,1:T(8,128)(2,1)S(1)} %copy.43), channel_id=1, source_target_pairs={{120,0},{0,8},{8,16},{16,24},{24,32},{32,40},{40,48},{48,56},{56,6... | collective-permute-start | bytes 245768 | tf_op jit(solution)/shard_map/while/body/eval_jaxpr/ppermute | solution.py:21
  307.7 7.1 %collective-permute-start.1 = (f32[64,1,5]{0,2,1:T(8,128)S(1)}, f32[64,1,5]{0,2,1:T(8,128)S(1)}, u32[]{:S(2)}, u32[]{:S(2)}) collective-permute-start(f32[64,1,5]{0,2,1:T(8,128)S(1)} %get-tuple-element.382), channel_id=1, source_target_pairs={{120,0},{0,8},{8,16},{16,24},{24,32},{32,40},{40,48},{48,56},{56,6... | collective-permute-start | bytes 3848 | tf_op jit(solution)/shard_map/while/body/eval_jaxpr/ppermute | solution.py:21
  311.9 5.6 %collective-permute-start.2 = (f32[64,1,5]{0,2,1:T(8,128)S(1)}, f32[64,1,5]{0,2,1:T(8,128)S(1)}, u32[]{:S(2)}, u32[]{:S(2)}) collective-permute-start(f32[64,1,5]{0,2,1:T(8,128)S(1)} %get-tuple-element.383), channel_id=1, source_target_pairs={{120,0},{0,8},{8,16},{16,24},{24,32},{32,40},{40,48},{48,56},{56,6... | collective-permute-start | bytes 3848 | tf_op jit(solution)/shard_map/while/body/eval_jaxpr/ppermute | solution.py:21
  322.5 20.2 %collective-permute-start.3 = (f32[64,1,5,128]{3,0,2,1:T(8,128)S(1)}, f32[64,1,5,128]{3,0,2,1:T(8,128)S(1)}, u32[]{:S(2)}, u32[]{:S(2)}) collective-permute-start(f32[64,1,5,128]{3,0,2,1:T(8,128)S(1)} %fusion.39), channel_id=1, source_target_pairs={{120,0},{0,8},{8,16},{16,24},{24,32},{32,40},{40,48},{48,56},{56,6... | collective-permute-start | bytes 491528 | tf_op jit(solution)/shard_map/while/body/eval_jaxpr/ppermute | solution.py:21
  328.3 14.3 %collective-permute-start = (bf16[64,1,5,128]{3,0,2,1:T(8,128)(2,1)S(1)}, bf16[64,1,5,128]{3,0,2,1:T(8,128)(2,1)S(1)}, u32[]{:S(2)}, u32[]{:S(2)}) collective-permute-start(bf16[64,1,5,128]{3,0,2,1:T(8,128)(2,1)S(1)} %copy.43), channel_id=1, source_target_pairs={{120,0},{0,8},{8,16},{16,24},{24,32},{32,40},{40,48},{48,56},{56,6... | collective-permute-start | bytes 245768 | tf_op jit(solution)/shard_map/while/body/eval_jaxpr/ppermute | solution.py:21
  330.3 12.0 %collective-permute-start.1 = (f32[64,1,5]{0,2,1:T(8,128)S(1)}, f32[64,1,5]{0,2,1:T(8,128)S(1)}, u32[]{:S(2)}, u32[]{:S(2)}) collective-permute-start(f32[64,1,5]{0,2,1:T(8,128)S(1)} %get-tuple-element.382), channel_id=1, source_target_pairs={{120,0},{0,8},{8,16},{16,24},{24,32},{32,40},{40,48},{48,56},{56,6... | collective-permute-start | bytes 3848 | tf_op jit(solution)/shard_map/while/body/eval_jaxpr/ppermute | solution.py:21
  332.2 10.5 %collective-permute-start.2 = (f32[64,1,5]{0,2,1:T(8,128)S(1)}, f32[64,1,5]{0,2,1:T(8,128)S(1)}, u32[]{:S(2)}, u32[]{:S(2)}) collective-permute-start(f32[64,1,5]{0,2,1:T(8,128)S(1)} %get-tuple-element.383), channel_id=1, source_target_pairs={{120,0},{0,8},{8,16},{16,24},{24,32},{32,40},{40,48},{48,56},{56,6... | collective-permute-start | bytes 3848 | tf_op jit(solution)/shard_map/while/body/eval_jaxpr/ppermute | solution.py:21
  (3 other events, 51.5 us)
where the time goes:
time: 414 us; the launch traced here: 411 us
  starting transfers between devices  204 us (49%)
  blocking collectives  66.3 us (16%)
  local copies, waits for them, and re-layouts  64.6 us (16%)
  waiting for transfers between devices  48.6 us (12%)
  matrix products  14.7 us (4%)
  other arithmetic  10.1 us (2%)
    ppermute x64, starting transfers between devices, passed_along(): return lax.ppermute(block, axis, route)  204 us
    ppermute x64, waiting for transfers between devices, passed_along(): return lax.ppermute(block, axis, route)  48.6 us
    all_to_all x1, blocking collectives, from_everyone(): lax.all_to_all(jnp.broadcast_to(x[None], (size, *x.shape)), axis, 0, 0, t...  45.5 us
    gather x16, local copies, waits for them, and re-layouts, prefix_part(): value_rows = block_values[chosen].reshape(MOST * BLOCK, kv_heads, HD)  29.2 us
    gather x16, local copies, waits for them, and re-layouts, prefix_part(): key_rows = block_keys[chosen].reshape(MOST * BLOCK, kv_heads, HD)  29.1 us
    all_to_all x1, blocking collectives, sent_and_summed(): lax.all_to_all(pieces, axis, split_axis=0, concat_axis=0, tiled=True)  20.8 us
  transfers between devices with their start and end apart: 64, of which 20 were waited for; matrix products, arithmetic and copies ran while one was open for 0% of the time, Pallas kernels for 0%

commit v1 on v0

v1 whole, which is shorter than its diff:
```python
import functools
import math

import jax
import jax.numpy as jnp
from jax import lax
from jax.experimental import pallas as pl
from jax.experimental.pallas import tpu as pltpu
from jax.sharding import PartitionSpec as P

HD = 128
GQA = 5
QB = 64
BLOCK = 128
MOST = 8
STEP = 4
ROWS = GQA * QB
FLOOR = -1e30
HIDDEN = -2e30
SCALE2 = math.log2(math.e) / math.sqrt(HD)
WIRE = HD + 16
VMEM_LIMIT = 48 * 2**20


def in_vmem():
    return pl.BlockSpec(memory_space=pltpu.VMEM)


def in_smem():
    return pl.BlockSpec(memory_space=pltpu.SMEM)


def params():
    return pltpu.CompilerParams(vmem_limit_bytes=VMEM_LIMIT)


def slots_kernel(pos_ref, kept_ref, out_ref, *, blocks_here):
    rel = kept_ref[...] - pos_ref[0] * blocks_here
    samples, keep = rel.shape
    lane = lax.broadcasted_iota(jnp.int32, (samples, 128), 1)
    present = jnp.zeros((samples, 128), jnp.int32)
    for i in range(keep):
        present = jnp.where(rel[:, i : i + 1] == lane, 1, present)
    present = jnp.where(lane < blocks_here, present, 0)
    earlier = lax.broadcasted_iota(jnp.int32, (128, 128), 0) < lax.broadcasted_iota(
        jnp.int32, (128, 128), 1
    )
    rank = jnp.dot(
        present.astype(jnp.float32).astype(jnp.bfloat16),
        earlier.astype(jnp.float32).astype(jnp.bfloat16),
        preferred_element_type=jnp.float32,
    ).astype(jnp.int32)
    out = jnp.where(lane == MOST, jnp.sum(present, axis=1, keepdims=True), 0)
    for k in range(MOST):
        chosen = jnp.sum(
            jnp.where((present > 0) & (rank == k), lane, 0), axis=1, keepdims=True
        )
        out = jnp.where(lane == k, chosen, out)
    out_ref[...] = out


def query_rows(q):
    return jnp.concatenate([q[:, j * HD : (j + 1) * HD] for j in range(GQA)], axis=0)


def online_step(carry, scores, values_t):
    top, acc = carry
    new_top = jnp.maximum(top, jnp.max(scores, axis=0, keepdims=True))
    prob = jnp.exp2(scores - new_top).astype(jnp.bfloat16)
    ones = jnp.ones((8, values_t.shape[1]), jnp.bfloat16)
    summed = jnp.dot(
        jnp.concatenate([values_t, ones], axis=0), prob, preferred_element_type=jnp.float32
    )
    return new_top, acc * jnp.exp2(top - new_top) + summed


def start_carry():
    return (
        jnp.full((1, ROWS), FLOOR, jnp.float32),
        jnp.zeros((HD + 8, ROWS), jnp.float32),
    )


def finish(carry):
    top, acc = carry
    total = acc[HD : HD + 1]
    some = total > 0.0
    safe = jnp.where(some, total, 1.0)
    return acc[:HD] / safe, jnp.where(some, top + jnp.log2(safe), FLOOR)


def wire(out, log_sum):
    high = log_sum.astype(jnp.bfloat16)
    rest = log_sum - high.astype(jnp.float32)
    middle = rest.astype(jnp.bfloat16)
    low = (rest - middle.astype(jnp.float32)).astype(jnp.bfloat16)
    row = lax.broadcasted_iota(jnp.int32, (16, out.shape[1]), 0)
    parts = jnp.where(
        row == 0,
        high.astype(jnp.float32),
        jnp.where(row == 1, middle.astype(jnp.float32), low.astype(jnp.float32)),
    )
    return jnp.concatenate([out, parts], axis=0).astype(jnp.bfloat16)


def unwire(packed):
    packed = packed.astype(jnp.float32)
    log_sum = packed[HD : HD + 1] + packed[HD + 1 : HD + 2] + packed[HD + 2 : HD + 3]
    return packed[:HD], log_sum


def merged(parts):
    top = functools.reduce(jnp.maximum, [log_sum for _, log_sum in parts])
    shares = [jnp.exp2(log_sum - top) for _, log_sum in parts]
    total = functools.reduce(jnp.add, shares)
    out = functools.reduce(
        jnp.add, [part * share for (part, _), share in zip(parts, shares, strict=True)]
    )
    return out / total, top + jnp.log2(total)


def prefix_kernel(pos_ref, slots_ref, *refs, offset, classes, ranges):
    q_refs, (k_ref, v_ref, out_ref) = refs[: len(ranges)], refs[len(ranges) :]
    group = lax.rem(pos_ref[0] + offset, classes)
    k = 0
    for q_ref, many in zip(q_refs, ranges, strict=True):
        for i in range(many):
            sample = group + classes * k
            count = slots_ref[sample, MOST]
            asking = query_rows(q_ref[i])

            def step(n, carry, sample=sample, count=count, asking=asking):
                scores, values_t = [], []
                for j in range(STEP):
                    slot = n * STEP + j
                    rows = pl.ds(pl.multiple_of(slots_ref[sample, slot] * BLOCK, BLOCK), BLOCK)
                    found = lax.dot_general(
                        k_ref[rows, :],
                        asking,
                        (((1,), (1,)), ((), ())),
                        preferred_element_type=jnp.float32,
                    )
                    bias = jnp.where(slot < count, 0.0, HIDDEN).astype(jnp.float32)
                    scores.append(found * SCALE2 + bias)
                    values_t.append(v_ref[rows, :].T)
                return online_step(
                    carry, jnp.concatenate(scores, axis=0), jnp.concatenate(values_t, axis=1)
                )

            carry = lax.fori_loop(0, lax.div(count + STEP - 1, STEP), step, start_carry())
            out_ref[:, k * ROWS : (k + 1) * ROWS] = wire(*finish(carry))
            k += 1


def suffix_kernel(length_ref, q_ref, k_ref, v_ref, out_ref):
    chunk = STEP * BLOCK
    asking = query_rows(q_ref[0])
    length = length_ref[0]
    token = lax.rem(lax.broadcasted_iota(jnp.int32, (chunk, ROWS), 1), QB)
    slot = lax.broadcasted_iota(jnp.int32, (chunk, ROWS), 0)

    def step(n, carry):
        rows = pl.ds(pl.multiple_of(n * chunk, chunk), chunk)
        scores = (
            lax.dot_general(
                k_ref[0, rows, :],
                asking,
                (((1,), (1,)), ((), ())),
                preferred_element_type=jnp.float32,
            )
            * SCALE2
        )
        scores = jnp.where(slot - token <= length - QB - n * chunk, scores, HIDDEN)
        return online_step(carry, scores, v_ref[0, rows, :].T)

    carry = lax.fori_loop(0, lax.div(length + chunk - 1, chunk), step, start_carry())
    out, log_sum = finish(carry)
    out_ref[:HD, :] = out
    out_ref[HD:, :] = jnp.broadcast_to(log_sum, (8, ROWS))


def class_kernel(own_ref, before_ref, after_ref, first_ref, second_ref, out_ref, *, members):
    half = first_ref.shape[1]
    for k in range(members):
        lanes = slice(k * ROWS, (k + 1) * ROWS)
        far = first_ref[:, lanes] if k * ROWS < half else second_ref[:, k * ROWS - half : (k + 1) * ROWS - half]
        parts = [
            unwire(x) for x in (own_ref[:, lanes], before_ref[:, lanes], after_ref[:, lanes], far)
        ]
        out_ref[k] = wire(*merged(parts))


def final_kernel(suffix_ref, parts_ref, out_ref):
    parts = [(suffix_ref[:HD, :], suffix_ref[HD : HD + 1, :])]
    parts += [unwire(parts_ref[i]) for i in range(parts_ref.shape[0])]
    out, _ = merged(parts)
    out_ref[0] = out.T.astype(jnp.bfloat16)


def project_kernel(pos_ref, *refs, classes, layout):
    in_refs, (w_ref, out_ref) = refs[: len(layout)], refs[len(layout) :]
    weight = w_ref[...]
    for ref, (offset, first) in zip(in_refs, layout, strict=True):
        group = lax.rem(pos_ref[0] + offset, classes)
        many = ref.shape[0]
        stacked = []
        for i in range(many):
            rows = ref[i]
            stacked.append(
                jnp.concatenate([rows[j * QB : (j + 1) * QB] for j in range(GQA)], axis=1)
            )
        result = jnp.dot(
            jnp.concatenate(stacked, axis=0), weight, preferred_element_type=jnp.float32
        ).astype(jnp.bfloat16)
        for i in range(many):
            sample = group + classes * (first + i)
            out_ref[pl.ds(pl.multiple_of(sample * QB, QB), QB), :] = result[i * QB : (i + 1) * QB]


def shifted(x, distance):
    size = lax.axis_size("seq")
    return lax.ppermute(x, "seq", [((i + distance) % size, i) for i in range(size)])


def body(
    queries,
    prefix_keys,
    prefix_values,
    suffix_keys,
    suffix_values,
    kept_blocks,
    suffix_lengths,
    out_weight,
):
    size, heads = lax.axis_size("seq"), lax.axis_size("head")
    classes = 4
    members = size // classes
    half = members // 2
    groups = [[g + classes * i for i in range(members)] for g in range(classes)]
    position = lax.axis_index("seq").astype(jnp.int32).reshape(1)
    blocks_here = prefix_keys.shape[0] // BLOCK
    bf16, f32 = jnp.bfloat16, jnp.float32

    slots = pl.pallas_call(
        functools.partial(slots_kernel, blocks_here=blocks_here),
        out_shape=jax.ShapeDtypeStruct((kept_blocks.shape[0], 128), jnp.int32),
        in_specs=[in_smem(), in_vmem()],
        out_specs=in_vmem(),
        name="kept_slots",
    )(position, kept_blocks)

    def prefix_part(offset, *asked):
        ranges = tuple(a.shape[0] for a in asked)
        return pl.pallas_call(
            functools.partial(prefix_kernel, offset=offset, classes=classes, ranges=ranges),
            out_shape=jax.ShapeDtypeStruct((WIRE, sum(ranges) * ROWS), bf16),
            in_specs=[in_smem(), in_smem()] + [in_vmem()] * (len(asked) + 2),
            out_specs=in_vmem(),
            compiler_params=params(),
            name="prefix_part",
        )(position, slots, *asked, prefix_keys, prefix_values)

    suffix = pl.pallas_call(
        suffix_kernel,
        out_shape=jax.ShapeDtypeStruct((HD + 8, ROWS), f32),
        in_specs=[in_smem()] + [in_vmem()] * 3,
        out_specs=in_vmem(),
        compiler_params=params(),
        name="suffix_part",
    )(suffix_lengths, queries, suffix_keys, suffix_values)

    mine = lax.all_gather(queries, "seq", axis=0, tiled=True, axis_index_groups=groups)
    from_after = shifted(mine, 1)
    from_before = shifted(mine, -1)
    from_far = (shifted(mine[:half], 2), shifted(mine[half:], -2))

    own = prefix_part(0, mine)
    for_after = prefix_part(1, from_after)
    for_before = prefix_part(3, from_before)
    for_far = prefix_part(2, *from_far)
    cut = half * ROWS
    by_before = shifted(for_after, -1)
    by_after = shifted(for_before, 1)
    by_far = (shifted(for_far[:, :cut], -2), shifted(for_far[:, cut:], 2))

    gathered = pl.pallas_call(
        functools.partial(class_kernel, members=members),
        out_shape=jax.ShapeDtypeStruct((members, WIRE, ROWS), bf16),
        in_specs=[in_vmem()] * 5,
        out_specs=in_vmem(),
        compiler_params=params(),
        name="class_sum",
    )(own, by_before, by_after, *by_far)
    arrived = lax.all_to_all(gathered, "seq", 0, 0, tiled=True, axis_index_groups=groups)
    attended = pl.pallas_call(
        final_kernel,
        out_shape=jax.ShapeDtypeStruct((1, ROWS, HD), bf16),
        in_specs=[in_vmem()] * 2,
        out_specs=in_vmem(),
        compiler_params=params(),
        name="attended",
    )(suffix, arrived)

    same = lax.all_gather(attended, "seq", axis=0, tiled=True, axis_index_groups=groups)
    pieces = [
        (same, (0, 0)),
        (shifted(same, 1), (1, 0)),
        (shifted(same, -1), (3, 0)),
        (shifted(same[:half], 2), (2, 0)),
        (shifted(same[half:], -2), (2, half)),
    ]
    partial_value = pl.pallas_call(
        functools.partial(
            project_kernel, classes=classes, layout=tuple(where for _, where in pieces)
        ),
        out_shape=jax.ShapeDtypeStruct((size * QB, out_weight.shape[1]), bf16),
        in_specs=[in_smem()] + [in_vmem()] * (len(pieces) + 1),
        out_specs=in_vmem(),
        compiler_params=params(),
        name="projection",
    )(position, *[piece for piece, _ in pieces], out_weight)
    sent = lax.all_to_all(
        partial_value.reshape(heads, size * QB // heads, -1), "head", 0, 0, tiled=True
    )
    return jnp.sum(sent.astype(f32), axis=0)


def solution(mesh):
    in_specs = (
        P(("prompt", "seq"), None, "head"),
        P(("prompt", "seq"), "head"),
        P(("prompt", "seq"), "head"),
        P(("prompt", "seq"), None, "head"),
        P(("prompt", "seq"), None, "head"),
        P("prompt", None),
        P(("prompt", "seq")),
        P("head", "seq"),
    )
    out_specs = P(("prompt", "head"), "seq")
    return jax.shard_map(body, mesh=mesh, in_specs=in_specs, out_specs=out_specs, check_vma=False)
```

time: 414 us -> 174 us (0.42)
  the two profiles are of different devices: /device:TPU:32 before, /device:TPU:64 now
where the time goes in v1:
time: 174 us; the launch traced here: 173 us
  blocking collectives  65.2 us (37%)
  starting transfers between devices  47.2 us (27%)
  waiting for transfers between devices  31.9 us (18%)
  Pallas kernels  24.5 us (14%)
  local copies, waits for them, and re-layouts  2.67 us (2%)
    ppermute x12, starting transfers between devices, shifted(): lax.ppermute(x, 'seq', [((i + distance) % size, i) for i in range(size)])  41.5 us
    all_gather x1, blocking collectives, body(): lax.all_gather(queries, 'seq', axis=0, tiled=True, axis_index_groups=groups)  27.3 us
    all_gather x1, blocking collectives, body(): lax.all_gather(attended, 'seq', axis=0, tiled=True, axis_index_groups=gro...  20.8 us
    pallas_call x4, Pallas kernels, prefix_part(): pl.pallas_call(functools.partial(prefix_kernel, offset=offset, classes=cl...  17.6 us
    all_to_all x1, blocking collectives, body(): lax.all_to_all(partial_value.reshape(heads, size * QB // heads, -1), 'hea...  17.1 us
    all_to_all x1, waiting for transfers between devices, body(): lax.all_to_all(gathered, 'seq', 0, 0, tiled=True, axis_index_groups=groups)  16.7 us
    ppermute x12, waiting for transfers between devices, shifted(): lax.ppermute(x, 'seq', [((i + distance) % size, i) for i in range(size)])  15.2 us
    all_to_all x1, starting transfers between devices, body(): lax.all_to_all(gathered, 'seq', 0, 0, tiled=True, axis_index_groups=groups)  5.77 us
  transfers between devices with their start and end apart: 13, of which 5 were waited for; matrix products, arithmetic and copies ran while one was open for 0% of the time, Pallas kernels for 13%

profile of v1, /device:TPU:64, one launch (start us, length us, event | category | flops | bytes accessed | tf_op | source)
XLA Modules:
  0.0 173.2 jit_solution(12997566672739702497)
XLA Ops:
  0.0 0.0 copy-start
  0.0 27.3 %all_gather.6.refs_0_ = bf16[4,64,640]{2,1,0:T(8,128)(2,1)S(1)} all-gather(bf16[1,64,640]{2,1,0:T(8,128)(2,1)} %q_ref.1), channel_id=1, replica_groups={{0,32,64,96},{8,40,72,104},{16,48,80,112},{24,56,88,120},{1,33,65,97},{..., dimensions={0}, use_global_device_ids=true | all-gather | bytes 409600 | tf_op jit(solution)/shard_map/all_gather | solution.py:272
  27.3 1.9 %collective-permute-start.2 = (bf16[4,64,640]{2,1,0:T(8,128)(2,1)S(1)}, bf16[4,64,640]{2,1,0:T(8,128)(2,1)S(1)}, u32[]{:S(2)}, u32[]{:S(2)}) collective-permute-start(bf16[4,64,640]{2,1,0:T(8,128)(2,1)S(1)} %all_gather.6.refs_0_), channel_id=1, source_target_pairs={{120,0},{0,8},{8,16},{16,24},{24,32},{32,40},{40,48},{48,56},{56,6... | collective-permute-start | bytes 983048 | tf_op jit(solution)/shard_map/ppermute | solution.py:222
  29.2 3.9 %collective-permute-start = (bf16[4,64,640]{2,1,0:T(8,128)(2,1)S(1)}, bf16[4,64,640]{2,1,0:T(8,128)(2,1)S(1)}, u32[]{:S(2)}, u32[]{:S(2)}) collective-permute-start(bf16[4,64,640]{2,1,0:T(8,128)(2,1)S(1)} %all_gather.6.refs_0_), channel_id=1, source_target_pairs={{8,0},{16,8},{24,16},{32,24},{40,32},{48,40},{56,48},{64,56},{72,6... | collective-permute-start | bytes 983048 | tf_op jit(solution)/shard_map/ppermute | solution.py:222
  33.2 4.3 %collective-permute-start.5 = (bf16[2,64,640]{2,1,0:T(8,128)(2,1)S(1)}, bf16[2,64,640]{2,1,0:T(8,128)(2,1)S(1)}, u32[]{:S(2)}, u32[]{:S(2)}) collective-permute-start(bf16[2,64,640]{2,1,0:T(8,128)(2,1)S(1)} %get-tuple-element.9), channel_id=1, source_target_pairs={{112,0},{120,8},{0,16},{8,24},{16,32},{24,40},{32,48},{40,56},{48,... | collective-permute-start | bytes 491528 | tf_op jit(solution)/shard_map/ppermute | solution.py:222
  37.5 2.4 %collective-permute-start.4 = (bf16[2,64,640]{2,1,0:T(8,128)(2,1)S(1)}, bf16[2,64,640]{2,1,0:T(8,128)(2,1)S(1)}, u32[]{:S(2)}, u32[]{:S(2)}) collective-permute-start(bf16[2,64,640]{2,1,0:T(8,128)(2,1)S(1)} %get-tuple-element.10), channel_id=1, source_target_pairs={{16,0},{24,8},{32,16},{40,24},{48,32},{56,40},{64,48},{72,56},{80,... | collective-permute-start | bytes 491528 | tf_op jit(solution)/shard_map/ppermute | solution.py:222
  39.9 1.8 %kept_slots.1.slots_ref = s32[16,128]{1,0:T(8,128)} custom-call(s32[1]{0:T(128)} %bitcast.pos_ref, s32[16,64]{1,0:T(8,128)} %kept_ref.1), custom_call_target="tpu_custom_call" | custom-call | tf_op jit(solution)/shard_map/kept_slots/pallas_call | solution.py:244
  41.7 1.0 collective-permute-done.5.refs_1_
  42.8 5.5 %collective-permute-done.4.refs_0_ = bf16[2,64,640]{2,1,0:T(8,128)(2,1)S(1)} collective-permute-done((bf16[2,64,640]{2,1,0:T(8,128)(2,1)S(1)}, bf16[2,64,640]{2,1,0:T(8,128)(2,1)S(1)}, u32[]{:S(2)}, u32[]{:S(2)}) %collective-permute-start.4) | collective-permute-done | bytes 163872 | tf_op jit(solution)/shard_map/ppermute | solution.py:222
  48.3 0.0 copy-done
  48.3 0.0 copy-start.1
  48.3 1.2 copy-done.1
  49.5 0.0 copy-start.6
  49.5 0.7 copy-done.6
  50.2 3.8 %prefix_part.7 = bf16[144,1280]{1,0:T(8,128)(2,1)S(1)} custom-call(s32[1]{0:T(128)} %bitcast.pos_ref, s32[16,128]{1,0:T(8,128)S(1)} %copy-done.6, bf16[2,64,640]{2,1,0:T(8,128)(2,1)S(1)} %collective-permute-done.4.refs_0_, bf16[2,64,640]{2,1,0:T(8,128)(2,1)S(1)} %collective-permute-done.5.refs_1_, bf16[4096,128]{1,0:T(8,128)(2,1)S(1)} %copy-done, ...), custom_call_target="tpu_custom_call" | custom-call | tf_op jit(solution)/shard_map/prefix_part/pallas_call | solution.py:254
  54.1 0.0 collective-permute-done.refs_0_
  54.1 5.0 %prefix_part.5 = bf16[144,1280]{1,0:T(8,128)(2,1)S(1)} custom-call(s32[1]{0:T(128)} %bitcast.pos_ref, s32[16,128]{1,0:T(8,128)S(1)} %copy-done.6, bf16[4,64,640]{2,1,0:T(8,128)(2,1)S(1)} %collective-permute-done.refs_0_, bf16[4096,128]{1,0:T(8,128)(2,1)S(1)} %copy-done, bf16[4096,128]{1,0:T(8,128)(2,1)S(1)} %copy-done.1), custom_call_target="tpu_custom_call" | custom-call | tf_op jit(solution)/shard_map/prefix_part/pallas_call | solution.py:254
  59.0 1.9 %collective-permute-start.1 = (bf16[144,1280]{1,0:T(8,128)(2,1)S(1)}, bf16[144,1280]{1,0:T(8,128)(2,1)S(1)}, u32[]{:S(2)}, u32[]{:S(2)}) collective-permute-start(bf16[144,1280]{1,0:T(8,128)(2,1)S(1)} %prefix_part.5), channel_id=1, source_target_pairs={{120,0},{0,8},{8,16},{16,24},{24,32},{32,40},{40,48},{48,56},{56,6... | collective-permute-start | bytes 1105928 | tf_op jit(solution)/shard_map/ppermute | solution.py:222
  61.0 0.0 collective-permute-done.2.refs_0_
  61.0 0.0 copy-start.2
  61.0 4.4 %prefix_part.6 = bf16[144,1280]{1,0:T(8,128)(2,1)S(1)} custom-call(s32[1]{0:T(128)} %bitcast.pos_ref, s32[16,128]{1,0:T(8,128)S(1)} %copy-done.6, bf16[4,64,640]{2,1,0:T(8,128)(2,1)S(1)} %collective-permute-done.2.refs_0_, bf16[4096,128]{1,0:T(8,128)(2,1)S(1)} %copy-done, bf16[4096,128]{1,0:T(8,128)(2,1)S(1)} %copy-done.1), custom_call_target="tpu_custom_call" | custom-call | tf_op jit(solution)/shard_map/prefix_part/pallas_call | solution.py:254
  65.4 3.9 %collective-permute-start.3 = (bf16[144,1280]{1,0:T(8,128)(2,1)S(1)}, bf16[144,1280]{1,0:T(8,128)(2,1)S(1)}, u32[]{:S(2)}, u32[]{:S(2)}) collective-permute-start(bf16[144,1280]{1,0:T(8,128)(2,1)S(1)} %prefix_part.6), channel_id=1, source_target_pairs={{8,0},{16,8},{24,16},{32,24},{40,32},{48,40},{56,48},{64,56},{72,6... | collective-permute-start | bytes 1105928 | tf_op jit(solution)/shard_map/ppermute | solution.py:222
  69.4 2.5 %collective-permute-start.7 = (bf16[144,640]{1,0:T(8,128)(2,1)S(1)}, bf16[144,640]{1,0:T(8,128)(2,1)S(1)}, u32[]{:S(2)}, u32[]{:S(2)}) collective-permute-start(bf16[144,640]{1,0:T(8,128)(2,1)S(1)} %get-tuple-element.5), channel_id=1, source_target_pairs={{16,0},{24,8},{32,16},{40,24},{48,32},{56,40},{64,48},{72,56},{80,... | collective-permute-start | bytes 552968 | tf_op jit(solution)/shard_map/ppermute | solution.py:222
  71.9 5.5 %collective-permute-start.6 = (bf16[144,640]{1,0:T(8,128)(2,1)S(1)}, bf16[144,640]{1,0:T(8,128)(2,1)S(1)}, u32[]{:S(2)}, u32[]{:S(2)}) collective-permute-start(bf16[144,640]{1,0:T(8,128)(2,1)S(1)} %get-tuple-element.6), channel_id=1, source_target_pairs={{112,0},{120,8},{0,16},{8,24},{16,32},{24,40},{32,48},{40,56},{48,... | collective-permute-start | bytes 552968 | tf_op jit(solution)/shard_map/ppermute | solution.py:222
  77.3 0.0 copy-done.2
  77.3 4.4 %prefix_part.4.own_ref = bf16[144,1280]{1,0:T(8,128)(2,1)S(1)} custom-call(s32[1]{0:T(128)} %bitcast.pos_ref, s32[16,128]{1,0:T(8,128)S(1)} %copy-done.6, bf16[4,64,640]{2,1,0:T(8,128)(2,1)S(1)} %all_gather.6.refs_0_, bf16[4096,128]{1,0:T(8,128)(2,1)S(1)} %copy-done, bf16[4096,128]{1,0:T(8,128)(2,1)S(1)} %copy-done.2), custom_call_target="tpu_custom_call" | custom-call | tf_op jit(solution)/shard_map/prefix_part/pallas_call | solution.py:254
  81.8 0.0 copy-start.3
  81.8 0.0 copy-start.4
  81.8 0.0 copy-start.5
  81.8 0.0 collective-permute-done.7.second_ref
  81.8 0.0 collective-permute-done.6.first_ref
  81.8 0.0 collective-permute-done.1.before_ref
  81.8 0.0 collective-permute-done.3.after_ref
  81.8 1.4 class_sum.1
  83.2 5.8 %all-to-all-start = ((bf16[4,144,320]{2,1,0:T(8,128)(2,1)}), bf16[4,144,320]{2,1,0:T(8,128)(2,1)S(1)}, u32[]{:S(2)}, u32[]{:S(2)}) async-start(bf16[4,144,320]{2,1,0:T(8,128)(2,1)} %class_sum.1), calls=%async_computation | async-start | bytes 884736 | tf_op jit(solution)/shard_map/all_to_all | solution.py:294
  89.6 0.0 copy-done.3
  89.6 0.0 copy-done.4
  89.6 0.0 copy-done.5
  89.6 2.6 %suffix_part.1.suffix_ref = f32[136,320]{1,0:T(8,128)S(1)} custom-call(s32[1]{0:T(128)S(6)} %copy.15.length_ref, bf16[1,64,640]{2,1,0:T(8,128)(2,1)S(1)} %copy-done.5, bf16[1,2048,128]{2,1,0:T(8,128)(2,1)S(1)} %copy-done.3, bf16[1,2048,128]{2,1,0:T(8,128)(2,1)S(1)} %copy-done.4), custom_call_target="tpu_custom_call" | custom-call | tf_op jit(solution)/shard_map/suffix_part/pallas_call | solution.py:263
  92.3 0.0 copy-start.7
  92.3 16.7 %all-to-all-done.parts_ref = bf16[4,144,320]{2,1,0:T(8,128)(2,1)S(1)} async-done(((bf16[4,144,320]{2,1,0:T(8,128)(2,1)}), bf16[4,144,320]{2,1,0:T(8,128)(2,1)S(1)}, u32[]{:S(2)}, u32[]{:S(2)}) %all-to-all-start) | async-done | bytes 368672 | tf_op jit(solution)/shard_map/all_to_all | solution.py:294
  109.0 0.2 attended.1
  109.2 20.8 %all_gather.7.refs_0_ = bf16[4,320,128]{2,1,0:T(8,128)(2,1)S(1)} all-gather(bf16[1,320,128]{2,1,0:T(8,128)(2,1)S(1)} %attended.1), channel_id=1, replica_groups={{0,32,64,96},{8,40,72,104},{16,48,80,112},{24,56,88,120},{1,33,65,97},{..., dimensions={0}, use_global_device_ids=true | all-gather | bytes 409600 | tf_op jit(solution)/shard_map/all_gather | solution.py:304
  130.0 6.5 %collective-permute-start.9 = (bf16[4,320,128]{2,1,0:T(8,128)(2,1)S(1)}, bf16[4,320,128]{2,1,0:T(8,128)(2,1)S(1)}, u32[]{:S(2)}, u32[]{:S(2)}) collective-permute-start(bf16[4,320,128]{2,1,0:T(8,128)(2,1)S(1)} %all_gather.7.refs_0_), channel_id=1, source_target_pairs={{120,0},{0,8},{8,16},{16,24},{24,32},{32,40},{40,48},{48,56},{56,6... | collective-permute-start | bytes 983048 | tf_op jit(solution)/shard_map/ppermute | solution.py:222
  136.4 1.9 %collective-permute-start.8 = (bf16[4,320,128]{2,1,0:T(8,128)(2,1)S(1)}, bf16[4,320,128]{2,1,0:T(8,128)(2,1)S(1)}, u32[]{:S(2)}, u32[]{:S(2)}) collective-permute-start(bf16[4,320,128]{2,1,0:T(8,128)(2,1)S(1)} %all_gather.7.refs_0_), channel_id=1, source_target_pairs={{8,0},{16,8},{24,16},{32,24},{40,32},{48,40},{56,48},{64,56},{72,6... | collective-permute-start | bytes 983048 | tf_op jit(solution)/shard_map/ppermute | solution.py:222
  138.4 4.6 %collective-permute-start.11 = (bf16[2,320,128]{2,1,0:T(8,128)(2,1)S(1)}, bf16[2,320,128]{2,1,0:T(8,128)(2,1)S(1)}, u32[]{:S(2)}, u32[]{:S(2)}) collective-permute-start(bf16[2,320,128]{2,1,0:T(8,128)(2,1)S(1)} %get-tuple-element.7), channel_id=1, source_target_pairs={{112,0},{120,8},{0,16},{8,24},{16,32},{24,40},{32,48},{40,56},{48,... | collective-permute-start | bytes 491528 | tf_op jit(solution)/shard_map/ppermute | solution.py:222
  143.0 2.2 %collective-permute-start.10 = (bf16[2,320,128]{2,1,0:T(8,128)(2,1)S(1)}, bf16[2,320,128]{2,1,0:T(8,128)(2,1)S(1)}, u32[]{:S(2)}, u32[]{:S(2)}) collective-permute-start(bf16[2,320,128]{2,1,0:T(8,128)(2,1)S(1)} %get-tuple-element.8), channel_id=1, source_target_pairs={{16,0},{24,8},{32,16},{40,24},{48,32},{56,40},{64,48},{72,56},{80,... | collective-permute-start | bytes 491528 | tf_op jit(solution)/shard_map/ppermute | solution.py:222
  145.2 0.0 copy-done.7
  145.2 0.3 copy.10.refs_5_
  145.4 2.2 %collective-permute-done.11.refs_4_ = bf16[2,320,128]{2,1,0:T(8,128)(2,1)S(1)} collective-permute-done((bf16[2,320,128]{2,1,0:T(8,128)(2,1)S(1)}, bf16[2,320,128]{2,1,0:T(8,128)(2,1)S(1)}, u32[]{:S(2)}, u32[]{:S(2)}) %collective-permute-start.11) | collective-permute-done | bytes 163872 | tf_op jit(solution)/shard_map/ppermute | solution.py:222
  147.6 6.5 %collective-permute-done.10.refs_3_ = bf16[2,320,128]{2,1,0:T(8,128)(2,1)S(1)} collective-permute-done((bf16[2,320,128]{2,1,0:T(8,128)(2,1)S(1)}, bf16[2,320,128]{2,1,0:T(8,128)(2,1)S(1)}, u32[]{:S(2)}, u32[]{:S(2)}) %collective-permute-start.10) | collective-permute-done | bytes 163872 | tf_op jit(solution)/shard_map/ppermute | solution.py:222
  154.1 0.0 collective-permute-done.9.refs_2_
  154.1 0.0 collective-permute-done.8.refs_1_
  154.1 0.9 projection.1
  155.0 0.4 copy.11
  155.3 17.1 %all_to_all.10 = bf16[8,128,320]{1,2,0:T(8,128)(2,1)S(1)} all-to-all(bf16[8,128,320]{1,2,0:T(8,128)(2,1)S(1)} %copy.11), channel_id=1, replica_groups=mesh['prompt'=4,'seq'=16,'head'=8] {'head'}, dimensions={0} | all-to-all | bytes 1310720 | tf_op jit(solution)/shard_map/all_to_all | solution.py:322
  172.5 0.8 convert_reduce_fusion
  (3 shorter events, 0.1 us)
Async XLA Ops:
  0.0 48.3 %copy-start = (bf16[4096,128]{1,0:T(8,128)(2,1)S(1)}, bf16[4096,128]{1,0:T(8,128)(2,1)}, u32[]{:S(2)}) copy-start(bf16[4096,128]{1,0:T(8,128)(2,1)} %refs_2_.7) | copy-start | bytes 3145732
  27.3 33.7 %collective-permute-start.2 = (bf16[4,64,640]{2,1,0:T(8,128)(2,1)S(1)}, bf16[4,64,640]{2,1,0:T(8,128)(2,1)S(1)}, u32[]{:S(2)}, u32[]{:S(2)}) collective-permute-start(bf16[4,64,640]{2,1,0:T(8,128)(2,1)S(1)} %all_gather.6.refs_0_), channel_id=1, source_target_pairs={{120,0},{0,8},{8,16},{16,24},{24,32},{32,40},{40,48},{48,56},{56,6... | collective-permute-start | bytes 983048 | tf_op jit(solution)/shard_map/ppermute | solution.py:222
  29.2 24.9 %collective-permute-start = (bf16[4,64,640]{2,1,0:T(8,128)(2,1)S(1)}, bf16[4,64,640]{2,1,0:T(8,128)(2,1)S(1)}, u32[]{:S(2)}, u32[]{:S(2)}) collective-permute-start(bf16[4,64,640]{2,1,0:T(8,128)(2,1)S(1)} %all_gather.6.refs_0_), channel_id=1, source_target_pairs={{8,0},{16,8},{24,16},{32,24},{40,32},{48,40},{56,48},{64,56},{72,6... | collective-permute-start | bytes 983048 | tf_op jit(solution)/shard_map/ppermute | solution.py:222
  33.2 9.6 %collective-permute-start.5 = (bf16[2,64,640]{2,1,0:T(8,128)(2,1)S(1)}, bf16[2,64,640]{2,1,0:T(8,128)(2,1)S(1)}, u32[]{:S(2)}, u32[]{:S(2)}) collective-permute-start(bf16[2,64,640]{2,1,0:T(8,128)(2,1)S(1)} %get-tuple-element.9), channel_id=1, source_target_pairs={{112,0},{120,8},{0,16},{8,24},{16,32},{24,40},{32,48},{40,56},{48,... | collective-permute-start | bytes 491528 | tf_op jit(solution)/shard_map/ppermute | solution.py:222
  37.5 10.8 %collective-permute-start.4 = (bf16[2,64,640]{2,1,0:T(8,128)(2,1)S(1)}, bf16[2,64,640]{2,1,0:T(8,128)(2,1)S(1)}, u32[]{:S(2)}, u32[]{:S(2)}) collective-permute-start(bf16[2,64,640]{2,1,0:T(8,128)(2,1)S(1)} %get-tuple-element.10), channel_id=1, source_target_pairs={{16,0},{24,8},{32,16},{40,24},{48,32},{56,40},{64,48},{72,56},{80,... | collective-permute-start | bytes 491528 | tf_op jit(solution)/shard_map/ppermute | solution.py:222
  48.3 1.2 copy-start.1
  49.5 0.7 copy-start.6
  59.0 22.8 %collective-permute-start.1 = (bf16[144,1280]{1,0:T(8,128)(2,1)S(1)}, bf16[144,1280]{1,0:T(8,128)(2,1)S(1)}, u32[]{:S(2)}, u32[]{:S(2)}) collective-permute-start(bf16[144,1280]{1,0:T(8,128)(2,1)S(1)} %prefix_part.5), channel_id=1, source_target_pairs={{120,0},{0,8},{8,16},{16,24},{24,32},{32,40},{40,48},{48,56},{56,6... | collective-permute-start | bytes 1105928 | tf_op jit(solution)/shard_map/ppermute | solution.py:222
  61.0 16.4 %copy-start.2 = (bf16[4096,128]{1,0:T(8,128)(2,1)S(1)}, bf16[4096,128]{1,0:T(8,128)(2,1)}, u32[]{:S(2)}) copy-start(bf16[4096,128]{1,0:T(8,128)(2,1)} %refs_3_.1) | copy-start | bytes 3145732
  65.4 16.4 %collective-permute-start.3 = (bf16[144,1280]{1,0:T(8,128)(2,1)S(1)}, bf16[144,1280]{1,0:T(8,128)(2,1)S(1)}, u32[]{:S(2)}, u32[]{:S(2)}) collective-permute-start(bf16[144,1280]{1,0:T(8,128)(2,1)S(1)} %prefix_part.6), channel_id=1, source_target_pairs={{8,0},{16,8},{24,16},{32,24},{40,32},{48,40},{56,48},{64,56},{72,6... | collective-permute-start | bytes 1105928 | tf_op jit(solution)/shard_map/ppermute | solution.py:222
  69.4 12.4 %collective-permute-start.7 = (bf16[144,640]{1,0:T(8,128)(2,1)S(1)}, bf16[144,640]{1,0:T(8,128)(2,1)S(1)}, u32[]{:S(2)}, u32[]{:S(2)}) collective-permute-start(bf16[144,640]{1,0:T(8,128)(2,1)S(1)} %get-tuple-element.5), channel_id=1, source_target_pairs={{16,0},{24,8},{32,16},{40,24},{48,32},{56,40},{64,48},{72,56},{80,... | collective-permute-start | bytes 552968 | tf_op jit(solution)/shard_map/ppermute | solution.py:222
  71.9 9.9 %collective-permute-start.6 = (bf16[144,640]{1,0:T(8,128)(2,1)S(1)}, bf16[144,640]{1,0:T(8,128)(2,1)S(1)}, u32[]{:S(2)}, u32[]{:S(2)}) collective-permute-start(bf16[144,640]{1,0:T(8,128)(2,1)S(1)} %get-tuple-element.6), channel_id=1, source_target_pairs={{112,0},{120,8},{0,16},{8,24},{16,32},{24,40},{32,48},{40,56},{48,... | collective-permute-start | bytes 552968 | tf_op jit(solution)/shard_map/ppermute | solution.py:222
  81.8 7.9 %copy-start.3 = (bf16[1,2048,128]{2,1,0:T(8,128)(2,1)S(1)}, bf16[1,2048,128]{2,1,0:T(8,128)(2,1)}, u32[]{:S(2)}) copy-start(bf16[1,2048,128]{2,1,0:T(8,128)(2,1)} %k_ref.1) | copy-start | bytes 1572868
  81.8 7.9 %copy-start.4 = (bf16[1,2048,128]{2,1,0:T(8,128)(2,1)S(1)}, bf16[1,2048,128]{2,1,0:T(8,128)(2,1)}, u32[]{:S(2)}) copy-start(bf16[1,2048,128]{2,1,0:T(8,128)(2,1)} %v_ref.1) | copy-start | bytes 1572868
  81.8 7.9 %copy-start.5 = (bf16[1,64,640]{2,1,0:T(8,128)(2,1)S(1)}, bf16[1,64,640]{2,1,0:T(8,128)(2,1)}, u32[]{:S(2)}) copy-start(bf16[1,64,640]{2,1,0:T(8,128)(2,1)} %q_ref.1) | copy-start | bytes 245764
  83.2 25.8 %all-to-all-start = ((bf16[4,144,320]{2,1,0:T(8,128)(2,1)}), bf16[4,144,320]{2,1,0:T(8,128)(2,1)S(1)}, u32[]{:S(2)}, u32[]{:S(2)}) async-start(bf16[4,144,320]{2,1,0:T(8,128)(2,1)} %class_sum.1), calls=%async_computation | async-start | bytes 884736 | tf_op jit(solution)/shard_map/all_to_all | solution.py:294
  92.3 52.9 %copy-start.7 = (bf16[640,320]{0,1:T(8,128)(2,1)S(1)}, bf16[640,320]{0,1:T(8,128)(2,1)}, u32[]{:S(2)}) copy-start(bf16[640,320]{0,1:T(8,128)(2,1)} %param.15) | copy-start | bytes 1228804
  130.0 24.1 %collective-permute-start.9 = (bf16[4,320,128]{2,1,0:T(8,128)(2,1)S(1)}, bf16[4,320,128]{2,1,0:T(8,128)(2,1)S(1)}, u32[]{:S(2)}, u32[]{:S(2)}) collective-permute-start(bf16[4,320,128]{2,1,0:T(8,128)(2,1)S(1)} %all_gather.7.refs_0_), channel_id=1, source_target_pairs={{120,0},{0,8},{8,16},{16,24},{24,32},{32,40},{40,48},{48,56},{56,6... | collective-permute-start | bytes 983048 | tf_op jit(solution)/shard_map/ppermute | solution.py:222
  136.4 17.6 %collective-permute-start.8 = (bf16[4,320,128]{2,1,0:T(8,128)(2,1)S(1)}, bf16[4,320,128]{2,1,0:T(8,128)(2,1)S(1)}, u32[]{:S(2)}, u32[]{:S(2)}) collective-permute-start(bf16[4,320,128]{2,1,0:T(8,128)(2,1)S(1)} %all_gather.7.refs_0_), channel_id=1, source_target_pairs={{8,0},{16,8},{24,16},{32,24},{40,32},{48,40},{56,48},{64,56},{72,6... | collective-permute-start | bytes 983048 | tf_op jit(solution)/shard_map/ppermute | solution.py:222
  138.4 9.2 %collective-permute-start.11 = (bf16[2,320,128]{2,1,0:T(8,128)(2,1)S(1)}, bf16[2,320,128]{2,1,0:T(8,128)(2,1)S(1)}, u32[]{:S(2)}, u32[]{:S(2)}) collective-permute-start(bf16[2,320,128]{2,1,0:T(8,128)(2,1)S(1)} %get-tuple-element.7), channel_id=1, source_target_pairs={{112,0},{120,8},{0,16},{8,24},{16,32},{24,40},{32,48},{40,56},{48,... | collective-permute-start | bytes 491528 | tf_op jit(solution)/shard_map/ppermute | solution.py:222
  143.0 11.1 %collective-permute-start.10 = (bf16[2,320,128]{2,1,0:T(8,128)(2,1)S(1)}, bf16[2,320,128]{2,1,0:T(8,128)(2,1)S(1)}, u32[]{:S(2)}, u32[]{:S(2)}) collective-permute-start(bf16[2,320,128]{2,1,0:T(8,128)(2,1)S(1)} %get-tuple-element.8), channel_id=1, source_target_pairs={{16,0},{24,8},{32,16},{40,24},{48,32},{56,40},{64,48},{72,56},{80,... | collective-permute-start | bytes 491528 | tf_op jit(solution)/shard_map/ppermute | solution.py:222

commit v2 on v1

v2 whole, which is shorter than its diff:
```python
import functools
import math

import jax
import jax.numpy as jnp
from jax import lax
from jax.experimental import pallas as pl
from jax.experimental.pallas import tpu as pltpu
from jax.sharding import PartitionSpec as P

HD = 128
GQA = 5
QB = 64
BLOCK = 128
MOST = 8
ROWS = GQA * QB
TILE = 128
TOKEN_RUNS = 8
WIDE = 384
FLOOR = -1e30
HIDDEN = -2e30
SCALE2 = math.log2(math.e) / math.sqrt(HD)
WIRE = ROWS + 16
VMEM_LIMIT = 24 * 2**20


def in_vmem():
    return pl.BlockSpec(memory_space=pltpu.VMEM)


def in_smem():
    return pl.BlockSpec(memory_space=pltpu.SMEM)


def params():
    return pltpu.CompilerParams(vmem_limit_bytes=VMEM_LIMIT)


def slots_kernel(pos_ref, kept_ref, out_ref, *, blocks_here):
    rel = kept_ref[...] - pos_ref[0] * blocks_here
    samples, keep = rel.shape
    lane = lax.broadcasted_iota(jnp.int32, (samples, 128), 1)
    present = jnp.zeros((samples, 128), jnp.int32)
    for i in range(keep):
        present = jnp.where(rel[:, i : i + 1] == lane, 1, present)
    present = jnp.where(lane < blocks_here, present, 0)
    earlier = lax.broadcasted_iota(jnp.int32, (128, 128), 0) < lax.broadcasted_iota(
        jnp.int32, (128, 128), 1
    )
    rank = jnp.dot(
        present.astype(jnp.float32).astype(jnp.bfloat16),
        earlier.astype(jnp.float32).astype(jnp.bfloat16),
        preferred_element_type=jnp.float32,
    ).astype(jnp.int32)
    out = jnp.where(lane == MOST, jnp.sum(present, axis=1, keepdims=True), 0)
    for k in range(MOST):
        chosen = jnp.sum(
            jnp.where((present > 0) & (rank == k), lane, 0), axis=1, keepdims=True
        )
        out = jnp.where(lane == k, chosen, out)
    out_ref[...] = out


def query_rows(q):
    return jnp.concatenate([q[:, j * HD : (j + 1) * HD] for j in range(GQA)], axis=0)


def across(asking, keys):
    return (
        lax.dot_general(
            asking, keys, (((1,), (1,)), ((), ())), preferred_element_type=jnp.float32
        )
        * SCALE2
    )


def weighted(prob, values):
    ones = jnp.ones((values.shape[0], HD), jnp.bfloat16)
    return jnp.dot(
        prob, jnp.concatenate([values, ones], axis=1), preferred_element_type=jnp.float32
    )


def laid_flat(stat):
    turned = jnp.concatenate([stat, jnp.zeros((WIDE - ROWS, TILE), jnp.float32)], axis=0).T

    def flat(i):
        row = turned[i : i + 1]
        return jnp.concatenate(
            [row[:, c * TILE : (c + 1) * TILE] for c in range(WIDE // TILE)], axis=0
        )

    return flat


def columns(flats):
    rows = [jnp.concatenate([f[c : c + 1] for c in range(WIDE // TILE)], axis=1) for f in flats]
    spare = -len(rows) % 8
    if spare:
        rows.append(jnp.zeros((spare, WIDE), jnp.float32))
    turned = jnp.concatenate(rows, axis=0).T
    return [turned[:ROWS, i : i + 1] for i in range(len(flats))]


def wire_rows(flat):
    high = flat.astype(jnp.bfloat16).astype(jnp.float32)
    middle = (flat - high).astype(jnp.bfloat16).astype(jnp.float32)
    low = flat - high - middle
    spare = jnp.zeros((WIRE - ROWS - 9, TILE), jnp.float32)
    return jnp.concatenate([high, middle, low, spare], axis=0).astype(jnp.bfloat16)


def unwire_rows(rows):
    rows = rows.astype(jnp.float32)
    return rows[0:3] + rows[3:6] + rows[6:9]


def shares_of(flats):
    top = functools.reduce(jnp.maximum, flats)
    shares = [jnp.exp2(f - top) for f in flats]
    total = functools.reduce(jnp.add, shares)
    return [share / total for share in shares], top + jnp.log2(total)


def added(parts, shares):
    return functools.reduce(
        jnp.add, [p.astype(jnp.float32) * c for p, c in zip(parts, shares, strict=True)]
    )


def prefix_kernel(pos_ref, slots_ref, *refs, offset, classes, ranges):
    n = len(ranges)
    q_refs, k_ref, v_ref, out_refs, stat_ref = refs[:n], refs[n], refs[n + 1], refs[n + 2 : -1], refs[-1]
    group = lax.rem(pos_ref[0] + offset, classes)
    lane = lax.broadcasted_iota(jnp.int32, (ROWS, TILE), 1)
    first = 0
    for q_ref, out_ref, many in zip(q_refs, out_refs, ranges, strict=True):

        def one(i, _, q_ref=q_ref, out_ref=out_ref, first=first):
            sample = group + classes * (first + i)
            count = slots_ref[sample, MOST]

            @pl.when(count == 0)
            def _():
                out_ref[i, :ROWS, :] = jnp.zeros((ROWS, HD), jnp.bfloat16)
                stat_ref[...] = jnp.where(lane == first + i, FLOOR, stat_ref[...])

            for most in range(2, MOST + 1, 2):

                @pl.when((count == most - 1) | (count == most))
                def _(most=most):
                    places = [
                        pl.ds(pl.multiple_of(slots_ref[sample, j] * BLOCK, BLOCK), BLOCK)
                        for j in range(most)
                    ]
                    asking = query_rows(q_ref[i])
                    bias = jnp.where(count == most, 0.0, HIDDEN).astype(jnp.float32)
                    scores = [across(asking, k_ref[place, :]) for place in places]
                    scores[-1] = scores[-1] + bias
                    top = jnp.max(
                        functools.reduce(jnp.maximum, scores), axis=1, keepdims=True
                    )
                    prob = jnp.concatenate(
                        [jnp.exp2(x - top).astype(jnp.bfloat16) for x in scores], axis=1
                    )
                    values = jnp.concatenate([v_ref[place, :] for place in places], axis=0)
                    both = weighted(prob, values)
                    total = both[:, HD:]
                    out_ref[i, :ROWS, :] = (both[:, :HD] / total).astype(jnp.bfloat16)
                    stat_ref[...] = jnp.where(
                        lane == first + i, top + jnp.log2(total), stat_ref[...]
                    )

            return 0

        lax.fori_loop(0, many, one, 0)
        first += many
    flat = laid_flat(stat_ref[...])
    first = 0
    for out_ref, many in zip(out_refs, ranges, strict=True):
        for i in range(many):
            out_ref[i, ROWS:, :] = wire_rows(flat(first + i))
        first += many


def suffix_kernel(length_ref, q_ref, k_ref, v_ref, out_ref):
    chunk = 4 * BLOCK
    asking = query_rows(q_ref[0])
    length = length_ref[0]
    token = lax.rem(lax.broadcasted_iota(jnp.int32, (ROWS, chunk), 0), QB)
    slot = lax.broadcasted_iota(jnp.int32, (ROWS, chunk), 1)

    def step(n, carry):
        top, both = carry
        rows = pl.ds(pl.multiple_of(n * chunk, chunk), chunk)
        scores = across(asking, k_ref[0, rows, :])
        scores = jnp.where(slot - token <= length - QB - n * chunk, scores, HIDDEN)
        new_top = jnp.maximum(top, jnp.max(scores, axis=1, keepdims=True))
        prob = jnp.exp2(scores - new_top).astype(jnp.bfloat16)
        both = both * jnp.exp2(top - new_top) + weighted(prob, v_ref[0, rows, :])
        return new_top, both

    start = (jnp.full((ROWS, 1), FLOOR, jnp.float32), jnp.zeros((ROWS, 2 * HD), jnp.float32))
    top, both = lax.fori_loop(0, lax.div(length + chunk - 1, chunk), step, start)
    total = both[:, HD:]
    out_ref[:ROWS, :] = both[:, :HD] / total
    flat = laid_flat(top + jnp.log2(total))(0)
    out_ref[ROWS:, :] = jnp.concatenate([flat, jnp.zeros((5, TILE), jnp.float32)], axis=0)


def class_kernel(own_ref, before_ref, after_ref, first_ref, second_ref, out_ref, *, members):
    half = first_ref.shape[0]
    parts, shares = [], []
    for k in range(members):
        far_ref, at = (first_ref, k) if k < half else (second_ref, k - half)
        here = [own_ref.at[k], before_ref.at[k], after_ref.at[k], far_ref.at[at]]
        share, log_sum = shares_of([unwire_rows(ref[ROWS:, :]) for ref in here])
        out_ref[k, ROWS:, :] = wire_rows(log_sum)
        parts.append(here)
        shares += share
    shares = columns(shares)
    for k, here in enumerate(parts):
        out_ref[k, :ROWS, :] = added(
            [ref[:ROWS, :] for ref in here], shares[k * len(here) : (k + 1) * len(here)]
        ).astype(jnp.bfloat16)


def final_kernel(suffix_ref, parts_ref, out_ref):
    members = parts_ref.shape[0]
    flats = [suffix_ref[ROWS : ROWS + 3, :]]
    flats += [unwire_rows(parts_ref[i, ROWS:, :]) for i in range(members)]
    shares = columns(shares_of(flats)[0])
    parts = [suffix_ref[:ROWS, :]] + [parts_ref[i, :ROWS, :] for i in range(members)]
    out_ref[0] = added(parts, shares).astype(jnp.bfloat16)


def project_kernel(pos_ref, *refs, classes, layout):
    n = len(layout)
    in_refs, w_ref, out_ref, rows_ref = refs[:n], refs[n], refs[n + 1], refs[n + 2]
    for ref, (offset, first) in zip(in_refs, layout, strict=True):
        group = lax.rem(pos_ref[0] + offset, classes)
        for i in range(ref.shape[0]):
            rows = ref[i]
            sample = group + classes * (first + i)
            rows_ref[pl.ds(pl.multiple_of(sample * QB, QB), QB), :] = jnp.concatenate(
                [rows[j * QB : (j + 1) * QB] for j in range(GQA)], axis=1
            )
    weight = w_ref[...]
    tokens = rows_ref.shape[0] // out_ref.shape[0]
    for i in range(out_ref.shape[0]):
        out_ref[i] = lax.dot_general(
            weight,
            rows_ref[i * tokens : (i + 1) * tokens, :],
            (((1,), (1,)), ((), ())),
            preferred_element_type=jnp.float32,
        ).astype(jnp.bfloat16)


def sum_kernel(parts_ref, out_ref):
    out_ref[...] = functools.reduce(
        jnp.add, [parts_ref[i].astype(jnp.float32) for i in range(parts_ref.shape[0])]
    )


def shifted(x, distance):
    size = lax.axis_size("seq")
    return lax.ppermute(x, "seq", [((i + distance) % size, i) for i in range(size)])


def head_exchange(x):
    return lax.all_to_all(x, "head", 0, 0, tiled=True)


def summed(parts):
    return pl.pallas_call(
        sum_kernel,
        out_shape=jax.ShapeDtypeStruct(parts.shape[1:], jnp.float32),
        in_specs=[in_vmem()],
        out_specs=in_vmem(),
        compiler_params=params(),
        name="head_sum",
    )(parts).T


def body(
    queries,
    prefix_keys,
    prefix_values,
    suffix_keys,
    suffix_values,
    kept_blocks,
    suffix_lengths,
    out_weight,
):
    size = lax.axis_size("seq")
    classes = 4
    members = size // classes
    half = members // 2
    groups = [[g + classes * i for i in range(members)] for g in range(classes)]
    position = lax.axis_index("seq").astype(jnp.int32).reshape(1)
    blocks_here = prefix_keys.shape[0] // BLOCK
    bf16, f32 = jnp.bfloat16, jnp.float32

    slots = pl.pallas_call(
        functools.partial(slots_kernel, blocks_here=blocks_here),
        out_shape=jax.ShapeDtypeStruct((kept_blocks.shape[0], 128), jnp.int32),
        in_specs=[in_smem(), in_vmem()],
        out_specs=in_vmem(),
        name="kept_slots",
    )(position, kept_blocks)

    def prefix_part(offset, *asked):
        ranges = tuple(a.shape[0] for a in asked)
        work = sum(ranges) * ROWS * MOST * BLOCK
        return pl.pallas_call(
            functools.partial(prefix_kernel, offset=offset, classes=classes, ranges=ranges),
            out_shape=[jax.ShapeDtypeStruct((many, WIRE, HD), bf16) for many in ranges],
            in_specs=[in_smem(), in_smem()] + [in_vmem()] * (len(asked) + 2),
            out_specs=[in_vmem()] * len(asked),
            scratch_shapes=[pltpu.VMEM((ROWS, TILE), f32)],
            compiler_params=params(),
            cost_estimate=pl.CostEstimate(
                flops=work * HD * 4, bytes_accessed=2**21, transcendentals=work
            ),
            name="prefix_part",
        )(position, slots, *asked, prefix_keys, prefix_values)

    suffix = pl.pallas_call(
        suffix_kernel,
        out_shape=jax.ShapeDtypeStruct((ROWS + 8, HD), f32),
        in_specs=[in_smem()] + [in_vmem()] * 3,
        out_specs=in_vmem(),
        compiler_params=params(),
        name="suffix_part",
    )(suffix_lengths, queries, suffix_keys, suffix_values)

    def gathered_class(x):
        return lax.all_gather(x, "seq", axis=0, tiled=True, axis_index_groups=groups)

    mine = gathered_class(queries)
    from_after = shifted(mine, 1)
    from_before = shifted(mine, -1)
    from_far = (shifted(mine[:half], 2), shifted(mine[half:], -2))

    (own,) = prefix_part(0, mine)
    (for_after,) = prefix_part(1, from_after)
    (for_before,) = prefix_part(3, from_before)
    for_far = prefix_part(2, *from_far)
    by_before = shifted(for_after, -1)
    by_after = shifted(for_before, 1)
    by_far = (shifted(for_far[0], -2), shifted(for_far[1], 2))

    gathered = pl.pallas_call(
        functools.partial(class_kernel, members=members),
        out_shape=jax.ShapeDtypeStruct((members, WIRE, HD), bf16),
        in_specs=[in_vmem()] * 5,
        out_specs=in_vmem(),
        compiler_params=params(),
        name="class_sum",
    )(own, by_before, by_after, *by_far)
    arrived = lax.all_to_all(gathered, "seq", 0, 0, tiled=True, axis_index_groups=groups)
    attended = pl.pallas_call(
        final_kernel,
        out_shape=jax.ShapeDtypeStruct((1, ROWS, HD), bf16),
        in_specs=[in_vmem()] * 2,
        out_specs=in_vmem(),
        compiler_params=params(),
        name="attended",
    )(suffix, arrived)

    same = gathered_class(attended)
    pieces = [
        (same, (0, 0)),
        (shifted(same, 1), (1, 0)),
        (shifted(same, -1), (3, 0)),
        (shifted(same[:half], 2), (2, 0)),
        (shifted(same[half:], -2), (2, half)),
    ]
    tokens, heads = size * QB, TOKEN_RUNS
    partial_value = pl.pallas_call(
        functools.partial(
            project_kernel, classes=classes, layout=tuple(where for _, where in pieces)
        ),
        out_shape=jax.ShapeDtypeStruct((heads, out_weight.shape[1], tokens // heads), bf16),
        in_specs=[in_smem()] + [in_vmem()] * (len(pieces) + 1),
        out_specs=in_vmem(),
        scratch_shapes=[pltpu.VMEM((tokens, GQA * HD), bf16)],
        compiler_params=params(),
        name="projection",
    )(position, *[piece for piece, _ in pieces], out_weight.T)
    return summed(head_exchange(partial_value))


def solution(mesh):
    in_specs = (
        P(("prompt", "seq"), None, "head"),
        P(("prompt", "seq"), "head"),
        P(("prompt", "seq"), "head"),
        P(("prompt", "seq"), None, "head"),
        P(("prompt", "seq"), None, "head"),
        P("prompt", None),
        P(("prompt", "seq")),
        P("head", "seq"),
    )
    out_specs = P(("prompt", "head"), "seq")
    return jax.shard_map(body, mesh=mesh, in_specs=in_specs, out_specs=out_specs, check_vma=False)
```

time: 174 us -> 162 us (0.931)
  the two profiles are of different devices: /device:TPU:64 before, /device:TPU:8 now
where the time goes in v2:
time: 162 us; the launch traced here: 161 us
  blocking collectives  61.4 us (38%)
  starting transfers between devices  54.6 us (34%)
  waiting for transfers between devices  23.3 us (14%)
  Pallas kernels  19.2 us (12%)
  local copies, waits for them, and re-layouts  2 us (1%)
    all_gather x2, blocking collectives, gathered_class(): lax.all_gather(x, 'seq', axis=0, tiled=True, axis_index_groups=groups)  47.8 us
    ppermute x12, starting transfers between devices, shifted(): lax.ppermute(x, 'seq', [((i + distance) % size, i) for i in range(size)])  47.1 us
    all_to_all x1, blocking collectives, head_exchange(): return lax.all_to_all(x, 'head', 0, 0, tiled=True)  13.7 us
    all_to_all x1, waiting for transfers between devices, body(): lax.all_to_all(gathered, 'seq', 0, 0, tiled=True, axis_index_groups=groups)  13.6 us
    pallas_call x4, Pallas kernels, prefix_part(): pl.pallas_call(functools.partial(prefix_kernel, offset=offset, classes=cl...  12.4 us
    ppermute x12, waiting for transfers between devices, shifted(): lax.ppermute(x, 'seq', [((i + distance) % size, i) for i in range(size)])  9.7 us
    all_to_all x1, starting transfers between devices, body(): lax.all_to_all(gathered, 'seq', 0, 0, tiled=True, axis_index_groups=groups)  7.51 us
  transfers between devices with their start and end apart: 13, of which 5 were waited for; matrix products, arithmetic and copies ran while one was open for 0% of the time, Pallas kernels for 9%

profile of v2, /device:TPU:8, one launch (start us, length us, event | category | flops | bytes accessed | tf_op | source)
XLA Modules:
  0.0 161.4 jit_solution(15543598869547251344)
XLA Ops:
  0.0 0.0 copy-start
  0.0 27.9 %all_gather.6.refs_0_ = bf16[4,64,640]{2,1,0:T(8,128)(2,1)S(1)} all-gather(bf16[1,64,640]{2,1,0:T(8,128)(2,1)} %q_ref.1), channel_id=1, replica_groups={{0,32,64,96},{8,40,72,104},{16,48,80,112},{24,56,88,120},{1,33,65,97},{..., dimensions={0}, use_global_device_ids=true | all-gather | bytes 409600 | tf_op jit(solution)/shard_map/all_gather | solution.py:338
  27.9 3.8 %collective-permute-start = (bf16[4,64,640]{2,1,0:T(8,128)(2,1)S(1)}, bf16[4,64,640]{2,1,0:T(8,128)(2,1)S(1)}, u32[]{:S(2)}, u32[]{:S(2)}) collective-permute-start(bf16[4,64,640]{2,1,0:T(8,128)(2,1)S(1)} %all_gather.6.refs_0_), channel_id=1, source_target_pairs={{8,0},{16,8},{24,16},{32,24},{40,32},{48,40},{56,48},{64,56},{72,6... | collective-permute-start | bytes 983048 | tf_op jit(solution)/shard_map/ppermute | solution.py:267
  31.7 2.2 %collective-permute-start.2 = (bf16[4,64,640]{2,1,0:T(8,128)(2,1)S(1)}, bf16[4,64,640]{2,1,0:T(8,128)(2,1)S(1)}, u32[]{:S(2)}, u32[]{:S(2)}) collective-permute-start(bf16[4,64,640]{2,1,0:T(8,128)(2,1)S(1)} %all_gather.6.refs_0_), channel_id=1, source_target_pairs={{120,0},{0,8},{8,16},{16,24},{24,32},{32,40},{40,48},{48,56},{56,6... | collective-permute-start | bytes 983048 | tf_op jit(solution)/shard_map/ppermute | solution.py:267
  33.9 4.4 %collective-permute-start.5 = (bf16[2,64,640]{2,1,0:T(8,128)(2,1)S(1)}, bf16[2,64,640]{2,1,0:T(8,128)(2,1)S(1)}, u32[]{:S(2)}, u32[]{:S(2)}) collective-permute-start(bf16[2,64,640]{2,1,0:T(8,128)(2,1)S(1)} %get-tuple-element.11), channel_id=1, source_target_pairs={{112,0},{120,8},{0,16},{8,24},{16,32},{24,40},{32,48},{40,56},{48,... | collective-permute-start | bytes 491528 | tf_op jit(solution)/shard_map/ppermute | solution.py:267
  38.4 3.5 %collective-permute-start.4 = (bf16[2,64,640]{2,1,0:T(8,128)(2,1)S(1)}, bf16[2,64,640]{2,1,0:T(8,128)(2,1)S(1)}, u32[]{:S(2)}, u32[]{:S(2)}) collective-permute-start(bf16[2,64,640]{2,1,0:T(8,128)(2,1)S(1)} %get-tuple-element.12), channel_id=1, source_target_pairs={{16,0},{24,8},{32,16},{40,24},{48,32},{56,40},{64,48},{72,56},{80,... | collective-permute-start | bytes 491528 | tf_op jit(solution)/shard_map/ppermute | solution.py:267
  41.9 1.8 %kept_slots.1.slots_ref = s32[16,128]{1,0:T(8,128)} custom-call(s32[1]{0:T(128)} %bitcast.pos_ref, s32[16,64]{1,0:T(8,128)} %kept_ref.1), custom_call_target="tpu_custom_call" | custom-call | tf_op jit(solution)/shard_map/kept_slots/pallas_call | solution.py:304
  43.7 0.0 collective-permute-done.refs_0_
  43.7 0.0 copy-done
  43.7 0.0 copy-start.1
  43.7 1.2 copy-done.1
  45.0 0.0 copy-start.7
  45.0 0.7 copy-done.7
  45.6 2.6 %prefix_part.5 = bf16[4,336,128]{2,1,0:T(8,128)(2,1)S(1)} custom-call(s32[1]{0:T(128)} %bitcast.pos_ref, s32[16,128]{1,0:T(8,128)S(1)} %copy-done.7, bf16[4,64,640]{2,1,0:T(8,128)(2,1)S(1)} %collective-permute-done.refs_0_, bf16[4096,128]{1,0:T(8,128)(2,1)S(1)} %copy-done, bf16[4096,128]{1,0:T(8,128)(2,1)S(1)} %copy-done.1), custom_call_target="tpu_custom_call" | custom-call | flops 671088640 | bytes 2097152 | tf_op jit(solution)/shard_map/prefix_part/pallas_call | solution.py:315
  48.3 2.3 %collective-permute-start.1 = (bf16[4,336,128]{2,1,0:T(8,128)(2,1)S(1)}, bf16[4,336,128]{2,1,0:T(8,128)(2,1)S(1)}, u32[]{:S(2)}, u32[]{:S(2)}) collective-permute-start(bf16[4,336,128]{2,1,0:T(8,128)(2,1)S(1)} %prefix_part.5), channel_id=1, source_target_pairs={{120,0},{0,8},{8,16},{16,24},{24,32},{32,40},{40,48},{48,56},{56,6... | collective-permute-start | bytes 1032200 | tf_op jit(solution)/shard_map/ppermute | solution.py:267
  50.6 0.0 collective-permute-done.2.refs_0_
  50.6 3.4 %prefix_part.6 = bf16[4,336,128]{2,1,0:T(8,128)(2,1)S(1)} custom-call(s32[1]{0:T(128)} %bitcast.pos_ref, s32[16,128]{1,0:T(8,128)S(1)} %copy-done.7, bf16[4,64,640]{2,1,0:T(8,128)(2,1)S(1)} %collective-permute-done.2.refs_0_, bf16[4096,128]{1,0:T(8,128)(2,1)S(1)} %copy-done, bf16[4096,128]{1,0:T(8,128)(2,1)S(1)} %copy-done.1), custom_call_target="tpu_custom_call" | custom-call | flops 671088640 | bytes 2097152 | tf_op jit(solution)/shard_map/prefix_part/pallas_call | solution.py:315
  54.0 0.0 copy-start.2
  54.0 4.2 %collective-permute-start.3 = (bf16[4,336,128]{2,1,0:T(8,128)(2,1)S(1)}, bf16[4,336,128]{2,1,0:T(8,128)(2,1)S(1)}, u32[]{:S(2)}, u32[]{:S(2)}) collective-permute-start(bf16[4,336,128]{2,1,0:T(8,128)(2,1)S(1)} %prefix_part.6), channel_id=1, source_target_pairs={{8,0},{16,8},{24,16},{32,24},{40,32},{48,40},{56,48},{64,56},{72,6... | collective-permute-start | bytes 1032200 | tf_op jit(solution)/shard_map/ppermute | solution.py:267
  58.2 0.0 collective-permute-done.5.refs_1_
  58.2 0.0 collective-permute-done.4.refs_0_
  58.2 3.6 %prefix_part.7 = (bf16[2,336,128]{2,1,0:T(8,128)(2,1)S(1)}, bf16[2,336,128]{2,1,0:T(8,128)(2,1)S(1)}) custom-call(s32[1]{0:T(128)} %bitcast.pos_ref, s32[16,128]{1,0:T(8,128)S(1)} %copy-done.7, bf16[2,64,640]{2,1,0:T(8,128)(2,1)S(1)} %collective-permute-done.4.refs_0_, bf16[2,64,640]{2,1,0:T(8,128)(2,1)S(1)} %collective-permute-done.5.refs_1_, ...), custom_call_target="tpu_custom_call" | custom-call | flops 671088640 | bytes 2097152 | tf_op jit(solution)/shard_map/prefix_part/pallas_call | solution.py:315
  61.9 1.9 %collective-permute-start.6 = (bf16[2,336,128]{2,1,0:T(8,128)(2,1)S(1)}, bf16[2,336,128]{2,1,0:T(8,128)(2,1)S(1)}, u32[]{:S(2)}, u32[]{:S(2)}) collective-permute-start(bf16[2,336,128]{2,1,0:T(8,128)(2,1)S(1)} %get-tuple-element.7), channel_id=1, source_target_pairs={{112,0},{120,8},{0,16},{8,24},{16,32},{24,40},{32,48},{40,56},{48,... | collective-permute-start | bytes 516104 | tf_op jit(solution)/shard_map/ppermute | solution.py:267
  63.8 6.0 %collective-permute-start.7 = (bf16[2,336,128]{2,1,0:T(8,128)(2,1)S(1)}, bf16[2,336,128]{2,1,0:T(8,128)(2,1)S(1)}, u32[]{:S(2)}, u32[]{:S(2)}) collective-permute-start(bf16[2,336,128]{2,1,0:T(8,128)(2,1)S(1)} %get-tuple-element.8), channel_id=1, source_target_pairs={{16,0},{24,8},{32,16},{40,24},{48,32},{56,40},{64,48},{72,56},{80,... | collective-permute-start | bytes 516104 | tf_op jit(solution)/shard_map/ppermute | solution.py:267
  69.8 0.0 copy-done.2
  69.9 2.7 %prefix_part.4.own_ref = bf16[4,336,128]{2,1,0:T(8,128)(2,1)S(1)} custom-call(s32[1]{0:T(128)} %bitcast.pos_ref, s32[16,128]{1,0:T(8,128)S(1)} %copy-done.7, bf16[4,64,640]{2,1,0:T(8,128)(2,1)S(1)} %all_gather.6.refs_0_, bf16[4096,128]{1,0:T(8,128)(2,1)S(1)} %copy-done, bf16[4096,128]{1,0:T(8,128)(2,1)S(1)} %copy-done.2), custom_call_target="tpu_custom_call" | custom-call | flops 671088640 | bytes 2097152 | tf_op jit(solution)/shard_map/prefix_part/pallas_call | solution.py:315
  72.6 0.5 collective-permute-done.6.first_ref
  73.0 1.8 %collective-permute-done.7.second_ref = bf16[2,336,128]{2,1,0:T(8,128)(2,1)S(1)} collective-permute-done((bf16[2,336,128]{2,1,0:T(8,128)(2,1)S(1)}, bf16[2,336,128]{2,1,0:T(8,128)(2,1)S(1)}, u32[]{:S(2)}, u32[]{:S(2)}) %collective-permute-start.7) | collective-permute-done | bytes 172064 | tf_op jit(solution)/shard_map/ppermute | solution.py:267
  74.9 0.0 collective-permute-done.1.before_ref
  74.9 0.0 collective-permute-done.3.after_ref
  74.9 0.0 copy-start.4
  74.9 1.7 %class_sum.1 = bf16[4,336,128]{2,1,0:T(8,128)(2,1)} custom-call(bf16[4,336,128]{2,1,0:T(8,128)(2,1)S(1)} %prefix_part.4.own_ref, bf16[4,336,128]{2,1,0:T(8,128)(2,1)S(1)} %collective-permute-done.1.before_ref, bf16[4,336,128]{2,1,0:T(8,128)(2,1)S(1)} %collective-permute-done.3.after_ref, bf16[2,336,128]{2,1,0:T(8,128)(2,1)S(1)} %collective-permute-done.6.first_ref, ...), custom_call_target="tpu_custom_call" | custom-call | tf_op jit(solution)/shard_map/class_sum/pallas_call | solution.py:353
  76.6 0.0 copy-start.3
  76.6 0.0 copy-start.6
  76.6 7.5 %all-to-all-start = ((bf16[4,336,128]{2,1,0:T(8,128)(2,1)}), bf16[4,336,128]{2,1,0:T(8,128)(2,1)S(1)}, u32[]{:S(2)}, u32[]{:S(2)}) async-start(bf16[4,336,128]{2,1,0:T(8,128)(2,1)} %class_sum.1), calls=%async_computation | async-start | bytes 688128 | tf_op jit(solution)/shard_map/all_to_all | solution.py:361
  84.8 0.0 copy-done.4
  84.8 0.0 copy-done.3
  84.8 0.0 copy-done.6
  84.8 0.9 suffix_part.1.suffix_ref
  85.7 13.6 %all-to-all-done.parts_ref = bf16[4,336,128]{2,1,0:T(8,128)(2,1)S(1)} async-done(((bf16[4,336,128]{2,1,0:T(8,128)(2,1)}), bf16[4,336,128]{2,1,0:T(8,128)(2,1)S(1)}, u32[]{:S(2)}, u32[]{:S(2)}) %all-to-all-start) | async-done | bytes 344096 | tf_op jit(solution)/shard_map/all_to_all | solution.py:361
  99.3 0.5 attended.1
  99.8 19.9 %all_gather.7.refs_0_ = bf16[4,320,128]{2,1,0:T(8,128)(2,1)S(1)} all-gather(bf16[1,320,128]{2,1,0:T(8,128)(2,1)S(1)} %attended.1), channel_id=1, replica_groups={{0,32,64,96},{8,40,72,104},{16,48,80,112},{24,56,88,120},{1,33,65,97},{..., dimensions={0}, use_global_device_ids=true | all-gather | bytes 409600 | tf_op jit(solution)/shard_map/all_gather | solution.py:338
  119.6 0.0 copy-start.5
  119.6 5.6 %collective-permute-start.9 = (bf16[4,320,128]{2,1,0:T(8,128)(2,1)S(1)}, bf16[4,320,128]{2,1,0:T(8,128)(2,1)S(1)}, u32[]{:S(2)}, u32[]{:S(2)}) collective-permute-start(bf16[4,320,128]{2,1,0:T(8,128)(2,1)S(1)} %all_gather.7.refs_0_), channel_id=1, source_target_pairs={{120,0},{0,8},{8,16},{16,24},{24,32},{32,40},{40,48},{48,56},{56,6... | collective-permute-start | bytes 983048 | tf_op jit(solution)/shard_map/ppermute | solution.py:267
  125.2 1.9 %collective-permute-start.8 = (bf16[4,320,128]{2,1,0:T(8,128)(2,1)S(1)}, bf16[4,320,128]{2,1,0:T(8,128)(2,1)S(1)}, u32[]{:S(2)}, u32[]{:S(2)}) collective-permute-start(bf16[4,320,128]{2,1,0:T(8,128)(2,1)S(1)} %all_gather.7.refs_0_), channel_id=1, source_target_pairs={{8,0},{16,8},{24,16},{32,24},{40,32},{48,40},{56,48},{64,56},{72,6... | collective-permute-start | bytes 983048 | tf_op jit(solution)/shard_map/ppermute | solution.py:267
  127.2 9.3 %collective-permute-start.11 = (bf16[2,320,128]{2,1,0:T(8,128)(2,1)S(1)}, bf16[2,320,128]{2,1,0:T(8,128)(2,1)S(1)}, u32[]{:S(2)}, u32[]{:S(2)}) collective-permute-start(bf16[2,320,128]{2,1,0:T(8,128)(2,1)S(1)} %get-tuple-element.9), channel_id=1, source_target_pairs={{112,0},{120,8},{0,16},{8,24},{16,32},{24,40},{32,48},{40,56},{48,... | collective-permute-start | bytes 491528 | tf_op jit(solution)/shard_map/ppermute | solution.py:267
  136.5 1.9 %collective-permute-start.10 = (bf16[2,320,128]{2,1,0:T(8,128)(2,1)S(1)}, bf16[2,320,128]{2,1,0:T(8,128)(2,1)S(1)}, u32[]{:S(2)}, u32[]{:S(2)}) collective-permute-start(bf16[2,320,128]{2,1,0:T(8,128)(2,1)S(1)} %get-tuple-element.10), channel_id=1, source_target_pairs={{16,0},{24,8},{32,16},{40,24},{48,32},{56,40},{64,48},{72,56},{80,... | collective-permute-start | bytes 491528 | tf_op jit(solution)/shard_map/ppermute | solution.py:267
  138.4 2.6 %collective-permute-done.11.refs_4_ = bf16[2,320,128]{2,1,0:T(8,128)(2,1)S(1)} collective-permute-done((bf16[2,320,128]{2,1,0:T(8,128)(2,1)S(1)}, bf16[2,320,128]{2,1,0:T(8,128)(2,1)S(1)}, u32[]{:S(2)}, u32[]{:S(2)}) %collective-permute-start.11) | collective-permute-done | bytes 163872 | tf_op jit(solution)/shard_map/ppermute | solution.py:267
  141.1 4.7 %collective-permute-done.10.refs_3_ = bf16[2,320,128]{2,1,0:T(8,128)(2,1)S(1)} collective-permute-done((bf16[2,320,128]{2,1,0:T(8,128)(2,1)S(1)}, bf16[2,320,128]{2,1,0:T(8,128)(2,1)S(1)}, u32[]{:S(2)}, u32[]{:S(2)}) %collective-permute-start.10) | collective-permute-done | bytes 163872 | tf_op jit(solution)/shard_map/ppermute | solution.py:267
  145.8 0.0 collective-permute-done.9.refs_2_
  145.8 0.0 collective-permute-done.8.refs_1_
  145.8 0.0 copy-done.5
  145.8 1.1 projection.1
  147.0 13.7 %all_to_all.10.parts_ref = bf16[8,320,128]{2,1,0:T(8,128)(2,1)S(1)} all-to-all(bf16[8,320,128]{2,1,0:T(8,128)(2,1)S(1)} %projection.1), channel_id=1, replica_groups=mesh['prompt'=4,'seq'=16,'head'=8] {'head'}, dimensions={0} | all-to-all | bytes 1310720 | tf_op jit(solution)/shard_map/all_to_all | solution.py:271
  160.6 0.8 head_sum.1
  (2 shorter events, 0.1 us)
Async XLA Ops:
  0.0 43.7 %copy-start = (bf16[4096,128]{1,0:T(8,128)(2,1)S(1)}, bf16[4096,128]{1,0:T(8,128)(2,1)}, u32[]{:S(2)}) copy-start(bf16[4096,128]{1,0:T(8,128)(2,1)} %refs_2_.7) | copy-start | bytes 3145732
  27.9 15.8 %collective-permute-start = (bf16[4,64,640]{2,1,0:T(8,128)(2,1)S(1)}, bf16[4,64,640]{2,1,0:T(8,128)(2,1)S(1)}, u32[]{:S(2)}, u32[]{:S(2)}) collective-permute-start(bf16[4,64,640]{2,1,0:T(8,128)(2,1)S(1)} %all_gather.6.refs_0_), channel_id=1, source_target_pairs={{8,0},{16,8},{24,16},{32,24},{40,32},{48,40},{56,48},{64,56},{72,6... | collective-permute-start | bytes 983048 | tf_op jit(solution)/shard_map/ppermute | solution.py:267
  31.7 18.9 %collective-permute-start.2 = (bf16[4,64,640]{2,1,0:T(8,128)(2,1)S(1)}, bf16[4,64,640]{2,1,0:T(8,128)(2,1)S(1)}, u32[]{:S(2)}, u32[]{:S(2)}) collective-permute-start(bf16[4,64,640]{2,1,0:T(8,128)(2,1)S(1)} %all_gather.6.refs_0_), channel_id=1, source_target_pairs={{120,0},{0,8},{8,16},{16,24},{24,32},{32,40},{40,48},{48,56},{56,6... | collective-permute-start | bytes 983048 | tf_op jit(solution)/shard_map/ppermute | solution.py:267
  33.9 24.3 %collective-permute-start.5 = (bf16[2,64,640]{2,1,0:T(8,128)(2,1)S(1)}, bf16[2,64,640]{2,1,0:T(8,128)(2,1)S(1)}, u32[]{:S(2)}, u32[]{:S(2)}) collective-permute-start(bf16[2,64,640]{2,1,0:T(8,128)(2,1)S(1)} %get-tuple-element.11), channel_id=1, source_target_pairs={{112,0},{120,8},{0,16},{8,24},{16,32},{24,40},{32,48},{40,56},{48,... | collective-permute-start | bytes 491528 | tf_op jit(solution)/shard_map/ppermute | solution.py:267
  38.4 19.9 %collective-permute-start.4 = (bf16[2,64,640]{2,1,0:T(8,128)(2,1)S(1)}, bf16[2,64,640]{2,1,0:T(8,128)(2,1)S(1)}, u32[]{:S(2)}, u32[]{:S(2)}) collective-permute-start(bf16[2,64,640]{2,1,0:T(8,128)(2,1)S(1)} %get-tuple-element.12), channel_id=1, source_target_pairs={{16,0},{24,8},{32,16},{40,24},{48,32},{56,40},{64,48},{72,56},{80,... | collective-permute-start | bytes 491528 | tf_op jit(solution)/shard_map/ppermute | solution.py:267
  43.7 1.2 copy-start.1
  45.0 0.7 copy-start.7
  48.3 26.6 %collective-permute-start.1 = (bf16[4,336,128]{2,1,0:T(8,128)(2,1)S(1)}, bf16[4,336,128]{2,1,0:T(8,128)(2,1)S(1)}, u32[]{:S(2)}, u32[]{:S(2)}) collective-permute-start(bf16[4,336,128]{2,1,0:T(8,128)(2,1)S(1)} %prefix_part.5), channel_id=1, source_target_pairs={{120,0},{0,8},{8,16},{16,24},{24,32},{32,40},{40,48},{48,56},{56,6... | collective-permute-start | bytes 1032200 | tf_op jit(solution)/shard_map/ppermute | solution.py:267
  54.0 15.9 %copy-start.2 = (bf16[4096,128]{1,0:T(8,128)(2,1)S(1)}, bf16[4096,128]{1,0:T(8,128)(2,1)}, u32[]{:S(2)}) copy-start(bf16[4096,128]{1,0:T(8,128)(2,1)} %refs_3_.1) | copy-start | bytes 3145732
  54.0 20.9 %collective-permute-start.3 = (bf16[4,336,128]{2,1,0:T(8,128)(2,1)S(1)}, bf16[4,336,128]{2,1,0:T(8,128)(2,1)S(1)}, u32[]{:S(2)}, u32[]{:S(2)}) collective-permute-start(bf16[4,336,128]{2,1,0:T(8,128)(2,1)S(1)} %prefix_part.6), channel_id=1, source_target_pairs={{8,0},{16,8},{24,16},{32,24},{40,32},{48,40},{56,48},{64,56},{72,6... | collective-permute-start | bytes 1032200 | tf_op jit(solution)/shard_map/ppermute | solution.py:267
  61.9 11.2 %collective-permute-start.6 = (bf16[2,336,128]{2,1,0:T(8,128)(2,1)S(1)}, bf16[2,336,128]{2,1,0:T(8,128)(2,1)S(1)}, u32[]{:S(2)}, u32[]{:S(2)}) collective-permute-start(bf16[2,336,128]{2,1,0:T(8,128)(2,1)S(1)} %get-tuple-element.7), channel_id=1, source_target_pairs={{112,0},{120,8},{0,16},{8,24},{16,32},{24,40},{32,48},{40,56},{48,... | collective-permute-start | bytes 516104 | tf_op jit(solution)/shard_map/ppermute | solution.py:267
  63.8 11.1 %collective-permute-start.7 = (bf16[2,336,128]{2,1,0:T(8,128)(2,1)S(1)}, bf16[2,336,128]{2,1,0:T(8,128)(2,1)S(1)}, u32[]{:S(2)}, u32[]{:S(2)}) collective-permute-start(bf16[2,336,128]{2,1,0:T(8,128)(2,1)S(1)} %get-tuple-element.8), channel_id=1, source_target_pairs={{16,0},{24,8},{32,16},{40,24},{48,32},{56,40},{64,48},{72,56},{80,... | collective-permute-start | bytes 516104 | tf_op jit(solution)/shard_map/ppermute | solution.py:267
  74.9 9.9 %copy-start.4 = (bf16[1,2048,128]{2,1,0:T(8,128)(2,1)S(1)}, bf16[1,2048,128]{2,1,0:T(8,128)(2,1)}, u32[]{:S(2)}) copy-start(bf16[1,2048,128]{2,1,0:T(8,128)(2,1)} %v_ref.1) | copy-start | bytes 1572868
  76.6 8.2 %copy-start.3 = (bf16[1,2048,128]{2,1,0:T(8,128)(2,1)S(1)}, bf16[1,2048,128]{2,1,0:T(8,128)(2,1)}, u32[]{:S(2)}) copy-start(bf16[1,2048,128]{2,1,0:T(8,128)(2,1)} %k_ref.1) | copy-start | bytes 1572868
  76.6 8.2 %copy-start.6 = (bf16[1,64,640]{2,1,0:T(8,128)(2,1)S(1)}, bf16[1,64,640]{2,1,0:T(8,128)(2,1)}, u32[]{:S(2)}) copy-start(bf16[1,64,640]{2,1,0:T(8,128)(2,1)} %q_ref.1) | copy-start | bytes 245764
  76.6 22.7 %all-to-all-start = ((bf16[4,336,128]{2,1,0:T(8,128)(2,1)}), bf16[4,336,128]{2,1,0:T(8,128)(2,1)S(1)}, u32[]{:S(2)}, u32[]{:S(2)}) async-start(bf16[4,336,128]{2,1,0:T(8,128)(2,1)} %class_sum.1), calls=%async_computation | async-start | bytes 688128 | tf_op jit(solution)/shard_map/all_to_all | solution.py:361
  119.6 26.2 %copy-start.5 = (bf16[640,320]{0,1:T(8,128)(2,1)S(1)}, bf16[640,320]{0,1:T(8,128)(2,1)}, u32[]{:S(2)}) copy-start(bf16[640,320]{0,1:T(8,128)(2,1)} %param.15) | copy-start | bytes 1228804
  119.6 26.2 %collective-permute-start.9 = (bf16[4,320,128]{2,1,0:T(8,128)(2,1)S(1)}, bf16[4,320,128]{2,1,0:T(8,128)(2,1)S(1)}, u32[]{:S(2)}, u32[]{:S(2)}) collective-permute-start(bf16[4,320,128]{2,1,0:T(8,128)(2,1)S(1)} %all_gather.7.refs_0_), channel_id=1, source_target_pairs={{120,0},{0,8},{8,16},{16,24},{24,32},{32,40},{40,48},{48,56},{56,6... | collective-permute-start | bytes 983048 | tf_op jit(solution)/shard_map/ppermute | solution.py:267
  125.2 20.6 %collective-permute-start.8 = (bf16[4,320,128]{2,1,0:T(8,128)(2,1)S(1)}, bf16[4,320,128]{2,1,0:T(8,128)(2,1)S(1)}, u32[]{:S(2)}, u32[]{:S(2)}) collective-permute-start(bf16[4,320,128]{2,1,0:T(8,128)(2,1)S(1)} %all_gather.7.refs_0_), channel_id=1, source_target_pairs={{8,0},{16,8},{24,16},{32,24},{40,32},{48,40},{56,48},{64,56},{72,6... | collective-permute-start | bytes 983048 | tf_op jit(solution)/shard_map/ppermute | solution.py:267
  127.2 13.9 %collective-permute-start.11 = (bf16[2,320,128]{2,1,0:T(8,128)(2,1)S(1)}, bf16[2,320,128]{2,1,0:T(8,128)(2,1)S(1)}, u32[]{:S(2)}, u32[]{:S(2)}) collective-permute-start(bf16[2,320,128]{2,1,0:T(8,128)(2,1)S(1)} %get-tuple-element.9), channel_id=1, source_target_pairs={{112,0},{120,8},{0,16},{8,24},{16,32},{24,40},{32,48},{40,56},{48,... | collective-permute-start | bytes 491528 | tf_op jit(solution)/shard_map/ppermute | solution.py:267
  136.5 9.3 %collective-permute-start.10 = (bf16[2,320,128]{2,1,0:T(8,128)(2,1)S(1)}, bf16[2,320,128]{2,1,0:T(8,128)(2,1)S(1)}, u32[]{:S(2)}, u32[]{:S(2)}) collective-permute-start(bf16[2,320,128]{2,1,0:T(8,128)(2,1)S(1)} %get-tuple-element.10), channel_id=1, source_target_pairs={{16,0},{24,8},{32,16},{40,24},{48,32},{56,40},{64,48},{72,56},{80,... | collective-permute-start | bytes 491528 | tf_op jit(solution)/shard_map/ppermute | solution.py:267

commit v3 on v2

v3 whole, which is shorter than its diff:
```python
import functools
import math

import jax
import jax.numpy as jnp
from jax import lax
from jax.experimental import pallas as pl
from jax.experimental.pallas import tpu as pltpu
from jax.sharding import PartitionSpec as P

HD = 128
GQA = 5
QB = 64
BLOCK = 128
MOST = 8
ROWS = GQA * QB
TILE = 128
TOKEN_RUNS = 8
WIDE = 384
FLOOR = -1e30
HIDDEN = -2e30
SCALE2 = math.log2(math.e) / math.sqrt(HD)
WIRE = ROWS + 16
VMEM_LIMIT = 24 * 2**20


def in_vmem():
    return pl.BlockSpec(memory_space=pltpu.VMEM)


def in_smem():
    return pl.BlockSpec(memory_space=pltpu.SMEM)


def params():
    return pltpu.CompilerParams(vmem_limit_bytes=VMEM_LIMIT)


def group_of(pos_ref, offset, classes):
    return lax.rem(pos_ref[0] + offset * pos_ref[1] + classes, classes)


def slots_of(rel, blocks_here):
    samples, keep = rel.shape
    here = (rel >= 0) & (rel < blocks_here)
    earlier = lax.broadcasted_iota(jnp.int32, (keep, keep), 0) < lax.broadcasted_iota(
        jnp.int32, (keep, keep), 1
    )
    rank = jnp.dot(
        here.astype(jnp.float32).astype(jnp.bfloat16),
        earlier.astype(jnp.float32).astype(jnp.bfloat16),
        preferred_element_type=jnp.float32,
    ).astype(jnp.int32)
    lane = lax.broadcasted_iota(jnp.int32, (samples, 128), 1)
    number = jnp.sum(here.astype(jnp.int32), axis=1, keepdims=True)
    out = jnp.where(lane == MOST, number, 0)
    first = None
    for k in range(MOST):
        chosen = jnp.sum(jnp.where(here & (rank == k), rel, 0), axis=1, keepdims=True)
        if k:
            chosen = jnp.where(number > k, chosen, first)
        else:
            first = chosen
        out = jnp.where(lane == k, chosen, out)
    return out


def query_rows(q):
    return jnp.concatenate([q[:, j * HD : (j + 1) * HD] for j in range(GQA)], axis=0)


def across(asking, keys):
    return (
        lax.dot_general(
            asking, keys, (((1,), (1,)), ((), ())), preferred_element_type=jnp.float32
        )
        * SCALE2
    )


def weighted(prob, values):
    ones = jnp.ones((values.shape[0], HD), jnp.bfloat16)
    return jnp.dot(
        prob, jnp.concatenate([values, ones], axis=1), preferred_element_type=jnp.float32
    )


def laid_flat(stat):
    turned = jnp.concatenate([stat, jnp.zeros((WIDE - ROWS, TILE), jnp.float32)], axis=0).T

    def flat(i):
        row = turned[i : i + 1]
        return jnp.concatenate(
            [row[:, c * TILE : (c + 1) * TILE] for c in range(WIDE // TILE)], axis=0
        )

    return flat


def columns(flats):
    rows = [jnp.concatenate([f[c : c + 1] for c in range(WIDE // TILE)], axis=1) for f in flats]
    spare = -len(rows) % 8
    if spare:
        rows.append(jnp.zeros((spare, WIDE), jnp.float32))
    turned = jnp.concatenate(rows, axis=0).T
    return [turned[:ROWS, i : i + 1] for i in range(len(flats))]


def wire_rows(flat):
    high = flat.astype(jnp.bfloat16).astype(jnp.float32)
    middle = (flat - high).astype(jnp.bfloat16).astype(jnp.float32)
    low = flat - high - middle
    spare = jnp.zeros((WIRE - ROWS - 9, TILE), jnp.float32)
    return jnp.concatenate([high, middle, low, spare], axis=0).astype(jnp.bfloat16)


def unwire_rows(rows):
    rows = rows.astype(jnp.float32)
    return rows[0:3] + rows[3:6] + rows[6:9]


def shares_of(flats):
    top = functools.reduce(jnp.maximum, flats)
    shares = [jnp.exp2(f - top) for f in flats]
    total = functools.reduce(jnp.add, shares)
    return [share / total for share in shares], top + jnp.log2(total)


def added(parts, shares):
    return functools.reduce(
        jnp.add, [p.astype(jnp.float32) * c for p, c in zip(parts, shares, strict=True)]
    )


def attend(group, classes, slots_ref, q_refs, k_ref, v_ref, out_refs):
    ranges = [q_ref.shape[0] for q_ref in q_refs]
    lane = lax.broadcasted_iota(jnp.int32, (ROWS, TILE), 1)
    stat = jnp.zeros((ROWS, TILE), jnp.float32)
    asked = [(q, o, i) for q, o, many in zip(q_refs, out_refs, ranges, strict=True) for i in range(many)]

    def places_of(k):
        return [
            pl.ds(pl.multiple_of(slots_ref[group + classes * k, j] * BLOCK, BLOCK), BLOCK)
            for j in range(MOST)
        ]

    def scores_of(k):
        q_ref, _, i = asked[k]
        asking = query_rows(q_ref[i])
        keys = [k_ref[place, :] for place in places_of(k)]
        return [
            across(asking, jnp.concatenate(keys[j : j + 2], axis=0)) for j in range(0, MOST, 2)
        ]

    coming = scores_of(0)
    for k, (_, out_ref, i) in enumerate(asked):
        scores = coming
        if k + 1 < len(asked):
            coming = scores_of(k + 1)
        count = slots_ref[group + classes * k, MOST]
        top = jnp.max(functools.reduce(jnp.maximum, scores), axis=1, keepdims=True)
        prob = jnp.concatenate([jnp.exp2(x - top).astype(jnp.bfloat16) for x in scores], axis=1)
        used = [(j < count).astype(jnp.float32).astype(jnp.bfloat16) for j in range(MOST)]
        values = jnp.concatenate(
            [
                jnp.concatenate(
                    [v_ref[place, :] * u, jnp.full((BLOCK, HD), u, jnp.bfloat16)], axis=1
                )
                for place, u in zip(places_of(k), used, strict=True)
            ],
            axis=0,
        )
        both = jnp.dot(prob, values, preferred_element_type=jnp.float32)
        total = both[:, HD:]
        some = total > 0.0
        total = jnp.where(some, total, 1.0)
        out_ref[i, :ROWS, :] = (both[:, :HD] / total).astype(jnp.bfloat16)
        stat = jnp.where(lane == k, jnp.where(some, top + jnp.log2(total), FLOOR), stat)
    flat = laid_flat(stat)
    first = 0
    for out_ref, many in zip(out_refs, ranges, strict=True):
        for i in range(many):
            out_ref[i, ROWS:, :] = wire_rows(flat(first + i))
        first += many


def first_kernel(
    pos_ref, kept_ref, q_ref, k_hbm, v_hbm, out_ref, slots_out_ref, k_ref, v_ref, slots_ref, sems, *, offset, classes
):
    k_copy = pltpu.make_async_copy(k_hbm, k_ref, sems.at[0])
    v_copy = pltpu.make_async_copy(v_hbm, v_ref, sems.at[1])
    k_copy.start()
    v_copy.start()
    slots_out_ref[...] = slots_of(kept_ref[...] - pos_ref[0] * (k_ref.shape[0] // BLOCK), k_ref.shape[0] // BLOCK)
    slots_copy = pltpu.make_async_copy(slots_out_ref, slots_ref, sems.at[2])
    slots_copy.start()
    slots_copy.wait()
    k_copy.wait()
    v_copy.wait()
    group = group_of(pos_ref, offset, classes)
    attend(group, classes, slots_ref, [q_ref], k_ref, v_ref, [out_ref])


def prefix_kernel(pos_ref, slots_ref, *refs, offset, classes, many):
    q_refs, k_ref, v_ref, out_refs = refs[:many], refs[many], refs[many + 1], refs[-many:]
    group = group_of(pos_ref, offset, classes)
    attend(group, classes, slots_ref, q_refs, k_ref, v_ref, out_refs)


def suffix_kernel(length_ref, q_ref, k_ref, v_ref, out_ref):
    chunk = 4 * BLOCK
    asking = query_rows(q_ref[0])
    length = length_ref[0]
    token = lax.rem(lax.broadcasted_iota(jnp.int32, (ROWS, chunk), 0), QB)
    slot = lax.broadcasted_iota(jnp.int32, (ROWS, chunk), 1)

    def step(n, carry):
        top, both = carry
        rows = pl.ds(pl.multiple_of(n * chunk, chunk), chunk)
        scores = across(asking, k_ref[0, rows, :])
        scores = jnp.where(slot - token <= length - QB - n * chunk, scores, HIDDEN)
        new_top = jnp.maximum(top, jnp.max(scores, axis=1, keepdims=True))
        prob = jnp.exp2(scores - new_top).astype(jnp.bfloat16)
        both = both * jnp.exp2(top - new_top) + weighted(prob, v_ref[0, rows, :])
        return new_top, both

    start = (jnp.full((ROWS, 1), FLOOR, jnp.float32), jnp.zeros((ROWS, 2 * HD), jnp.float32))
    top, both = lax.fori_loop(0, lax.div(length + chunk - 1, chunk), step, start)
    total = both[:, HD:]
    out_ref[:ROWS, :] = both[:, :HD] / total
    flat = laid_flat(top + jnp.log2(total))(0)
    out_ref[ROWS:, :] = jnp.concatenate([flat, jnp.zeros((5, TILE), jnp.float32)], axis=0)


def class_kernel(own_ref, before_ref, after_ref, far_ref, out_ref, *, members):
    parts, shares = [], []
    for k in range(members):
        here = [ref.at[k] for ref in (own_ref, before_ref, after_ref, far_ref)]
        share, log_sum = shares_of([unwire_rows(ref[ROWS:, :]) for ref in here])
        out_ref[k, ROWS:, :] = wire_rows(log_sum)
        parts.append(here)
        shares += share
    shares = columns(shares)
    for k, here in enumerate(parts):
        out_ref[k, :ROWS, :] = added(
            [ref[:ROWS, :] for ref in here], shares[k * len(here) : (k + 1) * len(here)]
        ).astype(jnp.bfloat16)


def final_kernel(suffix_ref, parts_ref, out_ref):
    members = parts_ref.shape[0]
    flats = [suffix_ref[ROWS : ROWS + 3, :]]
    flats += [unwire_rows(parts_ref[i, ROWS:, :]) for i in range(members)]
    shares = columns(shares_of(flats)[0])
    parts = [suffix_ref[:ROWS, :]] + [parts_ref[i, :ROWS, :] for i in range(members)]
    out_ref[0] = added(parts, shares).astype(jnp.bfloat16)


def put_rows(pos_ref, in_refs, rows_ref, classes, layout):
    for ref, (offset, first) in zip(in_refs, layout, strict=True):
        group = group_of(pos_ref, offset, classes)
        for i in range(ref.shape[0]):
            rows = ref[i]
            sample = group + classes * (first + i)
            rows_ref[pl.ds(pl.multiple_of(sample * QB, QB), QB), :] = jnp.concatenate(
                [rows[j * QB : (j + 1) * QB] for j in range(GQA)], axis=1
            )


def rows_kernel(pos_ref, *refs, classes, layout):
    put_rows(pos_ref, refs[:-1], refs[-1], classes, layout)


def project_kernel(pos_ref, *refs, classes, layout):
    n = len(layout)
    in_refs, w_ref, _, rows_ref, out_ref = refs[:n], *refs[n:]
    put_rows(pos_ref, in_refs, rows_ref, classes, layout)
    weight = w_ref[...]
    tokens = rows_ref.shape[0] // out_ref.shape[0]
    for i in range(out_ref.shape[0]):
        out_ref[i] = lax.dot_general(
            weight,
            rows_ref[i * tokens : (i + 1) * tokens, :],
            (((1,), (1,)), ((), ())),
            preferred_element_type=jnp.float32,
        ).astype(jnp.bfloat16)


def sum_kernel(parts_ref, out_ref):
    out_ref[...] = functools.reduce(
        jnp.add, [parts_ref[i].astype(jnp.float32) for i in range(parts_ref.shape[0])]
    )


def sign_of(prompt):
    return 1 - 2 * (prompt % 2)


def shifted(x, distance):
    prompts, size = lax.axis_size("prompt"), lax.axis_size("seq")
    route = [
        (p * size + (i + distance * sign_of(p)) % size, p * size + i)
        for p in range(prompts)
        for i in range(size)
    ]
    return lax.ppermute(x, ("prompt", "seq"), route)


def head_exchange(x):
    return lax.all_to_all(x, "head", 0, 0, tiled=True)


def summed(parts):
    return pl.pallas_call(
        sum_kernel,
        out_shape=jax.ShapeDtypeStruct(parts.shape[1:], jnp.float32),
        in_specs=[in_vmem()],
        out_specs=in_vmem(),
        compiler_params=params(),
        name="head_sum",
    )(parts).T


def body(
    queries,
    prefix_keys,
    prefix_values,
    suffix_keys,
    suffix_values,
    kept_blocks,
    suffix_lengths,
    out_weight,
):
    size = lax.axis_size("seq")
    classes = 4
    members = size // classes
    groups = [[g + classes * i for i in range(members)] for g in range(classes)]
    position = jnp.stack([lax.axis_index("seq"), sign_of(lax.axis_index("prompt"))]).astype(jnp.int32)
    bf16, f32 = jnp.bfloat16, jnp.float32

    def cost(many):
        work = many * ROWS * MOST * BLOCK
        return pl.CostEstimate(flops=work * HD * 4, bytes_accessed=2**21, transcendentals=work)

    def wired(many):
        return jax.ShapeDtypeStruct((many, WIRE, HD), bf16)

    def first_part(offset, asked):
        anywhere = pl.BlockSpec(memory_space=pltpu.HBM)
        return pl.pallas_call(
            functools.partial(first_kernel, offset=offset, classes=classes),
            out_shape=[
                wired(asked.shape[0]),
                jax.ShapeDtypeStruct((kept_blocks.shape[0], 128), jnp.int32),
                jax.ShapeDtypeStruct(prefix_keys.shape, bf16),
                jax.ShapeDtypeStruct(prefix_values.shape, bf16),
            ],
            in_specs=[in_smem(), in_vmem(), in_vmem(), anywhere, anywhere],
            out_specs=[in_vmem()] * 4,
            scratch_shapes=[
                pltpu.SMEM((kept_blocks.shape[0], 128), jnp.int32),
                pltpu.SemaphoreType.DMA((3,)),
            ],
            compiler_params=params(),
            cost_estimate=cost(asked.shape[0]),
            name="first_part",
        )(position, kept_blocks, asked, prefix_keys, prefix_values)

    def prefix_part(offset, slots, keys, values, *asked):
        return pl.pallas_call(
            functools.partial(prefix_kernel, offset=offset, classes=classes, many=len(asked)),
            out_shape=[wired(a.shape[0]) for a in asked],
            in_specs=[in_smem(), in_smem()] + [in_vmem()] * (len(asked) + 2),
            out_specs=[in_vmem()] * len(asked),
            compiler_params=params(),
            cost_estimate=cost(sum(a.shape[0] for a in asked)),
            name="prefix_part",
        )(position, slots, *asked, keys, values)

    suffix = pl.pallas_call(
        suffix_kernel,
        out_shape=jax.ShapeDtypeStruct((ROWS + 8, HD), f32),
        in_specs=[in_smem()] + [in_vmem()] * 3,
        out_specs=in_vmem(),
        compiler_params=params(),
        name="suffix_part",
    )(suffix_lengths, queries, suffix_keys, suffix_values)

    def gathered_class(x):
        return lax.all_gather(x, "seq", axis=0, tiled=True, axis_index_groups=groups)

    mine = gathered_class(queries)
    from_after = shifted(mine, 1)
    from_before = shifted(mine, -1)
    from_far = shifted(mine, 2)

    for_after, *held = first_part(1, from_after)
    (for_before,) = prefix_part(-1, *held, from_before)
    (for_far,) = prefix_part(2, *held, from_far)
    (own,) = prefix_part(0, *held, mine)
    by_before = shifted(for_after, -1)
    by_after = shifted(for_before, 1)
    by_far = shifted(for_far, -2)

    gathered = pl.pallas_call(
        functools.partial(class_kernel, members=members),
        out_shape=jax.ShapeDtypeStruct((members, WIRE, HD), bf16),
        in_specs=[in_vmem()] * 4,
        out_specs=in_vmem(),
        compiler_params=params(),
        name="class_sum",
    )(own, by_before, by_after, by_far)
    arrived = lax.all_to_all(gathered, "seq", 0, 0, tiled=True, axis_index_groups=groups)
    attended = pl.pallas_call(
        final_kernel,
        out_shape=jax.ShapeDtypeStruct((1, ROWS, HD), bf16),
        in_specs=[in_vmem()] * 2,
        out_specs=in_vmem(),
        compiler_params=params(),
        name="attended",
    )(suffix, arrived)

    same = gathered_class(attended)
    tokens, heads = size * QB, TOKEN_RUNS
    near = ((shifted(same, 1), (1, 0)), (shifted(same, -1), (-1, 0)))
    rest = (
        (same, (0, 0)),
        (shifted(same, 2), (2, 0)),
    )
    rows_shape = jax.ShapeDtypeStruct((tokens, GQA * HD), bf16)
    rows = pl.pallas_call(
        functools.partial(rows_kernel, classes=classes, layout=tuple(w for _, w in rest)),
        out_shape=rows_shape,
        in_specs=[in_smem()] + [in_vmem()] * len(rest),
        out_specs=in_vmem(),
        compiler_params=params(),
        cost_estimate=pl.CostEstimate(flops=3 * 10**10, bytes_accessed=2**21, transcendentals=0),
        name="far_rows",
    )(position, *[piece for piece, _ in rest])
    _, partial_value = pl.pallas_call(
        functools.partial(project_kernel, classes=classes, layout=tuple(w for _, w in near)),
        out_shape=[
            rows_shape,
            jax.ShapeDtypeStruct((heads, out_weight.shape[1], tokens // heads), bf16),
        ],
        in_specs=[in_smem()] + [in_vmem()] * (len(near) + 2),
        out_specs=[in_vmem()] * 2,
        input_output_aliases={len(near) + 2: 0},
        compiler_params=params(),
        name="projection",
    )(position, *[piece for piece, _ in near], out_weight.T, rows)
    return summed(head_exchange(partial_value))


def solution(mesh):
    in_specs = (
        P(("prompt", "seq"), None, "head"),
        P(("prompt", "seq"), "head"),
        P(("prompt", "seq"), "head"),
        P(("prompt", "seq"), None, "head"),
        P(("prompt", "seq"), None, "head"),
        P("prompt", None),
        P(("prompt", "seq")),
        P("head", "seq"),
    )
    out_specs = P(("prompt", "head"), "seq")
    return jax.shard_map(body, mesh=mesh, in_specs=in_specs, out_specs=out_specs, check_vma=False)
```

time: 162 us -> 155 us (0.957)
  starting transfers between devices: 54.6 us -> 34.6 us
  waiting for transfers between devices: 23.3 us -> 30.1 us
  blocking collectives: 61.4 us -> 65.8 us
    ppermute x12 -> x9, starting transfers between devices: 47.1 us -> 26.5 us  [shifted(): return lax.ppermute(x, ('prompt', 'seq'), route)]
    ppermute x12 -> x9, waiting for transfers between devices: 9.7 us -> 16.7 us  [shifted(): return lax.ppermute(x, ('prompt', 'seq'), route)]
    pallas_call x4 -> x3, Pallas kernels: 12.4 us -> 8.21 us  [prefix_part(): pl.pallas_call(functools.partial(prefix_kernel, offset=offset, classes=cl...]
    all_to_all x1, blocking collectives: 13.7 us -> 16.7 us  [head_exchange(): return lax.all_to_all(x, 'head', 0, 0, tiled=True)]
    pallas_call x1 -> x2, Pallas kernels: 1.81 us -> 4.3 us  [the longest x1 3.67 us: first_part(): pl.pallas_call(functools.partial(first_kernel, offset=offset, classes=cla...]
    pallas_call x1, Pallas kernels: 0.9 us -> 2.97 us  [body(): pl.pallas_call(suffix_kernel, out_shape=jax.ShapeDtypeStruct((ROWS + 8, H...]
  transfers between devices with their start and end apart: 13 -> 10, of which waited for: 5 -> 8; matrix products, arithmetic and copies ran while one was open for 0% -> 0% of each run, Pallas kernels for 9% -> 10%
where the time goes in v3:
time: 155 us; the launch traced here: 154 us
  blocking collectives  65.8 us (42%)
  starting transfers between devices  34.6 us (22%)
  waiting for transfers between devices  30.1 us (19%)
  Pallas kernels  20 us (13%)
  local copies, waits for them, and re-layouts  3.17 us (2%)
    all_gather x2, blocking collectives, gathered_class(): lax.all_gather(x, 'seq', axis=0, tiled=True, axis_index_groups=groups)  49.1 us
    ppermute x9, starting transfers between devices, shifted(): return lax.ppermute(x, ('prompt', 'seq'), route)  26.5 us
    all_to_all x1, blocking collectives, head_exchange(): return lax.all_to_all(x, 'head', 0, 0, tiled=True)  16.7 us
    ppermute x9, waiting for transfers between devices, shifted(): return lax.ppermute(x, ('prompt', 'seq'), route)  16.7 us
    all_to_all x1, waiting for transfers between devices, body(): lax.all_to_all(gathered, 'seq', 0, 0, tiled=True, axis_index_groups=groups)  13.4 us
    pallas_call x3, Pallas kernels, prefix_part(): pl.pallas_call(functools.partial(prefix_kernel, offset=offset, classes=cl...  8.21 us
    all_to_all x1, starting transfers between devices, body(): lax.all_to_all(gathered, 'seq', 0, 0, tiled=True, axis_index_groups=groups)  8.05 us
    pallas_call x1, Pallas kernels, first_part(): pl.pallas_call(functools.partial(first_kernel, offset=offset, classes=cla...  3.67 us
  transfers between devices with their start and end apart: 10, of which 8 were waited for; matrix products, arithmetic and copies ran while one was open for 0% of the time, Pallas kernels for 10%

profile of v3, /device:TPU:8, one launch (start us, length us, event | category | flops | bytes accessed | tf_op | source)
XLA Modules:
  0.0 154.5 jit_solution(9755108570444779348)
XLA Ops:
  0.0 27.8 %all_gather.6.refs_0_ = bf16[4,64,640]{2,1,0:T(8,128)(2,1)S(1)} all-gather(bf16[1,64,640]{2,1,0:T(8,128)(2,1)} %q_ref.1), channel_id=1, replica_groups={{0,32,64,96},{8,40,72,104},{16,48,80,112},{24,56,88,120},{1,33,65,97},{..., dimensions={0}, use_global_device_ids=true | all-gather | bytes 409600 | tf_op jit(solution)/shard_map/all_gather | solution.py:390
  27.8 3.8 %collective-permute-start = (bf16[4,64,640]{2,1,0:T(8,128)(2,1)S(1)}, bf16[4,64,640]{2,1,0:T(8,128)(2,1)S(1)}, u32[]{:S(2)}, u32[]{:S(2)}) collective-permute-start(bf16[4,64,640]{2,1,0:T(8,128)(2,1)S(1)} %all_gather.6.refs_0_), channel_id=1, source_target_pairs={{8,0},{16,8},{24,16},{32,24},{40,32},{48,40},{56,48},{64,56},{72,6... | collective-permute-start | bytes 983048 | tf_op jit(solution)/shard_map/ppermute | solution.py:306
  31.6 2.7 %collective-permute-start.4 = (bf16[4,64,640]{2,1,0:T(8,128)(2,1)S(1)}, bf16[4,64,640]{2,1,0:T(8,128)(2,1)S(1)}, u32[]{:S(2)}, u32[]{:S(2)}) collective-permute-start(bf16[4,64,640]{2,1,0:T(8,128)(2,1)S(1)} %all_gather.6.refs_0_), channel_id=1, source_target_pairs={{16,0},{24,8},{32,16},{40,24},{48,32},{56,40},{64,48},{72,56},{80,... | collective-permute-start | bytes 983048 | tf_op jit(solution)/shard_map/ppermute | solution.py:306
  34.3 2.9 %collective-permute-start.2 = (bf16[4,64,640]{2,1,0:T(8,128)(2,1)S(1)}, bf16[4,64,640]{2,1,0:T(8,128)(2,1)S(1)}, u32[]{:S(2)}, u32[]{:S(2)}) collective-permute-start(bf16[4,64,640]{2,1,0:T(8,128)(2,1)S(1)} %all_gather.6.refs_0_), channel_id=1, source_target_pairs={{120,0},{0,8},{8,16},{16,24},{24,32},{32,40},{40,48},{48,56},{56,6... | collective-permute-start | bytes 983048 | tf_op jit(solution)/shard_map/ppermute | solution.py:306
  37.3 0.1 pad_add_fusion.pos_ref
  37.3 0.9 collective-permute-done.q_ref
  38.2 0.0 copy-start.4
  38.2 1.2 copy-done.4
  39.5 0.0 copy-start.5
  39.5 1.2 copy-done.5
  40.7 0.0 copy-start.6
  40.7 0.7 copy-done.6
  41.4 3.7 %first_part.1 = (bf16[4,336,128]{2,1,0:T(8,128)(2,1)S(1)}, s32[16,128]{1,0:T(8,128)S(1)}, bf16[4096,128]{1,0:T(8,128)(2,1)S(1)}, bf16[4096,128]{1,0:T(8,128)(2,1)S(1)}) custom-call(s32[2]{0:T(128)S(1)} %pad_add_fusion.pos_ref, s32[16,64]{1,0:T(8,128)S(1)} %copy-done.6, bf16[4,64,640]{2,1,0:T(8,128)(2,1)S(1)} %collective-permute-done.q_ref, ...), custom_call_target="tpu_custom_call" | custom-call | flops 671088640 | bytes 2097152 | tf_op jit(solution)/shard_map/first_part/pallas_call | solution.py:350
  45.1 3.8 %collective-permute-done.4.refs_0_ = bf16[4,64,640]{2,1,0:T(8,128)(2,1)S(1)} collective-permute-done((bf16[4,64,640]{2,1,0:T(8,128)(2,1)S(1)}, bf16[4,64,640]{2,1,0:T(8,128)(2,1)S(1)}, u32[]{:S(2)}, u32[]{:S(2)}) %collective-permute-start.4) | collective-permute-done | bytes 327712 | tf_op jit(solution)/shard_map/ppermute | solution.py:306
  48.9 2.7 %prefix_part.5 = bf16[4,336,128]{2,1,0:T(8,128)(2,1)S(1)} custom-call(s32[2]{0:T(128)S(1)} %pad_add_fusion.pos_ref, s32[16,128]{1,0:T(8,128)S(1)} %get-tuple-element.10.slots_ref, bf16[4,64,640]{2,1,0:T(8,128)(2,1)S(1)} %collective-permute-done.4.refs_0_, bf16[4096,128]{1,0:T(8,128)(2,1)S(1)} %get-tuple-element.11.refs_1_, ...), custom_call_target="tpu_custom_call" | custom-call | flops 671088640 | bytes 2097152 | tf_op jit(solution)/shard_map/prefix_part/pallas_call | solution.py:370
  51.6 3.3 %collective-permute-start.5 = (bf16[4,336,128]{2,1,0:T(8,128)(2,1)S(1)}, bf16[4,336,128]{2,1,0:T(8,128)(2,1)S(1)}, u32[]{:S(2)}, u32[]{:S(2)}) collective-permute-start(bf16[4,336,128]{2,1,0:T(8,128)(2,1)S(1)} %prefix_part.5), channel_id=1, source_target_pairs={{112,0},{120,8},{0,16},{8,24},{16,32},{24,40},{32,48},{40,56},{48,... | collective-permute-start | bytes 1032200 | tf_op jit(solution)/shard_map/ppermute | solution.py:306
  55.0 0.0 collective-permute-done.2.refs_0_
  55.0 2.7 %prefix_part.4 = bf16[4,336,128]{2,1,0:T(8,128)(2,1)S(1)} custom-call(s32[2]{0:T(128)S(1)} %pad_add_fusion.pos_ref, s32[16,128]{1,0:T(8,128)S(1)} %get-tuple-element.10.slots_ref, bf16[4,64,640]{2,1,0:T(8,128)(2,1)S(1)} %collective-permute-done.2.refs_0_, bf16[4096,128]{1,0:T(8,128)(2,1)S(1)} %get-tuple-element.11.refs_1_, ...), custom_call_target="tpu_custom_call" | custom-call | flops 671088640 | bytes 2097152 | tf_op jit(solution)/shard_map/prefix_part/pallas_call | solution.py:370
  57.7 3.4 %collective-permute-start.3 = (bf16[4,336,128]{2,1,0:T(8,128)(2,1)S(1)}, bf16[4,336,128]{2,1,0:T(8,128)(2,1)S(1)}, u32[]{:S(2)}, u32[]{:S(2)}) collective-permute-start(bf16[4,336,128]{2,1,0:T(8,128)(2,1)S(1)} %prefix_part.4), channel_id=1, source_target_pairs={{8,0},{16,8},{24,16},{32,24},{40,32},{48,40},{56,48},{64,56},{72,6... | collective-permute-start | bytes 1032200 | tf_op jit(solution)/shard_map/ppermute | solution.py:306
  61.2 2.4 %collective-permute-start.1 = (bf16[4,336,128]{2,1,0:T(8,128)(2,1)S(1)}, bf16[4,336,128]{2,1,0:T(8,128)(2,1)S(1)}, u32[]{:S(2)}, u32[]{:S(2)}) collective-permute-start(bf16[4,336,128]{2,1,0:T(8,128)(2,1)S(1)} %get-tuple-element.13), channel_id=1, source_target_pairs={{120,0},{0,8},{8,16},{16,24},{24,32},{32,40},{40,48},{48,56},{56,6... | collective-permute-start | bytes 1032200 | tf_op jit(solution)/shard_map/ppermute | solution.py:306
  63.6 2.7 %prefix_part.3.own_ref = bf16[4,336,128]{2,1,0:T(8,128)(2,1)S(1)} custom-call(s32[2]{0:T(128)S(1)} %pad_add_fusion.pos_ref, s32[16,128]{1,0:T(8,128)S(1)} %get-tuple-element.10.slots_ref, bf16[4,64,640]{2,1,0:T(8,128)(2,1)S(1)} %all_gather.6.refs_0_, bf16[4096,128]{1,0:T(8,128)(2,1)S(1)} %get-tuple-element.11.refs_1_, ...), custom_call_target="tpu_custom_call" | custom-call | flops 671088640 | bytes 2097152 | tf_op jit(solution)/shard_map/prefix_part/pallas_call | solution.py:370
  66.3 0.0 copy-start
  66.3 0.0 copy-start.1
  66.3 0.0 copy-start.3
  66.4 1.1 collective-permute-done.5.far_ref
  67.4 0.0 collective-permute-done.3.after_ref
  67.4 4.1 %collective-permute-done.1.before_ref = bf16[4,336,128]{2,1,0:T(8,128)(2,1)S(1)} collective-permute-done((bf16[4,336,128]{2,1,0:T(8,128)(2,1)S(1)}, bf16[4,336,128]{2,1,0:T(8,128)(2,1)S(1)}, u32[]{:S(2)}, u32[]{:S(2)}) %collective-permute-start.1) | collective-permute-done | bytes 344096 | tf_op jit(solution)/shard_map/ppermute | solution.py:306
  71.5 1.7 %class_sum.1 = bf16[4,336,128]{2,1,0:T(8,128)(2,1)} custom-call(bf16[4,336,128]{2,1,0:T(8,128)(2,1)S(1)} %prefix_part.3.own_ref, bf16[4,336,128]{2,1,0:T(8,128)(2,1)S(1)} %collective-permute-done.1.before_ref, bf16[4,336,128]{2,1,0:T(8,128)(2,1)S(1)} %collective-permute-done.3.after_ref, bf16[4,336,128]{2,1,0:T(8,128)(2,1)S(1)} %collective-permute-done.5.far_ref), custom_call_target="tpu_custom_call" | custom-call | tf_op jit(solution)/shard_map/class_sum/pallas_call | solution.py:405
  73.2 8.0 %all-to-all-start = ((bf16[4,336,128]{2,1,0:T(8,128)(2,1)}), bf16[4,336,128]{2,1,0:T(8,128)(2,1)S(1)}, u32[]{:S(2)}, u32[]{:S(2)}) async-start(bf16[4,336,128]{2,1,0:T(8,128)(2,1)} %class_sum.1), calls=%async_computation | async-start | bytes 688128 | tf_op jit(solution)/shard_map/all_to_all | solution.py:413
  81.9 0.0 copy-done
  81.9 0.0 copy-done.1
  81.9 0.0 copy-done.3
  82.0 3.0 %suffix_part.1.suffix_ref = f32[328,128]{1,0:T(8,128)S(1)} custom-call(s32[1]{0:T(128)S(6)} %copy.11.length_ref, bf16[1,64,640]{2,1,0:T(8,128)(2,1)S(1)} %copy-done.3, bf16[1,2048,128]{2,1,0:T(8,128)(2,1)S(1)} %copy-done, bf16[1,2048,128]{2,1,0:T(8,128)(2,1)S(1)} %copy-done.1), custom_call_target="tpu_custom_call" | custom-call | tf_op jit(solution)/shard_map/suffix_part/pallas_call | solution.py:380
  84.9 13.4 %all-to-all-done.parts_ref = bf16[4,336,128]{2,1,0:T(8,128)(2,1)S(1)} async-done(((bf16[4,336,128]{2,1,0:T(8,128)(2,1)}), bf16[4,336,128]{2,1,0:T(8,128)(2,1)S(1)}, u32[]{:S(2)}, u32[]{:S(2)}) %all-to-all-start) | async-done | bytes 344096 | tf_op jit(solution)/shard_map/all_to_all | solution.py:413
  98.3 0.5 attended.1
  98.8 21.3 %all_gather.7.refs_0_ = bf16[4,320,128]{2,1,0:T(8,128)(2,1)S(1)} all-gather(bf16[1,320,128]{2,1,0:T(8,128)(2,1)S(1)} %attended.1), channel_id=1, replica_groups={{0,32,64,96},{8,40,72,104},{16,48,80,112},{24,56,88,120},{1,33,65,97},{..., dimensions={0}, use_global_device_ids=true | all-gather | bytes 409600 | tf_op jit(solution)/shard_map/all_gather | solution.py:390
  120.1 0.0 copy-start.2
  120.1 2.0 %collective-permute-start.8 = (bf16[4,320,128]{2,1,0:T(8,128)(2,1)S(1)}, bf16[4,320,128]{2,1,0:T(8,128)(2,1)S(1)}, u32[]{:S(2)}, u32[]{:S(2)}) collective-permute-start(bf16[4,320,128]{2,1,0:T(8,128)(2,1)S(1)} %all_gather.7.refs_0_), channel_id=1, source_target_pairs={{16,0},{24,8},{32,16},{40,24},{48,32},{56,40},{64,48},{72,56},{80,... | collective-permute-start | bytes 983048 | tf_op jit(solution)/shard_map/ppermute | solution.py:306
  122.1 2.4 %collective-permute-start.6 = (bf16[4,320,128]{2,1,0:T(8,128)(2,1)S(1)}, bf16[4,320,128]{2,1,0:T(8,128)(2,1)S(1)}, u32[]{:S(2)}, u32[]{:S(2)}) collective-permute-start(bf16[4,320,128]{2,1,0:T(8,128)(2,1)S(1)} %all_gather.7.refs_0_), channel_id=1, source_target_pairs={{8,0},{16,8},{24,16},{32,24},{40,32},{48,40},{56,48},{64,56},{72,6... | collective-permute-start | bytes 983048 | tf_op jit(solution)/shard_map/ppermute | solution.py:306
  124.5 3.5 %collective-permute-start.7 = (bf16[4,320,128]{2,1,0:T(8,128)(2,1)S(1)}, bf16[4,320,128]{2,1,0:T(8,128)(2,1)S(1)}, u32[]{:S(2)}, u32[]{:S(2)}) collective-permute-start(bf16[4,320,128]{2,1,0:T(8,128)(2,1)S(1)} %all_gather.7.refs_0_), channel_id=1, source_target_pairs={{120,0},{0,8},{8,16},{16,24},{24,32},{32,40},{40,48},{48,56},{56,6... | collective-permute-start | bytes 983048 | tf_op jit(solution)/shard_map/ppermute | solution.py:306
  128.0 2.8 %collective-permute-done.8.refs_1_ = bf16[4,320,128]{2,1,0:T(8,128)(2,1)S(1)} collective-permute-done((bf16[4,320,128]{2,1,0:T(8,128)(2,1)S(1)}, bf16[4,320,128]{2,1,0:T(8,128)(2,1)S(1)}, u32[]{:S(2)}, u32[]{:S(2)}) %collective-permute-start.8) | collective-permute-done | bytes 327712 | tf_op jit(solution)/shard_map/ppermute | solution.py:306
  130.8 0.6 far_rows.1.refs_3_
  131.4 3.1 %collective-permute-done.6.refs_0_ = bf16[4,320,128]{2,1,0:T(8,128)(2,1)S(1)} collective-permute-done((bf16[4,320,128]{2,1,0:T(8,128)(2,1)S(1)}, bf16[4,320,128]{2,1,0:T(8,128)(2,1)S(1)}, u32[]{:S(2)}, u32[]{:S(2)}) %collective-permute-start.6) | collective-permute-done | bytes 327712 | tf_op jit(solution)/shard_map/ppermute | solution.py:306
  134.6 0.9 collective-permute-done.7.refs_1_
  135.4 0.0 copy-done.2
  135.4 1.6 %projection.1 = (bf16[1024,640]{1,0:T(8,128)(2,1)S(1)}, bf16[8,320,128]{2,1,0:T(8,128)(2,1)S(1)}) custom-call(s32[2]{0:T(128)S(1)} %pad_add_fusion.pos_ref, bf16[4,320,128]{2,1,0:T(8,128)(2,1)S(1)} %collective-permute-done.6.refs_0_, bf16[4,320,128]{2,1,0:T(8,128)(2,1)S(1)} %collective-permute-done.7.refs_1_, ...), custom_call_target="tpu_custom_call", output_to_operand_aliasing={{0}: (4, {})} | custom-call | tf_op jit(solution)/shard_map/projection/pallas_call | solution.py:440
  137.0 16.7 %all_to_all.10.parts_ref = bf16[8,320,128]{2,1,0:T(8,128)(2,1)S(1)} all-to-all(bf16[8,320,128]{2,1,0:T(8,128)(2,1)S(1)} %get-tuple-element.14), channel_id=1, replica_groups=mesh['prompt'=4,'seq'=16,'head'=8] {'head'}, dimensions={0} | all-to-all | bytes 1310720 | tf_op jit(solution)/shard_map/all_to_all | solution.py:310
  153.7 0.8 head_sum.1
Async XLA Ops:
  27.8 10.4 %collective-permute-start = (bf16[4,64,640]{2,1,0:T(8,128)(2,1)S(1)}, bf16[4,64,640]{2,1,0:T(8,128)(2,1)S(1)}, u32[]{:S(2)}, u32[]{:S(2)}) collective-permute-start(bf16[4,64,640]{2,1,0:T(8,128)(2,1)S(1)} %all_gather.6.refs_0_), channel_id=1, source_target_pairs={{8,0},{16,8},{24,16},{32,24},{40,32},{48,40},{56,48},{64,56},{72,6... | collective-permute-start | bytes 983048 | tf_op jit(solution)/shard_map/ppermute | solution.py:306
  31.6 17.3 %collective-permute-start.4 = (bf16[4,64,640]{2,1,0:T(8,128)(2,1)S(1)}, bf16[4,64,640]{2,1,0:T(8,128)(2,1)S(1)}, u32[]{:S(2)}, u32[]{:S(2)}) collective-permute-start(bf16[4,64,640]{2,1,0:T(8,128)(2,1)S(1)} %all_gather.6.refs_0_), channel_id=1, source_target_pairs={{16,0},{24,8},{32,16},{40,24},{48,32},{56,40},{64,48},{72,56},{80,... | collective-permute-start | bytes 983048 | tf_op jit(solution)/shard_map/ppermute | solution.py:306
  34.3 20.6 %collective-permute-start.2 = (bf16[4,64,640]{2,1,0:T(8,128)(2,1)S(1)}, bf16[4,64,640]{2,1,0:T(8,128)(2,1)S(1)}, u32[]{:S(2)}, u32[]{:S(2)}) collective-permute-start(bf16[4,64,640]{2,1,0:T(8,128)(2,1)S(1)} %all_gather.6.refs_0_), channel_id=1, source_target_pairs={{120,0},{0,8},{8,16},{16,24},{24,32},{32,40},{40,48},{48,56},{56,6... | collective-permute-start | bytes 983048 | tf_op jit(solution)/shard_map/ppermute | solution.py:306
  38.2 1.2 copy-start.4
  39.5 1.2 copy-start.5
  40.7 0.7 copy-start.6
  51.6 15.8 %collective-permute-start.5 = (bf16[4,336,128]{2,1,0:T(8,128)(2,1)S(1)}, bf16[4,336,128]{2,1,0:T(8,128)(2,1)S(1)}, u32[]{:S(2)}, u32[]{:S(2)}) collective-permute-start(bf16[4,336,128]{2,1,0:T(8,128)(2,1)S(1)} %prefix_part.5), channel_id=1, source_target_pairs={{112,0},{120,8},{0,16},{8,24},{16,32},{24,40},{32,48},{40,56},{48,... | collective-permute-start | bytes 1032200 | tf_op jit(solution)/shard_map/ppermute | solution.py:306
  57.7 9.7 %collective-permute-start.3 = (bf16[4,336,128]{2,1,0:T(8,128)(2,1)S(1)}, bf16[4,336,128]{2,1,0:T(8,128)(2,1)S(1)}, u32[]{:S(2)}, u32[]{:S(2)}) collective-permute-start(bf16[4,336,128]{2,1,0:T(8,128)(2,1)S(1)} %prefix_part.4), channel_id=1, source_target_pairs={{8,0},{16,8},{24,16},{32,24},{40,32},{48,40},{56,48},{64,56},{72,6... | collective-permute-start | bytes 1032200 | tf_op jit(solution)/shard_map/ppermute | solution.py:306
  61.2 10.4 %collective-permute-start.1 = (bf16[4,336,128]{2,1,0:T(8,128)(2,1)S(1)}, bf16[4,336,128]{2,1,0:T(8,128)(2,1)S(1)}, u32[]{:S(2)}, u32[]{:S(2)}) collective-permute-start(bf16[4,336,128]{2,1,0:T(8,128)(2,1)S(1)} %get-tuple-element.13), channel_id=1, source_target_pairs={{120,0},{0,8},{8,16},{16,24},{24,32},{32,40},{40,48},{48,56},{56,6... | collective-permute-start | bytes 1032200 | tf_op jit(solution)/shard_map/ppermute | solution.py:306
  66.3 15.6 %copy-start = (bf16[1,2048,128]{2,1,0:T(8,128)(2,1)S(1)}, bf16[1,2048,128]{2,1,0:T(8,128)(2,1)}, u32[]{:S(2)}) copy-start(bf16[1,2048,128]{2,1,0:T(8,128)(2,1)} %k_ref.1) | copy-start | bytes 1572868
  66.3 15.6 %copy-start.1 = (bf16[1,2048,128]{2,1,0:T(8,128)(2,1)S(1)}, bf16[1,2048,128]{2,1,0:T(8,128)(2,1)}, u32[]{:S(2)}) copy-start(bf16[1,2048,128]{2,1,0:T(8,128)(2,1)} %v_ref.1) | copy-start | bytes 1572868
  66.3 15.6 %copy-start.3 = (bf16[1,64,640]{2,1,0:T(8,128)(2,1)S(1)}, bf16[1,64,640]{2,1,0:T(8,128)(2,1)}, u32[]{:S(2)}) copy-start(bf16[1,64,640]{2,1,0:T(8,128)(2,1)} %q_ref.1) | copy-start | bytes 245764
  73.2 25.1 %all-to-all-start = ((bf16[4,336,128]{2,1,0:T(8,128)(2,1)}), bf16[4,336,128]{2,1,0:T(8,128)(2,1)S(1)}, u32[]{:S(2)}, u32[]{:S(2)}) async-start(bf16[4,336,128]{2,1,0:T(8,128)(2,1)} %class_sum.1), calls=%async_computation | async-start | bytes 688128 | tf_op jit(solution)/shard_map/all_to_all | solution.py:413
  120.1 15.4 %copy-start.2 = (bf16[640,320]{0,1:T(8,128)(2,1)S(1)}, bf16[640,320]{0,1:T(8,128)(2,1)}, u32[]{:S(2)}) copy-start(bf16[640,320]{0,1:T(8,128)(2,1)} %param.15) | copy-start | bytes 1228804
  120.1 10.7 %collective-permute-start.8 = (bf16[4,320,128]{2,1,0:T(8,128)(2,1)S(1)}, bf16[4,320,128]{2,1,0:T(8,128)(2,1)S(1)}, u32[]{:S(2)}, u32[]{:S(2)}) collective-permute-start(bf16[4,320,128]{2,1,0:T(8,128)(2,1)S(1)} %all_gather.7.refs_0_), channel_id=1, source_target_pairs={{16,0},{24,8},{32,16},{40,24},{48,32},{56,40},{64,48},{72,56},{80,... | collective-permute-start | bytes 983048 | tf_op jit(solution)/shard_map/ppermute | solution.py:306
  122.1 12.4 %collective-permute-start.6 = (bf16[4,320,128]{2,1,0:T(8,128)(2,1)S(1)}, bf16[4,320,128]{2,1,0:T(8,128)(2,1)S(1)}, u32[]{:S(2)}, u32[]{:S(2)}) collective-permute-start(bf16[4,320,128]{2,1,0:T(8,128)(2,1)S(1)} %all_gather.7.refs_0_), channel_id=1, source_target_pairs={{8,0},{16,8},{24,16},{32,24},{40,32},{48,40},{56,48},{64,56},{72,6... | collective-permute-start | bytes 983048 | tf_op jit(solution)/shard_map/ppermute | solution.py:306
  124.5 10.9 %collective-permute-start.7 = (bf16[4,320,128]{2,1,0:T(8,128)(2,1)S(1)}, bf16[4,320,128]{2,1,0:T(8,128)(2,1)S(1)}, u32[]{:S(2)}, u32[]{:S(2)}) collective-permute-start(bf16[4,320,128]{2,1,0:T(8,128)(2,1)S(1)} %all_gather.7.refs_0_), channel_id=1, source_target_pairs={{120,0},{0,8},{8,16},{16,24},{24,32},{32,40},{40,48},{48,56},{56,6... | collective-permute-start | bytes 983048 | tf_op jit(solution)/shard_map/ppermute | solution.py:306

commit v4 on v3

--- a/solution.py
+++ b/solution.py
@@ -256,25 +256,34 @@
     out_ref[0] = added(parts, shares).astype(jnp.bfloat16)
 
 
-def put_rows(pos_ref, in_refs, rows_ref, classes, layout):
+def placed(pos_ref, in_refs, classes, layout):
     for ref, (offset, first) in zip(in_refs, layout, strict=True):
         group = group_of(pos_ref, offset, classes)
         for i in range(ref.shape[0]):
             rows = ref[i]
-            sample = group + classes * (first + i)
-            rows_ref[pl.ds(pl.multiple_of(sample * QB, QB), QB), :] = jnp.concatenate(
-                [rows[j * QB : (j + 1) * QB] for j in range(GQA)], axis=1
+            yield (
+                group + classes * (first + i),
+                jnp.concatenate([rows[j * QB : (j + 1) * QB] for j in range(GQA)], axis=1),
             )
 
 
 def rows_kernel(pos_ref, *refs, classes, layout):
-    put_rows(pos_ref, refs[:-1], refs[-1], classes, layout)
+    for sample, rows in placed(pos_ref, refs[:-1], classes, layout):
+        refs[-1][lax.div(sample, 2)] = rows
 
 
 def project_kernel(pos_ref, *refs, classes, layout):
     n = len(layout)
-    in_refs, w_ref, _, rows_ref, out_ref = refs[:n], *refs[n:]
-    put_rows(pos_ref, in_refs, rows_ref, classes, layout)
+    in_refs, w_ref, done_ref, out_ref, rows_ref = refs[:n], *refs[n:]
+
+    def at(sample):
+        return pl.ds(pl.multiple_of(sample * QB, QB), QB)
+
+    own_parity = lax.rem(pos_ref[0], 2)
+    for i in range(done_ref.shape[0]):
+        rows_ref[at(2 * i + own_parity), :] = done_ref[i]
+    for sample, rows in placed(pos_ref, in_refs, classes, layout):
+        rows_ref[at(sample), :] = rows
     weight = w_ref[...]
     tokens = rows_ref.shape[0] // out_ref.shape[0]
     for i in range(out_ref.shape[0]):
@@ -427,25 +436,23 @@
         (same, (0, 0)),
         (shifted(same, 2), (2, 0)),
     )
-    rows_shape = jax.ShapeDtypeStruct((tokens, GQA * HD), bf16)
     rows = pl.pallas_call(
         functools.partial(rows_kernel, classes=classes, layout=tuple(w for _, w in rest)),
-        out_shape=rows_shape,
+        out_shape=jax.ShapeDtypeStruct((size // 2, QB, GQA * HD), bf16),
         in_specs=[in_smem()] + [in_vmem()] * len(rest),
         out_specs=in_vmem(),
         compiler_params=params(),
-        cost_estimate=pl.CostEstimate(flops=3 * 10**10, bytes_accessed=2**21, transcendentals=0),
+        cost_estimate=pl.CostEstimate(
+            flops=3 * 10**10, bytes_accessed=2**21, transcendentals=0
+        ),
         name="far_rows",
     )(position, *[piece for piece, _ in rest])
-    _, partial_value = pl.pallas_call(
+    partial_value = pl.pallas_call(
         functools.partial(project_kernel, classes=classes, layout=tuple(w for _, w in near)),
-        out_shape=[
-            rows_shape,
-            jax.ShapeDtypeStruct((heads, out_weight.shape[1], tokens // heads), bf16),
-        ],
+        out_shape=jax.ShapeDtypeStruct((heads, out_weight.shape[1], tokens // heads), bf16),
         in_specs=[in_smem()] + [in_vmem()] * (len(near) + 2),
-        out_specs=[in_vmem()] * 2,
-        input_output_aliases={len(near) + 2: 0},
+        out_specs=in_vmem(),
+        scratch_shapes=[pltpu.VMEM((tokens, GQA * HD), bf16)],
         compiler_params=params(),
         name="projection",
     )(position, *[piece for piece, _ in near], out_weight.T, rows)

time: 155 us -> 159 us (1.026)
  blocking collectives: 65.8 us -> 69 us
    ppermute x9, waiting for transfers between devices: 16.7 us -> 19.3 us  [shifted(): return lax.ppermute(x, ('prompt', 'seq'), route)]
    all_to_all x1, blocking collectives: 16.7 us -> 19 us  [head_exchange(): return lax.all_to_all(x, 'head', 0, 0, tiled=True)]
where the time goes in v4:
time: 159 us; the launch traced here: 158 us
  blocking collectives  69 us (43%)
  starting transfers between devices  34.7 us (22%)
  waiting for transfers between devices  31.4 us (20%)
  Pallas kernels  20 us (13%)
  local copies, waits for them, and re-layouts  2.47 us (2%)
    all_gather x2, blocking collectives, gathered_class(): lax.all_gather(x, 'seq', axis=0, tiled=True, axis_index_groups=groups)  50 us
    ppermute x9, starting transfers between devices, shifted(): return lax.ppermute(x, ('prompt', 'seq'), route)  26.5 us
    ppermute x9, waiting for transfers between devices, shifted(): return lax.ppermute(x, ('prompt', 'seq'), route)  19.3 us
    all_to_all x1, blocking collectives, head_exchange(): return lax.all_to_all(x, 'head', 0, 0, tiled=True)  19 us
    all_to_all x1, waiting for transfers between devices, body(): lax.all_to_all(gathered, 'seq', 0, 0, tiled=True, axis_index_groups=groups)  12 us
    pallas_call x3, Pallas kernels, prefix_part(): pl.pallas_call(functools.partial(prefix_kernel, offset=offset, classes=cl...  8.21 us
    all_to_all x1, starting transfers between devices, body(): lax.all_to_all(gathered, 'seq', 0, 0, tiled=True, axis_index_groups=groups)  8.18 us
    pallas_call x1, Pallas kernels, first_part(): pl.pallas_call(functools.partial(first_kernel, offset=offset, classes=cla...  3.68 us
  transfers between devices with their start and end apart: 10, of which 8 were waited for; matrix products, arithmetic and copies ran while one was open for 0% of the time, Pallas kernels for 10%

profile of v4, /device:TPU:8, one launch (start us, length us, event | category | flops | bytes accessed | tf_op | source)
XLA Modules:
  0.0 158.5 jit_solution(12316805562669870039)
XLA Ops:
  0.0 27.8 %all_gather.6.refs_0_ = bf16[4,64,640]{2,1,0:T(8,128)(2,1)S(1)} all-gather(bf16[1,64,640]{2,1,0:T(8,128)(2,1)} %q_ref.1), channel_id=1, replica_groups={{0,32,64,96},{8,40,72,104},{16,48,80,112},{24,56,88,120},{1,33,65,97},{..., dimensions={0}, use_global_device_ids=true | all-gather | bytes 409600 | tf_op jit(solution)/shard_map/all_gather | solution.py:399
  27.8 3.8 %collective-permute-start = (bf16[4,64,640]{2,1,0:T(8,128)(2,1)S(1)}, bf16[4,64,640]{2,1,0:T(8,128)(2,1)S(1)}, u32[]{:S(2)}, u32[]{:S(2)}) collective-permute-start(bf16[4,64,640]{2,1,0:T(8,128)(2,1)S(1)} %all_gather.6.refs_0_), channel_id=1, source_target_pairs={{8,0},{16,8},{24,16},{32,24},{40,32},{48,40},{56,48},{64,56},{72,6... | collective-permute-start | bytes 983048 | tf_op jit(solution)/shard_map/ppermute | solution.py:315
  31.6 2.7 %collective-permute-start.4 = (bf16[4,64,640]{2,1,0:T(8,128)(2,1)S(1)}, bf16[4,64,640]{2,1,0:T(8,128)(2,1)S(1)}, u32[]{:S(2)}, u32[]{:S(2)}) collective-permute-start(bf16[4,64,640]{2,1,0:T(8,128)(2,1)S(1)} %all_gather.6.refs_0_), channel_id=1, source_target_pairs={{16,0},{24,8},{32,16},{40,24},{48,32},{56,40},{64,48},{72,56},{80,... | collective-permute-start | bytes 983048 | tf_op jit(solution)/shard_map/ppermute | solution.py:315
  34.3 2.9 %collective-permute-start.2 = (bf16[4,64,640]{2,1,0:T(8,128)(2,1)S(1)}, bf16[4,64,640]{2,1,0:T(8,128)(2,1)S(1)}, u32[]{:S(2)}, u32[]{:S(2)}) collective-permute-start(bf16[4,64,640]{2,1,0:T(8,128)(2,1)S(1)} %all_gather.6.refs_0_), channel_id=1, source_target_pairs={{120,0},{0,8},{8,16},{16,24},{24,32},{32,40},{40,48},{48,56},{56,6... | collective-permute-start | bytes 983048 | tf_op jit(solution)/shard_map/ppermute | solution.py:315
  37.2 0.0 copy-start.6
  37.3 0.1 pad_add_fusion.pos_ref
  37.3 0.9 collective-permute-done.q_ref
  38.2 0.0 copy-done.6
  38.2 0.0 copy-start.4
  38.2 1.2 copy-done.4
  39.5 0.0 copy-start.5
  39.5 1.2 copy-done.5
  40.7 3.7 %first_part.1 = (bf16[4,336,128]{2,1,0:T(8,128)(2,1)S(1)}, s32[16,128]{1,0:T(8,128)S(1)}, bf16[4096,128]{1,0:T(8,128)(2,1)S(1)}, bf16[4096,128]{1,0:T(8,128)(2,1)S(1)}) custom-call(s32[2]{0:T(128)S(1)} %pad_add_fusion.pos_ref, s32[16,64]{1,0:T(8,128)S(1)} %copy-done.6, bf16[4,64,640]{2,1,0:T(8,128)(2,1)S(1)} %collective-permute-done.q_ref, ...), custom_call_target="tpu_custom_call" | custom-call | flops 671088640 | bytes 2097152 | tf_op jit(solution)/shard_map/first_part/pallas_call | solution.py:359
  44.4 4.5 %collective-permute-done.4.refs_0_ = bf16[4,64,640]{2,1,0:T(8,128)(2,1)S(1)} collective-permute-done((bf16[4,64,640]{2,1,0:T(8,128)(2,1)S(1)}, bf16[4,64,640]{2,1,0:T(8,128)(2,1)S(1)}, u32[]{:S(2)}, u32[]{:S(2)}) %collective-permute-start.4) | collective-permute-done | bytes 327712 | tf_op jit(solution)/shard_map/ppermute | solution.py:315
  48.9 2.7 %prefix_part.5 = bf16[4,336,128]{2,1,0:T(8,128)(2,1)S(1)} custom-call(s32[2]{0:T(128)S(1)} %pad_add_fusion.pos_ref, s32[16,128]{1,0:T(8,128)S(1)} %get-tuple-element.9.slots_ref, bf16[4,64,640]{2,1,0:T(8,128)(2,1)S(1)} %collective-permute-done.4.refs_0_, bf16[4096,128]{1,0:T(8,128)(2,1)S(1)} %get-tuple-element.10.refs_1_, ...), custom_call_target="tpu_custom_call" | custom-call | flops 671088640 | bytes 2097152 | tf_op jit(solution)/shard_map/prefix_part/pallas_call | solution.py:379
  51.6 3.3 %collective-permute-start.5 = (bf16[4,336,128]{2,1,0:T(8,128)(2,1)S(1)}, bf16[4,336,128]{2,1,0:T(8,128)(2,1)S(1)}, u32[]{:S(2)}, u32[]{:S(2)}) collective-permute-start(bf16[4,336,128]{2,1,0:T(8,128)(2,1)S(1)} %prefix_part.5), channel_id=1, source_target_pairs={{112,0},{120,8},{0,16},{8,24},{16,32},{24,40},{32,48},{40,56},{48,... | collective-permute-start | bytes 1032200 | tf_op jit(solution)/shard_map/ppermute | solution.py:315
  55.0 0.0 collective-permute-done.2.refs_0_
  55.0 2.7 %prefix_part.4 = bf16[4,336,128]{2,1,0:T(8,128)(2,1)S(1)} custom-call(s32[2]{0:T(128)S(1)} %pad_add_fusion.pos_ref, s32[16,128]{1,0:T(8,128)S(1)} %get-tuple-element.9.slots_ref, bf16[4,64,640]{2,1,0:T(8,128)(2,1)S(1)} %collective-permute-done.2.refs_0_, bf16[4096,128]{1,0:T(8,128)(2,1)S(1)} %get-tuple-element.10.refs_1_, ...), custom_call_target="tpu_custom_call" | custom-call | flops 671088640 | bytes 2097152 | tf_op jit(solution)/shard_map/prefix_part/pallas_call | solution.py:379
  57.7 3.4 %collective-permute-start.3 = (bf16[4,336,128]{2,1,0:T(8,128)(2,1)S(1)}, bf16[4,336,128]{2,1,0:T(8,128)(2,1)S(1)}, u32[]{:S(2)}, u32[]{:S(2)}) collective-permute-start(bf16[4,336,128]{2,1,0:T(8,128)(2,1)S(1)} %prefix_part.4), channel_id=1, source_target_pairs={{8,0},{16,8},{24,16},{32,24},{40,32},{48,40},{56,48},{64,56},{72,6... | collective-permute-start | bytes 1032200 | tf_op jit(solution)/shard_map/ppermute | solution.py:315
  61.2 2.4 %collective-permute-start.1 = (bf16[4,336,128]{2,1,0:T(8,128)(2,1)S(1)}, bf16[4,336,128]{2,1,0:T(8,128)(2,1)S(1)}, u32[]{:S(2)}, u32[]{:S(2)}) collective-permute-start(bf16[4,336,128]{2,1,0:T(8,128)(2,1)S(1)} %get-tuple-element.12), channel_id=1, source_target_pairs={{120,0},{0,8},{8,16},{16,24},{24,32},{32,40},{40,48},{48,56},{56,6... | collective-permute-start | bytes 1032200 | tf_op jit(solution)/shard_map/ppermute | solution.py:315
  63.6 2.7 %prefix_part.3.own_ref = bf16[4,336,128]{2,1,0:T(8,128)(2,1)S(1)} custom-call(s32[2]{0:T(128)S(1)} %pad_add_fusion.pos_ref, s32[16,128]{1,0:T(8,128)S(1)} %get-tuple-element.9.slots_ref, bf16[4,64,640]{2,1,0:T(8,128)(2,1)S(1)} %all_gather.6.refs_0_, bf16[4096,128]{1,0:T(8,128)(2,1)S(1)} %get-tuple-element.10.refs_1_, ...), custom_call_target="tpu_custom_call" | custom-call | flops 671088640 | bytes 2097152 | tf_op jit(solution)/shard_map/prefix_part/pallas_call | solution.py:379
  66.3 0.0 collective-permute-done.5.far_ref
  66.3 0.5 collective-permute-done.3.after_ref
  66.9 4.7 %collective-permute-done.1.before_ref = bf16[4,336,128]{2,1,0:T(8,128)(2,1)S(1)} collective-permute-done((bf16[4,336,128]{2,1,0:T(8,128)(2,1)S(1)}, bf16[4,336,128]{2,1,0:T(8,128)(2,1)S(1)}, u32[]{:S(2)}, u32[]{:S(2)}) %collective-permute-start.1) | collective-permute-done | bytes 344096 | tf_op jit(solution)/shard_map/ppermute | solution.py:315
  71.5 0.0 copy-start.1
  71.5 1.7 %class_sum.1 = bf16[4,336,128]{2,1,0:T(8,128)(2,1)} custom-call(bf16[4,336,128]{2,1,0:T(8,128)(2,1)S(1)} %prefix_part.3.own_ref, bf16[4,336,128]{2,1,0:T(8,128)(2,1)S(1)} %collective-permute-done.1.before_ref, bf16[4,336,128]{2,1,0:T(8,128)(2,1)S(1)} %collective-permute-done.3.after_ref, bf16[4,336,128]{2,1,0:T(8,128)(2,1)S(1)} %collective-permute-done.5.far_ref), custom_call_target="tpu_custom_call" | custom-call | tf_op jit(solution)/shard_map/class_sum/pallas_call | solution.py:414
  73.2 0.0 copy-start
  73.2 0.0 copy-start.3
  73.2 8.2 %all-to-all-start = ((bf16[4,336,128]{2,1,0:T(8,128)(2,1)}), bf16[4,336,128]{2,1,0:T(8,128)(2,1)S(1)}, u32[]{:S(2)}, u32[]{:S(2)}) async-start(bf16[4,336,128]{2,1,0:T(8,128)(2,1)} %class_sum.1), calls=%async_computation | async-start | bytes 688128 | tf_op jit(solution)/shard_map/all_to_all | solution.py:422
  82.0 0.0 copy-done.1
  82.1 0.0 copy-done
  82.1 0.0 copy-done.3
  82.1 3.0 %suffix_part.1.suffix_ref = f32[328,128]{1,0:T(8,128)S(1)} custom-call(s32[1]{0:T(128)S(6)} %copy.9.length_ref, bf16[1,64,640]{2,1,0:T(8,128)(2,1)S(1)} %copy-done.3, bf16[1,2048,128]{2,1,0:T(8,128)(2,1)S(1)} %copy-done, bf16[1,2048,128]{2,1,0:T(8,128)(2,1)S(1)} %copy-done.1), custom_call_target="tpu_custom_call" | custom-call | tf_op jit(solution)/shard_map/suffix_part/pallas_call | solution.py:389
  85.0 12.0 %all-to-all-done.parts_ref = bf16[4,336,128]{2,1,0:T(8,128)(2,1)S(1)} async-done(((bf16[4,336,128]{2,1,0:T(8,128)(2,1)}), bf16[4,336,128]{2,1,0:T(8,128)(2,1)S(1)}, u32[]{:S(2)}, u32[]{:S(2)}) %all-to-all-start) | async-done | bytes 344096 | tf_op jit(solution)/shard_map/all_to_all | solution.py:422
  97.1 0.5 attended.1
  97.5 22.2 %all_gather.7.refs_0_ = bf16[4,320,128]{2,1,0:T(8,128)(2,1)S(1)} all-gather(bf16[1,320,128]{2,1,0:T(8,128)(2,1)S(1)} %attended.1), channel_id=1, replica_groups={{0,32,64,96},{8,40,72,104},{16,48,80,112},{24,56,88,120},{1,33,65,97},{..., dimensions={0}, use_global_device_ids=true | all-gather | bytes 409600 | tf_op jit(solution)/shard_map/all_gather | solution.py:399
  119.7 0.0 copy-start.2
  119.7 2.0 %collective-permute-start.8 = (bf16[4,320,128]{2,1,0:T(8,128)(2,1)S(1)}, bf16[4,320,128]{2,1,0:T(8,128)(2,1)S(1)}, u32[]{:S(2)}, u32[]{:S(2)}) collective-permute-start(bf16[4,320,128]{2,1,0:T(8,128)(2,1)S(1)} %all_gather.7.refs_0_), channel_id=1, source_target_pairs={{16,0},{24,8},{32,16},{40,24},{48,32},{56,40},{64,48},{72,56},{80,... | collective-permute-start | bytes 983048 | tf_op jit(solution)/shard_map/ppermute | solution.py:315
  121.8 2.0 %collective-permute-start.6 = (bf16[4,320,128]{2,1,0:T(8,128)(2,1)S(1)}, bf16[4,320,128]{2,1,0:T(8,128)(2,1)S(1)}, u32[]{:S(2)}, u32[]{:S(2)}) collective-permute-start(bf16[4,320,128]{2,1,0:T(8,128)(2,1)S(1)} %all_gather.7.refs_0_), channel_id=1, source_target_pairs={{8,0},{16,8},{24,16},{32,24},{40,32},{48,40},{56,48},{64,56},{72,6... | collective-permute-start | bytes 983048 | tf_op jit(solution)/shard_map/ppermute | solution.py:315
  123.8 3.8 %collective-permute-start.7 = (bf16[4,320,128]{2,1,0:T(8,128)(2,1)S(1)}, bf16[4,320,128]{2,1,0:T(8,128)(2,1)S(1)}, u32[]{:S(2)}, u32[]{:S(2)}) collective-permute-start(bf16[4,320,128]{2,1,0:T(8,128)(2,1)S(1)} %all_gather.7.refs_0_), channel_id=1, source_target_pairs={{120,0},{0,8},{8,16},{16,24},{24,32},{32,40},{40,48},{48,56},{56,6... | collective-permute-start | bytes 983048 | tf_op jit(solution)/shard_map/ppermute | solution.py:315
  127.6 3.6 %collective-permute-done.8.refs_1_ = bf16[4,320,128]{2,1,0:T(8,128)(2,1)S(1)} collective-permute-done((bf16[4,320,128]{2,1,0:T(8,128)(2,1)S(1)}, bf16[4,320,128]{2,1,0:T(8,128)(2,1)S(1)}, u32[]{:S(2)}, u32[]{:S(2)}) %collective-permute-start.8) | collective-permute-done | bytes 327712 | tf_op jit(solution)/shard_map/ppermute | solution.py:315
  131.3 0.6 far_rows.1.refs_3_
  131.9 2.2 %collective-permute-done.6.refs_0_ = bf16[4,320,128]{2,1,0:T(8,128)(2,1)S(1)} collective-permute-done((bf16[4,320,128]{2,1,0:T(8,128)(2,1)S(1)}, bf16[4,320,128]{2,1,0:T(8,128)(2,1)S(1)}, u32[]{:S(2)}, u32[]{:S(2)}) %collective-permute-start.6) | collective-permute-done | bytes 327712 | tf_op jit(solution)/shard_map/ppermute | solution.py:315
  134.2 2.9 %collective-permute-done.7.refs_1_ = bf16[4,320,128]{2,1,0:T(8,128)(2,1)S(1)} collective-permute-done((bf16[4,320,128]{2,1,0:T(8,128)(2,1)S(1)}, bf16[4,320,128]{2,1,0:T(8,128)(2,1)S(1)}, u32[]{:S(2)}, u32[]{:S(2)}) %collective-permute-start.7) | collective-permute-done | bytes 327712 | tf_op jit(solution)/shard_map/ppermute | solution.py:315
  137.1 0.0 copy-done.2
  137.1 1.6 %projection.1 = bf16[8,320,128]{2,1,0:T(8,128)(2,1)S(1)} custom-call(s32[2]{0:T(128)S(1)} %pad_add_fusion.pos_ref, bf16[4,320,128]{2,1,0:T(8,128)(2,1)S(1)} %collective-permute-done.6.refs_0_, bf16[4,320,128]{2,1,0:T(8,128)(2,1)S(1)} %collective-permute-done.7.refs_1_, bf16[320,640]{1,0:T(8,128)(2,1)S(1)} %bitcast.4, bf16[8,64,640]{2,1,0:T(8,128)(2,1)S(1)} %far_rows.1.refs_3_), custom_call_target="tpu_custom_call" | custom-call | tf_op jit(solution)/shard_map/projection/pallas_call | solution.py:450
  138.7 19.0 %all_to_all.10.parts_ref = bf16[8,320,128]{2,1,0:T(8,128)(2,1)S(1)} all-to-all(bf16[8,320,128]{2,1,0:T(8,128)(2,1)S(1)} %projection.1), channel_id=1, replica_groups=mesh['prompt'=4,'seq'=16,'head'=8] {'head'}, dimensions={0} | all-to-all | bytes 1310720 | tf_op jit(solution)/shard_map/all_to_all | solution.py:319
  157.7 0.8 head_sum.1
Async XLA Ops:
  27.8 10.4 %collective-permute-start = (bf16[4,64,640]{2,1,0:T(8,128)(2,1)S(1)}, bf16[4,64,640]{2,1,0:T(8,128)(2,1)S(1)}, u32[]{:S(2)}, u32[]{:S(2)}) collective-permute-start(bf16[4,64,640]{2,1,0:T(8,128)(2,1)S(1)} %all_gather.6.refs_0_), channel_id=1, source_target_pairs={{8,0},{16,8},{24,16},{32,24},{40,32},{48,40},{56,48},{64,56},{72,6... | collective-permute-start | bytes 983048 | tf_op jit(solution)/shard_map/ppermute | solution.py:315
  31.6 17.3 %collective-permute-start.4 = (bf16[4,64,640]{2,1,0:T(8,128)(2,1)S(1)}, bf16[4,64,640]{2,1,0:T(8,128)(2,1)S(1)}, u32[]{:S(2)}, u32[]{:S(2)}) collective-permute-start(bf16[4,64,640]{2,1,0:T(8,128)(2,1)S(1)} %all_gather.6.refs_0_), channel_id=1, source_target_pairs={{16,0},{24,8},{32,16},{40,24},{48,32},{56,40},{64,48},{72,56},{80,... | collective-permute-start | bytes 983048 | tf_op jit(solution)/shard_map/ppermute | solution.py:315
  34.3 20.6 %collective-permute-start.2 = (bf16[4,64,640]{2,1,0:T(8,128)(2,1)S(1)}, bf16[4,64,640]{2,1,0:T(8,128)(2,1)S(1)}, u32[]{:S(2)}, u32[]{:S(2)}) collective-permute-start(bf16[4,64,640]{2,1,0:T(8,128)(2,1)S(1)} %all_gather.6.refs_0_), channel_id=1, source_target_pairs={{120,0},{0,8},{8,16},{16,24},{24,32},{32,40},{40,48},{48,56},{56,6... | collective-permute-start | bytes 983048 | tf_op jit(solution)/shard_map/ppermute | solution.py:315
  37.2 1.0 copy-start.6
  38.2 1.2 copy-start.4
  39.5 1.2 copy-start.5
  51.6 14.7 %collective-permute-start.5 = (bf16[4,336,128]{2,1,0:T(8,128)(2,1)S(1)}, bf16[4,336,128]{2,1,0:T(8,128)(2,1)S(1)}, u32[]{:S(2)}, u32[]{:S(2)}) collective-permute-start(bf16[4,336,128]{2,1,0:T(8,128)(2,1)S(1)} %prefix_part.5), channel_id=1, source_target_pairs={{112,0},{120,8},{0,16},{8,24},{16,32},{24,40},{32,48},{40,56},{48,... | collective-permute-start | bytes 1032200 | tf_op jit(solution)/shard_map/ppermute | solution.py:315
  57.7 9.1 %collective-permute-start.3 = (bf16[4,336,128]{2,1,0:T(8,128)(2,1)S(1)}, bf16[4,336,128]{2,1,0:T(8,128)(2,1)S(1)}, u32[]{:S(2)}, u32[]{:S(2)}) collective-permute-start(bf16[4,336,128]{2,1,0:T(8,128)(2,1)S(1)} %prefix_part.4), channel_id=1, source_target_pairs={{8,0},{16,8},{24,16},{32,24},{40,32},{48,40},{56,48},{64,56},{72,6... | collective-permute-start | bytes 1032200 | tf_op jit(solution)/shard_map/ppermute | solution.py:315
  61.2 10.4 %collective-permute-start.1 = (bf16[4,336,128]{2,1,0:T(8,128)(2,1)S(1)}, bf16[4,336,128]{2,1,0:T(8,128)(2,1)S(1)}, u32[]{:S(2)}, u32[]{:S(2)}) collective-permute-start(bf16[4,336,128]{2,1,0:T(8,128)(2,1)S(1)} %get-tuple-element.12), channel_id=1, source_target_pairs={{120,0},{0,8},{8,16},{16,24},{24,32},{32,40},{40,48},{48,56},{56,6... | collective-permute-start | bytes 1032200 | tf_op jit(solution)/shard_map/ppermute | solution.py:315
  71.5 10.5 %copy-start.1 = (bf16[1,2048,128]{2,1,0:T(8,128)(2,1)S(1)}, bf16[1,2048,128]{2,1,0:T(8,128)(2,1)}, u32[]{:S(2)}) copy-start(bf16[1,2048,128]{2,1,0:T(8,128)(2,1)} %v_ref.1) | copy-start | bytes 1572868
  73.2 8.8 %copy-start = (bf16[1,2048,128]{2,1,0:T(8,128)(2,1)S(1)}, bf16[1,2048,128]{2,1,0:T(8,128)(2,1)}, u32[]{:S(2)}) copy-start(bf16[1,2048,128]{2,1,0:T(8,128)(2,1)} %k_ref.1) | copy-start | bytes 1572868
  73.2 8.9 %copy-start.3 = (bf16[1,64,640]{2,1,0:T(8,128)(2,1)S(1)}, bf16[1,64,640]{2,1,0:T(8,128)(2,1)}, u32[]{:S(2)}) copy-start(bf16[1,64,640]{2,1,0:T(8,128)(2,1)} %q_ref.1) | copy-start | bytes 245764
  73.2 23.8 %all-to-all-start = ((bf16[4,336,128]{2,1,0:T(8,128)(2,1)}), bf16[4,336,128]{2,1,0:T(8,128)(2,1)S(1)}, u32[]{:S(2)}, u32[]{:S(2)}) async-start(bf16[4,336,128]{2,1,0:T(8,128)(2,1)} %class_sum.1), calls=%async_computation | async-start | bytes 688128 | tf_op jit(solution)/shard_map/all_to_all | solution.py:422
  119.7 17.3 %copy-start.2 = (bf16[640,320]{0,1:T(8,128)(2,1)S(1)}, bf16[640,320]{0,1:T(8,128)(2,1)}, u32[]{:S(2)}) copy-start(bf16[640,320]{0,1:T(8,128)(2,1)} %param.15) | copy-start | bytes 1228804
  119.7 11.5 %collective-permute-start.8 = (bf16[4,320,128]{2,1,0:T(8,128)(2,1)S(1)}, bf16[4,320,128]{2,1,0:T(8,128)(2,1)S(1)}, u32[]{:S(2)}, u32[]{:S(2)}) collective-permute-start(bf16[4,320,128]{2,1,0:T(8,128)(2,1)S(1)} %all_gather.7.refs_0_), channel_id=1, source_target_pairs={{16,0},{24,8},{32,16},{40,24},{48,32},{56,40},{64,48},{72,56},{80,... | collective-permute-start | bytes 983048 | tf_op jit(solution)/shard_map/ppermute | solution.py:315
  121.8 12.4 %collective-permute-start.6 = (bf16[4,320,128]{2,1,0:T(8,128)(2,1)S(1)}, bf16[4,320,128]{2,1,0:T(8,128)(2,1)S(1)}, u32[]{:S(2)}, u32[]{:S(2)}) collective-permute-start(bf16[4,320,128]{2,1,0:T(8,128)(2,1)S(1)} %all_gather.7.refs_0_), channel_id=1, source_target_pairs={{8,0},{16,8},{24,16},{32,24},{40,32},{48,40},{56,48},{64,56},{72,6... | collective-permute-start | bytes 983048 | tf_op jit(solution)/shard_map/ppermute | solution.py:315
  123.8 13.3 %collective-permute-start.7 = (bf16[4,320,128]{2,1,0:T(8,128)(2,1)S(1)}, bf16[4,320,128]{2,1,0:T(8,128)(2,1)S(1)}, u32[]{:S(2)}, u32[]{:S(2)}) collective-permute-start(bf16[4,320,128]{2,1,0:T(8,128)(2,1)S(1)} %all_gather.7.refs_0_), channel_id=1, source_target_pairs={{120,0},{0,8},{8,16},{16,24},{24,32},{32,40},{40,48},{48,56},{56,6... | collective-permute-start | bytes 983048 | tf_op jit(solution)/shard_map/ppermute | solution.py:315
